TPU v7x, 32 devices: a whole 2x2x4 slice. The times are simulated.
32 devices in a mesh: var: 8 (over y, x, core), space: 4 (over z).
Axes of the slice: x: 2, y: 2, z: 4, core: 2. Of those that a mesh axis runs over, the one named last changes fastest.
Arguments:
- patches: bfloat16 [48, 1024, 256], P('var', 'space'), may hold values from -6 to 6
- embed_weight: bfloat16 [48, 256, 1024], P('var'), may hold values from -0.375 to 0.375
- var_embed: float32 [48, 1024], P('var'), may hold values from -3 to 3
- agg_query: float32 [1024], replicated, may hold values from -240 to 240
- agg_kv: bfloat16 [1024, 2048], replicated, may hold values from -0.1875 to 0.1875
- agg_out: bfloat16 [1024, 1024], replicated, may hold values from -0.1875 to 0.1875
- norm_gain: float32 [1024], replicated, may hold values from 0.5 to 1.5
- qkv_weight: bfloat16 [1024, 3072], P(None, 'var'), may hold values from -4 to 4
- out_weight: bfloat16 [1024, 1024], P('var'), may hold values from -0.1875 to 0.1875
- cotangent: bfloat16 [1024, 1024], P('space'), may hold values from -6 to 6
Outputs:
- grad_embed: float32 [48, 256, 1024], P('var', None, 'space')
- grad_var_embed: float32 [48, 1024], P('var', 'space')
- grad_agg_query: float32 [1024], P('space')
- grad_agg_kv: float32 [1024, 2048], P(None, 'space')
- grad_agg_out: float32 [1024, 1024], P(None, 'space')
- grad_norm_gain: float32 [1024], P('space')
- grad_qkv: float32 [1024, 3072], P('space', 'var')
- grad_out_weight: float32 [1024, 1024], P('var', 'space')
All inputs are finite; a program needn't handle non-finite values.
Results may differ from a plain program's by a relative error of at most 0.019.
The roundings to bfloat16 on the way count: a program that leaves them out, or rounds other values in their place, can miss the bound.
Values may be sent and summed in bfloat16 or wider, within the bound.
No kernel may reach another device: no remote copies, remote signals or barrier semaphores. Data moves between devices by JAX's collectives and lax.ppermute only.
A program may use at most 128 MiB of HBM per device.

v0:
```python
import math

import jax
import jax.numpy as jnp
from jax import lax
from jax.sharding import PartitionSpec as P

HEADS = 16


EPSILON = 1e-05


def for_sending(array):
    return jax.tree.map(lambda a: a.astype(jnp.bfloat16) if a.dtype == jnp.float32 else a, array)


def combined_all(part, axis, combine):
    gathered = jax.tree.map(lambda a: lax.all_gather(a, axis), part)

    def take(source):
        return jax.tree.map(lambda a: lax.dynamic_index_in_dim(a, source, 0, False), gathered)

    return lax.fori_loop(
        1, lax.axis_size(axis), lambda source, state: combine(state, take(source)), take(0)
    )


def combine_pool(left_part, right_part):
    left_max, left_sum, left_value = left_part
    right_max, right_sum, right_value = right_part
    row_count, head_count = left_max.shape
    new_max = jnp.maximum(left_max, right_max)
    left_factor = jnp.exp(left_max - new_max)
    right_factor = jnp.exp(right_max - new_max)
    new_sum = left_sum * left_factor + right_sum * right_factor
    new_value = (
        left_value.reshape(row_count, head_count, -1) * left_factor[..., None]
        + right_value.reshape(row_count, head_count, -1) * right_factor[..., None]
    )
    return (new_max, new_sum, new_value.reshape(left_value.shape))


def sum_over_var(operand):
    return jax.tree.map(
        lambda part: part.astype(jnp.float32), lax.psum(for_sending(operand), "var")
    )


def shards(
    patches,
    embed_weight,
    var_embed,
    agg_query,
    agg_kv,
    agg_out,
    norm_gain,
    qkv_weight,
    out_weight,
    cotangent,
):
    var_count, rows_here, pixel_count = patches.shape
    model_width = agg_out.shape[0]
    head_size = model_width // HEADS
    score_scale = 1.0 / math.sqrt(head_size)
    head_query = agg_query.reshape(HEADS, head_size)
    embedded = (
        jnp.einsum("vtp,vpd->vtd", patches, embed_weight, preferred_element_type=jnp.float32)
        + var_embed[:, None, :]
    ).astype(jnp.bfloat16)
    projected = jnp.einsum("vtd,de->vte", embedded, agg_kv, preferred_element_type=jnp.float32)
    key_rows = projected[..., :model_width].reshape(var_count, rows_here, HEADS, head_size)
    value_rows = projected[..., model_width:].reshape(var_count, rows_here, HEADS, head_size)
    scores = jnp.sum(key_rows * head_query, axis=-1) * score_scale
    local_max = jnp.max(scores, axis=0)
    local_weight = jnp.exp(scores - local_max)
    local_sum = jnp.sum(local_weight, axis=0)
    local_value = jnp.sum(local_weight[..., None] * value_rows, axis=0).reshape(
        rows_here, model_width
    )
    maxima, totals, weighted = combined_all(
        (local_max, local_sum, local_value), "var", combine_pool
    )
    mixed_heads = weighted.reshape(rows_here, HEADS, head_size) / totals[..., None]
    pooled = mixed_heads.reshape(rows_here, model_width).astype(jnp.bfloat16)
    joined_tokens = jnp.dot(pooled, agg_out, preferred_element_type=jnp.float32).astype(
        jnp.bfloat16
    )
    joined_wide = joined_tokens.astype(jnp.float32)
    feature_mean = jnp.mean(joined_wide, axis=-1, keepdims=True)
    spread_sq = jnp.mean((joined_wide - feature_mean) ** 2, axis=-1, keepdims=True)
    inv_spread = lax.rsqrt(spread_sq + EPSILON)
    centred = (joined_wide - feature_mean) * inv_spread
    normed = (centred * norm_gain).astype(jnp.bfloat16)
    local_heads = qkv_weight.shape[1] // (3 * head_size)
    qkv_rows = jnp.dot(normed, qkv_weight, preferred_element_type=jnp.float32).astype(jnp.bfloat16)
    qkv_rows = qkv_rows.reshape(rows_here, local_heads, 3, head_size)
    queries = qkv_rows[:, :, 0]
    own_pairs = qkv_rows[:, :, 1:].reshape(rows_here, local_heads * 2 * head_size)
    all_pairs = lax.all_gather(own_pairs, "space", axis=0, tiled=True).reshape(
        -1, local_heads, 2, head_size
    )
    keys_all = all_pairs[:, :, 0]
    values_all = all_pairs[:, :, 1]
    logits = (
        jnp.einsum("thd,lhd->htl", queries, keys_all, preferred_element_type=jnp.float32)
        * score_scale
    )
    shifted = jnp.exp(logits - jnp.max(logits, axis=-1, keepdims=True))
    probs = shifted / jnp.sum(shifted, axis=-1, keepdims=True)
    probs_b = probs.astype(jnp.bfloat16)
    attn = jnp.einsum(
        "htl,lhd->thd", probs_b, values_all, preferred_element_type=jnp.float32
    ).astype(jnp.bfloat16)
    attn = attn.reshape(rows_here, local_heads * head_size)
    d_attn = jnp.dot(cotangent, out_weight.T, preferred_element_type=jnp.float32).astype(
        jnp.bfloat16
    )
    d_attn = d_attn.reshape(rows_here, local_heads, head_size)
    dprob = jnp.einsum("thd,lhd->htl", d_attn, values_all, preferred_element_type=jnp.float32)
    row_delta = jnp.sum(probs * dprob, axis=-1, keepdims=True)
    dscore = (probs * (dprob - row_delta) * score_scale).astype(jnp.bfloat16)
    grad_q = jnp.einsum("htl,lhd->thd", dscore, keys_all, preferred_element_type=jnp.float32)
    grad_k = jnp.einsum("htc,thd->chd", dscore, queries, preferred_element_type=jnp.float32)
    grad_v = jnp.einsum("htc,thd->chd", probs_b, d_attn, preferred_element_type=jnp.float32)
    own_grads = lax.psum_scatter(
        jnp.stack([grad_k, grad_v], axis=2)
        .reshape(lax.axis_size("space") * rows_here, local_heads * 2 * head_size)
        .astype(jnp.bfloat16),
        "space",
        scatter_dimension=0,
        tiled=True,
    ).astype(jnp.float32)
    own_grads = own_grads.reshape(rows_here, local_heads, 2, head_size)
    d_qkv = jnp.concatenate([grad_q[:, :, None], own_grads], axis=2).astype(jnp.bfloat16)
    d_qkv = d_qkv.reshape(rows_here, local_heads * 3 * head_size)
    grad_out_part = jnp.dot(attn.T, cotangent, preferred_element_type=jnp.float32)
    grad_qkv_part = jnp.dot(normed.T, d_qkv, preferred_element_type=jnp.float32)
    d_normed = sum_over_var(jnp.dot(d_qkv, qkv_weight.T, preferred_element_type=jnp.float32))
    grad_gain_part = jnp.sum(d_normed * centred, axis=0)
    gained = d_normed * norm_gain
    d_joined = (
        cotangent.astype(jnp.float32)
        + (
            gained
            - jnp.mean(gained, axis=-1, keepdims=True)
            - centred * jnp.mean(gained * centred, axis=-1, keepdims=True)
        )
        * inv_spread
    ).astype(jnp.bfloat16)
    grad_agg_out_part = jnp.dot(pooled.T, d_joined, preferred_element_type=jnp.float32)
    d_pooled = jnp.dot(d_joined, agg_out.T, preferred_element_type=jnp.float32).reshape(
        rows_here, HEADS, head_size
    )
    center = jnp.sum(d_pooled * mixed_heads, axis=-1)
    soft_weight = jnp.exp(scores - maxima) / totals
    dweight = jnp.sum(d_pooled * value_rows, axis=-1)
    dlogit = soft_weight * (dweight - center)
    d_key = dlogit[..., None] * head_query * score_scale
    d_value = soft_weight[..., None] * d_pooled
    grad_query_part = (jnp.sum(dlogit[..., None] * key_rows, axis=(0, 1)) * score_scale).reshape(
        model_width
    )
    d_proj = jnp.concatenate(
        [
            d_key.reshape(var_count, rows_here, model_width),
            d_value.reshape(var_count, rows_here, model_width),
        ],
        axis=-1,
    ).astype(jnp.bfloat16)
    grad_proj_part = jnp.einsum("vtd,vte->de", embedded, d_proj, preferred_element_type=jnp.float32)
    d_tokens = jnp.einsum("vte,de->vtd", d_proj, agg_kv, preferred_element_type=jnp.float32).astype(
        jnp.bfloat16
    )
    grad_embed_part = jnp.einsum(
        "vtp,vtd->vpd", patches, d_tokens, preferred_element_type=jnp.float32
    )
    grad_offset_part = jnp.sum(d_tokens.astype(jnp.float32), axis=1)
    grad_query_part, grad_proj_part = sum_over_var((grad_query_part, grad_proj_part))
    shares = (
        lax.psum_scatter(
            grad_embed_part.astype(jnp.bfloat16), "space", scatter_dimension=2, tiled=True
        ).astype(jnp.float32),
        lax.psum_scatter(
            grad_offset_part.astype(jnp.bfloat16), "space", scatter_dimension=1, tiled=True
        ).astype(jnp.float32),
        lax.psum_scatter(
            grad_query_part.astype(jnp.bfloat16), "space", scatter_dimension=0, tiled=True
        ).astype(jnp.float32),
        lax.psum_scatter(
            grad_proj_part.astype(jnp.bfloat16), "space", scatter_dimension=1, tiled=True
        ).astype(jnp.float32),
        lax.psum_scatter(
            grad_agg_out_part.astype(jnp.bfloat16), "space", scatter_dimension=1, tiled=True
        ).astype(jnp.float32),
        lax.psum_scatter(
            grad_gain_part.astype(jnp.bfloat16), "space", scatter_dimension=0, tiled=True
        ).astype(jnp.float32),
        lax.psum_scatter(
            grad_qkv_part.astype(jnp.bfloat16), "space", scatter_dimension=0, tiled=True
        ).astype(jnp.float32),
        lax.psum_scatter(
            grad_out_part.astype(jnp.bfloat16), "space", scatter_dimension=1, tiled=True
        ).astype(jnp.float32),
    )
    (
        grad_embed,
        grad_var_embed,
        grad_agg_query,
        grad_agg_kv,
        grad_agg_out,
        grad_norm_gain,
        grad_qkv,
        grad_out_weight,
    ) = shares
    return (
        grad_embed,
        grad_var_embed,
        grad_agg_query,
        grad_agg_kv,
        grad_agg_out,
        grad_norm_gain,
        grad_qkv,
        grad_out_weight,
    )


def solution(mesh):
    return jax.shard_map(
        shards,
        mesh=mesh,
        in_specs=(
            P("var", "space", None),
            P("var", None, None),
            P("var", None),
            P(),
            P(),
            P(),
            P(),
            P(None, "var"),
            P("var", None),
            P("space", None),
        ),
        out_specs=(
            P("var", None, "space"),
            P("var", "space"),
            P("space"),
            P(None, "space"),
            P(None, "space"),
            P("space"),
            P("space", "var"),
            P("var", "space"),
        ),
        check_vma=False,
    )
```

profile of v0, /device:TPU:0, one launch (start us, length us, event | category | flops | bytes accessed | tf_op | source)
XLA Modules:
  0.0 626.4 jit_solution(16406013480835584954)
XLA Ops:
  13.1 6.8 %fusion.8 = f32[6,256,2048]{2,1,0:T(8,128)S(1)} fusion(bf16[6,256,1024]{2,1,0:T(8,128)(2,1)S(1)} %add_convert_fusion, bf16[1024,2048]{1,0:T(8,128)(2,1)S(1)} %copy-done.22), kind=kOutput, calls=%fused_computation.26 | convolution fusion | flops 6442450944 | bytes 19922944 | tf_op jit(solution)/shard_map/vtd,de->vte/dot_general | solution.py:71
  19.9 4.6 copy-done.2
  27.7 6.6 %copy.67 = f32[6,256,1024]{1,2,0:T(8,128)} copy(f32[6,256,1024]{2,1,0:T(8,128)} %slice.30) | data formatting | bytes 12582912 | tf_op jit(solution)/shard_map/slice | solution.py:72
  34.3 3.7 multiply_reduce_fusion.3
  41.2 6.6 %copy.68 = f32[6,256,1024]{2,1,0:T(8,128)} copy(f32[6,256,1024]{1,2,0:T(8,128)} %bitcast.162) | data formatting | bytes 12582912 | tf_op jit(solution)/shard_map/mul | solution.py:78
  47.8 10.7 %fusion.81 = (f32[6,256,1024]{2,1,0:T(8,128)}, f32[256,1024]{1,0:T(8,128)}) fusion(f32[6,256,2048]{2,1,0:T(8,128)} %copy-done.2, f32[6,256,1024]{2,1,0:T(8,128)} %copy.68), kind=kLoop, calls=%fused_computation.106 | loop fusion | flops 2883584 | bytes 19922944 | tf_op jit(solution)/shard_map/slice | solution.py:73
  58.5 10.9 %all-gather.1 = f32[2048,16]{0,1:T(8,128)S(1)} all-gather(f32[256,16]{0,1:T(8,128)S(1)} %get-tuple-element.267), channel_id=3, replica_groups=mesh['var'=8,'space'=4] {'var'}, dimensions={0}, use_global_device_ids=true | all-gather | bytes 147456 | tf_op jit(solution)/shard_map/all_gather | solution.py:19
  69.4 9.5 %all-gather = f32[2048,16]{0,1:T(8,128)S(1)} all-gather(f32[256,16]{0,1:T(8,128)S(1)} %multiply_reduce_fusion.7), channel_id=2, replica_groups=mesh['var'=8,'space'=4] {'var'}, dimensions={0}, use_global_device_ids=true | all-gather | bytes 147456 | tf_op jit(solution)/shard_map/all_gather | solution.py:19
  79.3 36.9 %all-gather.5.cloned.1.call-done = f32[2048,1024]{1,0:T(8,128)} async-done(((f32[256,1024]{1,0:T(8,128)}), f32[2048,1024]{1,0:T(8,128)}) %all-gather.5.cloned.1.call-update) | async-done | bytes 8388624 | tf_op jit(solution)/shard_map/all_gather | solution.py:19
  117.9 22.7 %while.19 = (s32[]{:T(128)}, f32[256,16]{0,1:T(8,128)S(1)}, f32[256,16]{0,1:T(8,128)S(1)}, f32[256,1024]{0,1:T(8,128)S(1)}, f32[8,256,16]{1,0,2:T(8,128)S(1)}, /...) while((s32[]{:T(128)}, f32[256,16]{0,1:T(8,128)S(1)}, ...), condition=%wide.region_5.6_spmd, body=%wide.region_4.5_spmd.sunk | while | flops 811013 | bytes 8618191 | solution.py:24
  144.2 16.1 %all_gather.23 = bf16[1024,256]{0,1:T(8,128)(2,1)S(1)} all-gather(bf16[256,256]{0,1:T(8,128)(2,1)S(1)} %bitcast.182), channel_id=1, replica_groups=mesh['var'=8,'space'=4] {'space'}, dimensions={0}, use_global_device_ids=true | all-gather | bytes 655360 | tf_op jit(solution)/shard_map/all_gather | solution.py:100
  165.9 6.8 %fusion.34 = bf16[1024,2,1,64]{0,3,1,2:T(8,128)(2,1)} fusion(f32[2,256,1024]{2,1,0:T(8,128)} %fusion.58, bf16[256,2,3,64]{0,3,2,1:T(8,128)(2,1)S(1)} %bitcast.180, f32[2,256,1024]{2,1,0:T(8,128)} %get-tuple-element.278, f32[2,256]{1,0:T(2,128)S(1)} %get-tuple-element.277), kind=kOutput, calls=%fused_computation.58 | convolution fusion | flops 70911488 | bytes 8720384 | tf_op jit(solution)/shard_map/htc,thd->chd/dot_general | solution.py:124
  174.6 5.7 fusion.40
  180.4 16.4 %reduce-scatter.8.cloned.1.call-done = bf16[256,256]{0,1:T(8,128)(2,1)} async-done(((bf16[1024,256]{0,1:T(8,128)(2,1)}), bf16[256,256]{0,1:T(8,128)(2,1)}) %reduce-scatter.8.cloned.1.call-update) | async-done | bytes 131088 | tf_op jit(solution)/shard_map/reduce_scatter | solution.py:126
  200.4 6.6 %copy.80 = f32[6,256,1024]{1,2,0:T(8,128)} copy(f32[6,256,1024]{2,1,0:T(8,128)} %get-tuple-element.271) | data formatting | bytes 12582912 | tf_op jit(solution)/shard_map/slice | solution.py:73
  207.0 46.3 %all-reduce.6.cloned.1.call-done = bf16[256,1024]{1,0:T(8,128)(2,1)} async-done(((bf16[256,1024]{1,0:T(8,128)(2,1)}), bf16[256,1024]{1,0:T(8,128)(2,1)}) %all-reduce.6.cloned.1.call-update) | async-done | bytes 524304 | tf_op jit(solution)/shard_map/psum | solution.py:46
  260.3 3.9 multiply_reduce_fusion.1
  267.4 6.5 %copy.81 = f32[6,256,1024]{2,1,0:T(8,128)} copy(f32[6,256,1024]{1,2,0:T(8,128)} %bitcast.163) | data formatting | bytes 12582912 | tf_op jit(solution)/shard_map/mul | solution.py:159
  273.9 6.7 %multiply_reduce_fusion = (f32[1024]{0:T(1024)S(1)}, bf16[6,256,1024]{2,1,0:T(8,128)(2,1)}) fusion(f32[6,256,1024]{2,1,0:T(8,128)} %copy.81, f32[6,256,2048]{2,1,0:T(8,128)} %copy-done.2, f32[1024]{0:T(1024)S(1)} %copy-done.20), kind=kLoop, calls=%fused_computation.17 | loop fusion | flops 7863296 | bytes 15736832 | tf_op jit(solution)/shard_map/reduce_sum | solution.py:161
  283.7 6.6 %copy.82 = f32[6,256,1024]{2,1,0:T(8,128)} copy(f32[6,256,1024]{1,2,0:T(8,128)} %bitcast.164) | data formatting | bytes 12582912 | tf_op jit(solution)/shard_map/mul | solution.py:160
  290.4 4.0 multiply_convert_fusion
  296.1 8.8 %bitcast_convert_fusion = bf16[1024,2048]{1,0:T(8,128)(2,1)} fusion(bf16[6,256,1024]{2,1,0:T(8,128)(2,1)S(1)} %copy-done.5, bf16[6,256,1024]{2,1,0:T(8,128)(2,1)S(1)} %multiply_convert_fusion, bf16[6,256,1024]{2,1,0:T(8,128)(2,1)S(1)} %copy-done.6), kind=kOutput, calls=%fused_computation.15 | convolution fusion | flops 6457131008 | bytes 13631488 | tf_op jit(solution)/shard_map/vtd,vte->de/dot_general | solution.py:171
  309.0 13.1 %fusion.83 = (bf16[6,1024]{1,0:T(8,128)(2,1)}, bf16[6,256,1024]{2,1,0:T(8,128)(2,1)}) fusion(bf16[1024,2048]{1,0:T(8,128)(2,1)} %param.16, bf16[6,256,1024]{2,1,0:T(8,128)(2,1)} %copy-done.8, bf16[6,256,1024]{2,1,0:T(8,128)(2,1)} %get-tuple-element.274), kind=kOutput, calls=%fused_computation.108 | convolution fusion | flops 6458173440 | bytes 13643776 | tf_op jit(solution)/shard_map/vte,de->vtd/dot_general | solution.py:172
  326.2 4.8 convert_bitcast_fusion
  331.1 50.0 %reduce-scatter.20.cloned.1.call-done = bf16[1024,512]{1,0:T(8,128)(2,1)} async-done(((bf16[1024,2048]{1,0:T(8,128)(2,1)}), bf16[1024,512]{1,0:T(8,128)(2,1)}) %reduce-scatter.20.cloned.1.call-update) | async-done | bytes 1048592 | tf_op jit(solution)/shard_map/reduce_scatter | solution.py:190
  382.4 21.5 %reduce-scatter.18.cloned.1.call-done = bf16[128,256]{1,0:T(8,128)(2,1)} async-done(((bf16[128,1024]{1,0:T(8,128)(2,1)}), bf16[128,256]{1,0:T(8,128)(2,1)}) %reduce-scatter.18.cloned.1.call-update) | async-done | bytes 65552 | tf_op jit(solution)/shard_map/reduce_scatter | solution.py:202
  405.4 8.8 %all-reduce.2 = (bf16[1024]{0:T(1024)(128)(2,1)S(1)}, bf16[1024]{0:T(1024)(128)(2,1)S(1)}) all-reduce(bf16[1024]{0:T(1024)(128)(2,1)S(1)} %multiply_convert_fusion.3, bf16[1024]{0:T(1024)(128)(2,1)S(1)} %get-tuple-element.242), channel_id=8, replica_groups=mesh['var'=8,'space'=4] {'space'}, use_global_device_ids=true, to_apply=%region_22.23.clone | all-reduce | flops 2048 | bytes 8192
  414.3 12.3 %psum.24 = bf16[256]{0:T(256)(128)(2,1)S(1)} all-reduce(bf16[256]{0:T(256)(128)(2,1)S(1)} %dynamic-slice.1), channel_id=1, replica_groups=mesh['var'=8,'space'=4] {'var'}, use_global_device_ids=true, to_apply=%region_21.22 | all-reduce | flops 256 | bytes 1024 | tf_op jit(solution)/shard_map/psum | solution.py:46
  429.1 19.1 %reduce-scatter.16.cloned.1.call-done = bf16[256,384]{1,0:T(8,128)(2,1)} async-done(((bf16[1024,384]{1,0:T(8,128)(2,1)}), bf16[256,384]{1,0:T(8,128)(2,1)}) %reduce-scatter.16.cloned.1.call-update) | async-done | bytes 196624 | tf_op jit(solution)/shard_map/reduce_scatter | solution.py:199
  449.9 44.3 %reduce-scatter.14.cloned.1.call-done = bf16[1024,256]{1,0:T(8,128)(2,1)} async-done(((bf16[1024,1024]{1,0:T(8,128)(2,1)}), bf16[1024,256]{1,0:T(8,128)(2,1)}) %reduce-scatter.14.cloned.1.call-update) | async-done | bytes 524304 | tf_op jit(solution)/shard_map/reduce_scatter | solution.py:193
  496.5 59.8 %reduce-scatter.10.cloned.1.call-done = bf16[6,256,256]{1,2,0:T(8,128)(2,1)} async-done(((bf16[6,256,1024]{1,2,0:T(8,128)(2,1)}), bf16[6,256,256]{1,2,0:T(8,128)(2,1)}) %reduce-scatter.10.cloned.1.call-update) | async-done | bytes 786448 | tf_op jit(solution)/shard_map/reduce_scatter | solution.py:181
  558.8 57.5 %all-reduce.8.cloned.1.call-done = bf16[1024,512]{1,0:T(8,128)(2,1)} async-done(((bf16[1024,512]{1,0:T(8,128)(2,1)}), bf16[1024,512]{1,0:T(8,128)(2,1)}) %all-reduce.8.cloned.1.call-update) | async-done | bytes 1048592 | tf_op jit(solution)/shard_map/psum | solution.py:46
  (178 shorter events, 88.7 us)
Async XLA Ops:
  7.2 1.9 copy-start
  7.2 109.0 %all-gather.5.cloned.1.call-start = ((), (), s32[]{:S(2)}) async-start(), calls=%async_computation.14 | async-start | bytes 9437184 | tf_op jit(solution)/shard_map/all_gather | solution.py:19
  9.1 4.0 copy-start.22
  11.3 1.8 copy-start.4
  19.9 4.6 copy-start.2
  27.7 6.6 %copy-start.20 = (f32[1024]{0:T(1024)S(1)}, f32[1024]{0:T(1024)}, u32[]{:S(2)}) copy-start(f32[1024]{0:T(1024)} %param.15) | copy-start | bytes 12292
  47.8 31.3 %copy-start.9 = (bf16[256,1024]{1,0:T(8,128)(2,1)S(1)}, bf16[256,1024]{1,0:T(8,128)(2,1)}, u32[]{:S(2)}) copy-start(bf16[256,1024]{1,0:T(8,128)(2,1)} %param.21) | copy-start | bytes 1572868
  47.8 31.3 %copy-start.19 = (bf16[128,1024]{1,0:T(8,128)(2,1)S(1)}, bf16[128,1024]{1,0:T(8,128)(2,1)}, u32[]{:S(2)}) copy-start(bf16[128,1024]{1,0:T(8,128)(2,1)} %param.20) | copy-start | bytes 786436
  58.5 138.3 %reduce-scatter.8.cloned.1.call-start = ((), (), s32[]{:S(2)}) async-start(), calls=%async_computation.7 | async-start | bytes 655360 | tf_op jit(solution)/shard_map/reduce_scatter | solution.py:126
  140.6 2.9 copy-start.14
  140.6 2.9 copy-start.21
  144.1 21.7 %copy-start.15 = (bf16[256,384]{0,1:T(8,128)(2,1)}, bf16[256,384]{0,1:T(8,128)(2,1)S(1)}, u32[]{:S(2)}) copy-start(bf16[256,384]{0,1:T(8,128)(2,1)S(1)} %copy.73) | copy-start | bytes 589828
  160.2 14.4 %copy-start.12 = (bf16[1024,256]{0,1:T(8,128)(2,1)}, bf16[1024,256]{0,1:T(8,128)(2,1)S(1)}, u32[]{:S(2)}) copy-start(bf16[1024,256]{0,1:T(8,128)(2,1)S(1)} %all_gather.23) | copy-start | bytes 1572868
  174.6 78.7 %all-reduce.6.cloned.1.call-start = ((), (), s32[]{:S(2)}) async-start(), calls=%async_computation.8 | async-start | bytes 1048576 | tf_op jit(solution)/shard_map/psum | solution.py:46
  200.1 181.0 %reduce-scatter.20.cloned.1.call-start = ((), (), s32[]{:S(2)}) async-start(), calls=%async_computation.15 | async-start | bytes 5242880 | tf_op jit(solution)/shard_map/reduce_scatter | solution.py:190
  200.4 54.5 %copy-start.10 = (bf16[256,1024]{1,0:T(8,128)(2,1)S(1)}, bf16[256,1024]{1,0:T(8,128)(2,1)}, u32[]{:S(2)}) copy-start(bf16[256,1024]{1,0:T(8,128)(2,1)} %param.21) | copy-start | bytes 1572868
  283.7 6.6 %copy-start.3 = (f32[256,1024]{1,0:T(8,128)S(1)}, f32[256,1024]{1,0:T(8,128)}, u32[]{:S(2)}) copy-start(f32[256,1024]{1,0:T(8,128)} %fusion.69) | copy-start | bytes 3145732
  290.4 5.7 copy-start.5
  290.4 5.7 copy-start.6
  294.4 1.7 copy-start.8
  304.8 1.0 copy-start.13
  304.8 2.9 copy-start.11
  304.8 99.0 %reduce-scatter.18.cloned.1.call-start = ((), (), s32[]{:S(2)}) async-start(), calls=%async_computation.13 | async-start | bytes 327680 | tf_op jit(solution)/shard_map/reduce_scatter | solution.py:202
  308.7 15.1 %copy-start.16 = (bf16[256,1024]{1,0:T(8,128)(2,1)S(1)}, bf16[256,1024]{1,0:T(8,128)(2,1)}, u32[]{:S(2)}) copy-start(bf16[256,1024]{1,0:T(8,128)(2,1)} %all-reduce.6.cloned.1.call-done) | copy-start | bytes 1572868
  308.7 119.1 %reduce-scatter.12.cloned.1.call-start = ((), (), s32[]{:S(2)}) async-start(), calls=%async_computation.10 | async-start | bytes 20480 | tf_op jit(solution)/shard_map/reduce_scatter | solution.py:184
  322.1 126.1 %reduce-scatter.16.cloned.1.call-start = ((), (), s32[]{:S(2)}) async-start(), calls=%async_computation.12 | async-start | bytes 983040 | tf_op jit(solution)/shard_map/reduce_scatter | solution.py:199
  323.7 2.5 copy-start.7
  323.7 170.5 %reduce-scatter.14.cloned.1.call-start = ((), (), s32[]{:S(2)}) async-start(), calls=%async_computation.11 | async-start | bytes 2621440 | tf_op jit(solution)/shard_map/reduce_scatter | solution.py:193
  326.2 230.1 %reduce-scatter.10.cloned.1.call-start = ((), (), s32[]{:S(2)}) async-start(), calls=%async_computation.9 | async-start | bytes 3932160 | tf_op jit(solution)/shard_map/reduce_scatter | solution.py:181
  331.0 50.1 %copy-start.23 = (u32[32]{0:T(128)S(1)}, u32[32]{0:T(128)}, u32[]{:S(2)}) copy-start(u32[32]{0:T(128)} %constant.77) | copy-start | bytes 388
  331.0 285.3 %all-reduce.8.cloned.1.call-start = ((), (), s32[]{:S(2)}) async-start(), calls=%async_computation.16 | async-start | bytes 2097152 | tf_op jit(solution)/shard_map/psum | solution.py:46
  494.3 124.9 %copy-start.1 = (bf16[6,256,1024]{2,1,0:T(8,128)(2,1)S(1)}, bf16[6,256,1024]{2,1,0:T(8,128)(2,1)}, u32[]{:S(2)}) copy-start(bf16[6,256,1024]{2,1,0:T(8,128)(2,1)} %param.13) | copy-start | bytes 9437188
  (14 other events, 10.9 us)
Sparse Core Ops, SparseCore 0:
  58.6 57.6 all-gather.4
  174.7 22.0 reduce-scatter.7
  200.4 52.8 all-reduce.5
  305.0 76.0 reduce-scatter.19
  383.8 20.0 reduce-scatter.17
  406.6 17.1 reduce-scatter.11
  426.7 21.4 reduce-scatter.15
  451.1 43.1 reduce-scatter.13
  496.7 59.5 reduce-scatter.9
  559.6 56.6 all-reduce.7
where the time goes:
time: 636 us; the launch traced here: 626 us
  waiting for transfers between devices  352 us (55%)
  local copies, waits for them, and re-layouts  83.1 us (13%)
  matrix products  69.8 us (11%)
  blocking collectives  57.6 us (9%)
  other arithmetic  47.1 us (7%)
  between operations  15.6 us (2%)
    psum x2, waiting for transfers between devices, sum_over_var(): lax.psum(for_sending(operand), 'var')  104 us
    reduce_scatter x1, waiting for transfers between devices, shards(): lax.psum_scatter(grad_embed_part.astype(jnp.bfloat16), 'space', scatter_d...  59.8 us
    reduce_scatter x1, waiting for transfers between devices, shards(): lax.psum_scatter(grad_proj_part.astype(jnp.bfloat16), 'space', scatter_di...  50 us
    reduce_scatter x1, waiting for transfers between devices, shards(): lax.psum_scatter(grad_agg_out_part.astype(jnp.bfloat16), 'space', scatter...  44.3 us
    all_gather x1, waiting for transfers between devices, combined_all(): gathered = jax.tree.map(lambda a: lax.all_gather(a, axis), part)  36.9 us
    reduce_scatter x1, waiting for transfers between devices, shards(): lax.psum_scatter(grad_out_part.astype(jnp.bfloat16), 'space', scatter_dim...  21.5 us
    all_gather x2, blocking collectives, combined_all(): gathered = jax.tree.map(lambda a: lax.all_gather(a, axis), part)  20.4 us
    reduce_scatter x1, waiting for transfers between devices, shards(): lax.psum_scatter(grad_qkv_part.astype(jnp.bfloat16), 'space', scatter_dim...  19.1 us
  transfers between devices with their start and end apart: 10, of which 9 were waited for; matrix products, arithmetic and copies ran while one was open for 8% of the time, Pallas kernels for 0%

commit v1 on v0

v1 whole, which is shorter than its diff:
```python
import functools
import math

import jax
import jax.numpy as jnp
from jax import lax
from jax.experimental import pallas as pl
from jax.experimental.pallas import tpu as pltpu
from jax.sharding import PartitionSpec as P

HEADS = 16
LANES = 128
EPSILON = 1e-05
MIB = 1 << 20

F32 = jnp.float32
BF16 = jnp.bfloat16

NN = (((1,), (0,)), ((), ()))
NT = (((1,), (1,)), ((), ()))
TN = (((0,), (0,)), ((), ()))


def mm(a, b, dims=NN):
    return lax.dot_general(a, b, dims, preferred_element_type=F32)


def iota(shape, axis):
    return lax.broadcasted_iota(jnp.int32, shape, axis)


def parts3(x):
    hi = x.astype(BF16).astype(F32)
    rest = x - hi
    mid = rest.astype(BF16).astype(F32)
    return hi, mid, rest - mid


def pack(x, y=None):
    group = iota(x.shape, 1) >> 4
    hi, mid, lo = parts3(x)
    out = jnp.where(group == 0, hi, jnp.where(group == 1, mid, jnp.where(group == 2, lo, 0.0)))
    if y is not None:
        hi, mid, lo = parts3(y)
        out = jnp.where(group == 3, hi, jnp.where(group == 4, mid, jnp.where(group == 5, lo, out)))
    return out.astype(BF16)


def unpack(packed, first_group=0):
    row, column = iota((LANES, LANES), 0), iota((LANES, LANES), 1)
    group = row >> 4
    take = ((row & 15) == (column & 15)) & (group >= first_group) & (group < first_group + 3)
    return mm(packed, jnp.where(take, 1.0, 0.0).astype(BF16))


def spread_matrix(width, size, first=0):
    row, column = iota((LANES, width), 0), iota((LANES, width), 1)
    shift = size.bit_length() - 1
    take = ((row & 15) == ((column + first) >> shift)) & (row < 48)
    return jnp.where(take, 1.0, 0.0).astype(BF16)


def fold_matrix(width, size):
    row, column = iota((width, LANES), 0), iota((width, LANES), 1)
    shift = size.bit_length() - 1
    return jnp.where((column & 15) == (row >> shift), 1.0, 0.0).astype(BF16)


def head_sums(x, fold):
    hi, mid, lo = parts3(x)
    return mm(hi.astype(BF16), fold) + mm(mid.astype(BF16), fold) + mm(lo.astype(BF16), fold)


def call(body, out_shape, limit=32, **kw):
    return pl.pallas_call(
        body,
        out_shape=out_shape,
        compiler_params=pltpu.CompilerParams(vmem_limit_bytes=limit * MIB),
        **kw,
    )


def struct(shape, dtype):
    return jax.ShapeDtypeStruct(shape, dtype)


def cost(flops, moved):
    return pl.CostEstimate(flops=int(flops), bytes_accessed=int(moved), transcendentals=0)


SMEM = pl.BlockSpec(memory_space=pltpu.SMEM)


def xor_rows(me, source, target, count):
    block = target.shape[0] // count
    for k in range(count):
        start = pl.multiple_of((me ^ k) * block, block)
        target[k * block : (k + 1) * block, :] = source[pl.ds(start, block), :]


def swap(x, axis, k, keep=None):
    pairs = [(i, i ^ k) for i in range(lax.axis_size(axis))]
    if keep is not None:
        pairs = [pair for pair in pairs if keep(pair[1])]
    return lax.ppermute(x, axis, pairs)


def gather_direct(x, axis):
    return [x] + [swap(x, axis, k) for k in range(1, lax.axis_size(axis))]


def exchange_direct(blocks, axis):
    return [blocks[0]] + [swap(blocks[k], axis, k) for k in range(1, len(blocks))]


def gather_pairs(x, axis):
    n = lax.axis_size(axis)
    even = {k: (x if k == 0 else swap(x, axis, k)) for k in range(0, n, 2)}
    odd = {k + 1: swap(even[k], axis, 1) for k in range(0, n, 2)}
    return [even[k] if k % 2 == 0 else odd[k] for k in range(n)]


def early_body(n_var, n_space, me_ref, cot_ref, outw_ref, qkvw_ref, dattn_ref, own_ref, wperm_ref, *rest):
    cot_refs, (rows_ref, cols_ref) = rest[:n_space], rest[n_space:]
    me_v, me_s = me_ref[0], me_ref[1]
    xor_rows(me_v, cot_ref, rows_ref, n_var)
    cot = rows_ref[...]
    dattn_ref[...] = mm(cot, outw_ref[...], NT).astype(BF16)
    own_ref[...] = rows_ref[: own_ref.shape[0], :]
    width = cols_ref.shape[2]
    for c in range(n_space):
        cols_ref[c] = cot[:, c * width : (c + 1) * width]
    for k in range(n_space):
        cot_refs[k][...] = cols_ref[me_s ^ k]
    wperm_ref[...] = mm(qkvw_ref[...], head_order(qkvw_ref.shape[1])).astype(BF16)


def head_order(width, size=64):
    heads = width // (3 * size)
    row, column = iota((width, width), 0), iota((width, width), 1)
    take = jnp.zeros((width, width), jnp.bool_)
    for h in range(heads):
        for c in range(3):
            start, target = h * 3 * size + c * size, c * heads * size + h * size
            inside = (column >= target) & (column < target + size)
            take = take | (inside & ((row - start) == (column - target)))
    return jnp.where(take, 1.0, 0.0).astype(BF16)


def forward_body(
    n_var, scale, me_ref, patches_ref, embed_ref, offset_ref, query_ref, wk_ref, wv_ref,
    tokens_ref, value_ref, scores_ref, wback_ref, *rest,
):
    send_refs, (wq_ref, max_ref, sum_ref, acc_ref, rows_ref) = rest[:n_var], rest[n_var:]
    v = pl.program_id(0)
    width = wv_ref.shape[1]
    size = width // HEADS

    @pl.when(v == 0)
    def _():
        fold = fold_matrix(width, size).astype(F32)
        hi, mid, lo = parts3(query_ref[...])
        wq = jnp.zeros((width, LANES), F32)
        for part in (hi, mid, lo):
            wq = wq + mm(wk_ref[...], (part * fold).astype(BF16))
        hi, mid, lo = parts3(wq * scale)
        wq_ref[:, :LANES] = hi.astype(BF16)
        wq_ref[:, LANES : 2 * LANES] = mid.astype(BF16)
        wq_ref[:, 2 * LANES :] = lo.astype(BF16)
        group = iota((width, LANES), 1) >> 4
        back = jnp.where((group == 0) | (group == 2), hi, jnp.where(group == 1, mid, 0.0))
        wback_ref[...] = back.astype(BF16)

    xor_rows(me_ref[0], patches_ref.at[0], rows_ref, n_var)
    tokens = (mm(rows_ref[...], embed_ref[0]) + offset_ref[0]).astype(BF16)
    tokens_ref[0] = tokens
    pieces = mm(tokens, wq_ref[...])
    scores = pieces[:, :LANES] + pieces[:, LANES : 2 * LANES] + pieces[:, 2 * LANES :]
    scores_ref[0] = scores
    value = mm(tokens, wv_ref[...])
    value_ref[0] = value

    @pl.when(v == 0)
    def _():
        max_ref[...] = scores
        sum_ref[...] = jnp.ones_like(scores)
        acc_ref[...] = value

    @pl.when(v > 0)
    def _():
        spread = spread_matrix(width, size)
        new_max = jnp.maximum(max_ref[...], scores)
        old = jnp.exp(max_ref[...] - new_max)
        new = jnp.exp(scores - new_max)
        max_ref[...] = new_max
        sum_ref[...] = sum_ref[...] * old + new
        acc_ref[...] = acc_ref[...] * mm(pack(old), spread) + value * mm(pack(new), spread)

    @pl.when(v == pl.num_programs(0) - 1)
    def _():
        block = send_refs[0].shape[0]
        low = iota((block, LANES), 1) < LANES // 2
        for k in range(n_var):
            rows = slice(k * block, (k + 1) * block)
            send_refs[k][:, :width] = acc_ref[rows, :]
            send_refs[k][:, width:] = jnp.where(low, max_ref[rows, :], sum_ref[rows, :])


def pool_body(n_var, *refs):
    ins, (mixed_ref, packet_ref) = refs[:n_var], refs[n_var:]
    width = mixed_ref.shape[1]
    low = iota((mixed_ref.shape[0], LANES), 1) < LANES // 2
    maxima, sums = [], []
    for ref in ins:
        both = ref[:, width:]
        turned = pltpu.roll(both, LANES // 2, 1)
        maxima.append(jnp.where(low, both, turned))
        sums.append(jnp.where(low, turned, both))
    top = functools.reduce(jnp.maximum, maxima)
    factors = [jnp.exp(m - top) for m in maxima]
    total = sum(s * f for s, f in zip(sums, factors))
    spread = spread_matrix(width, width // HEADS)
    mixed = jnp.zeros(mixed_ref.shape, F32)
    for ref, factor in zip(ins, factors):
        mixed = mixed + ref[:, :width] * mm(pack(factor / total), spread)
    mixed_ref[...] = mixed
    packet_ref[:, :width] = mixed.astype(BF16)
    packet_ref[:, width:] = pack(top, total)


def norm_body(n_var, n_space, me_ref, *refs):
    ins = refs[:n_var]
    agg_ref, gain_ref, w_ref, pooled_ref, stats_ref, qkv_ref, centred_ref, inv_ref = refs[n_var : n_var + 8]
    normed_refs, (cols_ref,) = refs[n_var + 8 : n_var + 8 + n_space], refs[n_var + 8 + n_space :]
    width = agg_ref.shape[0]
    block = ins[0].shape[0]
    for k in range(n_var):
        pooled_ref[k * block : (k + 1) * block, :] = ins[k][:, :width]
        stats_ref[k * block : (k + 1) * block, :] = ins[k][:, width:]
    joined = mm(pooled_ref[...], agg_ref[...]).astype(BF16).astype(F32)
    mean = jnp.mean(joined, axis=-1, keepdims=True)
    spread_sq = jnp.mean((joined - mean) ** 2, axis=-1, keepdims=True)
    inv = lax.rsqrt(spread_sq + EPSILON)
    centred = (joined - mean) * inv
    normed = (centred * gain_ref[...]).astype(BF16)
    qkv_ref[...] = mm(normed, w_ref[...]).astype(BF16)
    centred_ref[...] = centred[:block, :]
    inv_ref[...] = jnp.broadcast_to(inv[:block, :], inv_ref.shape)
    cols = cols_ref.shape[2]
    for c in range(n_space):
        cols_ref[c] = normed[:, c * cols : (c + 1) * cols]
    for k in range(n_space):
        normed_refs[k][...] = cols_ref[me_ref[1] ^ k]


def attention_body(n_var, n_space, size, scale, *refs):
    qkv_refs, dattn_refs = refs[:n_space], refs[n_space : 2 * n_space]
    w_ref, attn_ref, dqkv_ref = refs[2 * n_space : 2 * n_space + 3]
    dn_refs = refs[2 * n_space + 3 : 2 * n_space + 3 + n_var]
    k_ref, v_ref, dk_ref, dv_ref = refs[2 * n_space + 3 + n_var :]
    rows, group = dattn_refs[0].shape
    heads = group // size
    for b in range(n_space):
        at = slice(b * rows, (b + 1) * rows)
        k_ref[at, :] = qkv_refs[b][:, group : 2 * group]
        v_ref[at, :] = qkv_refs[b][:, 2 * group :]
    lane_head = iota((rows, group), 1) // size if heads > 1 else None
    for b in range(n_space):
        at = slice(b * rows, (b + 1) * rows)
        queries, d_out = qkv_refs[b][:, :group], dattn_refs[b][...]
        attn = dq = None
        for h in range(heads):
            if heads > 1:
                q_h = jnp.where(lane_head == h, queries.astype(F32), 0.0).astype(BF16)
                do_h = jnp.where(lane_head == h, d_out.astype(F32), 0.0).astype(BF16)
            else:
                q_h, do_h = queries, d_out
            logits = mm(q_h, k_ref[...], NT) * scale
            shifted = jnp.exp(logits - jnp.max(logits, axis=-1, keepdims=True))
            probs = shifted * (1.0 / jnp.sum(shifted, axis=-1, keepdims=True))
            probs_b = probs.astype(BF16)
            attn_h = mm(probs_b, v_ref[...])
            dprob = mm(do_h, v_ref[...], NT)
            delta = jnp.sum(probs * dprob, axis=-1, keepdims=True)
            dscore = (probs * (dprob - delta) * scale).astype(BF16)
            dq_h = mm(dscore, k_ref[...])
            dk = mm(dscore, q_h, TN)
            dv = mm(probs_b, do_h, TN)
            if b == 0 and h == 0:
                dk_ref[...] = dk
                dv_ref[...] = dv
            else:
                dk_ref[...] += dk
                dv_ref[...] += dv
            attn = attn_h if attn is None else jnp.where(lane_head == h, attn_h, attn)
            dq = dq_h if dq is None else jnp.where(lane_head == h, dq_h, dq)
        attn_ref[at, :] = attn.astype(BF16)
        dqkv_ref[at, :group] = dq.astype(BF16)
    dqkv_ref[:, group : 2 * group] = dk_ref[...].astype(BF16)
    dqkv_ref[:, 2 * group :] = dv_ref[...].astype(BF16)
    d_normed = mm(dqkv_ref[:rows, :], w_ref[...], NT).astype(BF16)
    block = dn_refs[0].shape[0]
    for k in range(n_var):
        dn_refs[k][...] = d_normed[k * block : (k + 1) * block, :]


def head_grads_body(n_space, *refs):
    normed_refs, cot_refs = refs[:n_space], refs[n_space : 2 * n_space]
    dqkv_ref, attn_ref, gqkv_ref, gout_ref = refs[2 * n_space :]
    rows = normed_refs[0].shape[0]
    order = head_order(dqkv_ref.shape[1])
    natural = mm(dqkv_ref[...], order, NT).astype(BF16)
    gqkv, gout = 0.0, 0.0
    for b in range(n_space):
        at = slice(b * rows, (b + 1) * rows)
        gqkv = gqkv + mm(normed_refs[b][...], natural[at, :], TN)
        gout = gout + mm(attn_ref[at, :], cot_refs[b][...], TN)
    gqkv_ref[...] = gqkv
    gout_ref[...] = gout


def joined_body(n_var, *refs):
    ins = refs[:n_var]
    centred_ref, inv_ref, gain_ref, cot_ref, mixed_ref, agg_ref, packet_ref, dgain_ref = refs[n_var:]
    width = agg_ref.shape[0]
    d_normed = ins[0][...].astype(F32)
    for ref in ins[1:]:
        d_normed = d_normed + ref[...].astype(F32)
    centred = centred_ref[...]
    dgain_ref[...] = jnp.broadcast_to(jnp.sum(d_normed * centred, axis=0, keepdims=True), dgain_ref.shape)
    gained = d_normed * gain_ref[...]
    inner = (
        gained
        - jnp.mean(gained, axis=-1, keepdims=True)
        - centred * jnp.mean(gained * centred, axis=-1, keepdims=True)
    )
    d_joined = (cot_ref[...].astype(F32) + inner * inv_ref[:, :1]).astype(BF16)
    d_pooled = mm(d_joined, agg_ref[...], NT)
    center = head_sums(d_pooled * mixed_ref[...], fold_matrix(width, width // HEADS))
    packet_ref[:, :width] = d_joined
    packet_ref[:, width:] = pack(center)


def backward_body(n_var, n_space, me_ref, *refs):
    packets = refs[:n_var]
    (
        stats_ref, tokens_ref, value_ref, scores_ref, patches_ref, wv_ref, wback_ref, agg_ref,
        djoined_ref, dvalue_ref, dlogit_ref,
    ) = refs[n_var : n_var + 11]
    grad_refs = refs[n_var + 11 : n_var + 11 + n_space]
    dpool_ref, stat_ref, rows_ref, cols_ref = refs[n_var + 11 + n_space :]
    width = agg_ref.shape[0]
    size = width // HEADS

    @pl.when(pl.program_id(0) == 0)
    def _():
        block = packets[0].shape[0]
        for k in range(n_var):
            at = slice(k * block, (k + 1) * block)
            djoined_ref[at, :] = packets[k][:, :width]
            stat_ref[0, at, :] = unpack(packets[k][:, width:])
        dpool_ref[...] = mm(djoined_ref[...], agg_ref[...], NT)
        stat_ref[1] = unpack(stats_ref[...], 0)
        stat_ref[2] = 1.0 / unpack(stats_ref[...], 3)

    xor_rows(me_ref[0], patches_ref.at[0], rows_ref, n_var)
    weight = jnp.exp(scores_ref[0] - stat_ref[1]) * stat_ref[2]
    dweight = head_sums(dpool_ref[...] * value_ref[0], fold_matrix(width, size))
    dlogit = weight * (dweight - stat_ref[0])
    hi = dlogit.astype(BF16).astype(F32)
    lo = (dlogit - hi).astype(BF16)
    dlogit_ref[0, :, :LANES] = hi.astype(BF16)
    dlogit_ref[0, :, LANES:] = lo
    group = iota(dlogit.shape, 1) >> 4
    mixed = jnp.where(group < 2, hi, jnp.where(group == 2, lo.astype(F32), 0.0)).astype(BF16)
    d_value = (mm(pack(weight), spread_matrix(width, size)) * dpool_ref[...]).astype(BF16)
    dvalue_ref[0] = d_value
    d_tokens = (mm(d_value, wv_ref[...], NT) + mm(mixed, wback_ref[...], NT)).astype(BF16)
    grad = mm(rows_ref[...], d_tokens, TN).astype(BF16)
    offset = jnp.sum(d_tokens.astype(F32), axis=0, keepdims=True)
    o_hi, o_mid, o_lo = parts3(offset)
    row = iota((16, width), 0)
    extra = jnp.where(row == 0, o_hi, jnp.where(row == 1, o_mid, jnp.where(row == 2, o_lo, 0.0)))
    extra = extra.astype(BF16)
    cols = cols_ref.shape[2]
    pixels = rows_ref.shape[1]
    for c in range(n_space):
        cols_ref[c, :pixels, :] = grad[:, c * cols : (c + 1) * cols]
        cols_ref[c, pixels:, :] = extra[:, c * cols : (c + 1) * cols]
    for k in range(n_space):
        grad_refs[k][0] = cols_ref[me_ref[1] ^ k]


def value_grad_body(n_var, me_ref, tokens_ref, dvalue_ref, dlogit_ref, *refs):
    out_refs, (all_ref,) = refs[:n_var], refs[n_var:]
    width = tokens_ref.shape[2]
    flat = tokens_ref.shape[0] * tokens_ref.shape[1]
    tokens = tokens_ref[...].reshape(flat, width)
    step = 256
    for c in range(0, width, step):
        all_ref[:, c : c + step] = mm(
            tokens, dvalue_ref[:, :, c : c + step].reshape(flat, step), TN
        ).astype(BF16)
    both = mm(tokens, dlogit_ref[...].reshape(flat, 2 * LANES), TN)
    all_ref[:, width:] = pack(both[:, :LANES] + both[:, LANES:])
    block = out_refs[0].shape[0]
    for k in range(n_var):
        start = pl.multiple_of((me_ref[0] ^ k) * block, block)
        out_refs[k][...] = all_ref[pl.ds(start, block), :]


def out_grad_body(n_space, me_ref, pooled_ref, djoined_ref, dgain_ref, *refs):
    out_refs, (all_ref, cols_ref) = refs[:n_space], refs[n_space:]
    all_ref[...] = mm(pooled_ref[...], djoined_ref[...], TN)
    cols = cols_ref.shape[2]
    block = out_refs[0].shape[0] - 16
    start = pl.multiple_of(me_ref[0] * block, block)
    own = all_ref[pl.ds(start, block), :].astype(BF16)
    hi, mid, lo = parts3(dgain_ref[:1, :])
    row = iota((16, dgain_ref.shape[1]), 0)
    extra = jnp.where(row == 0, hi, jnp.where(row == 1, mid, jnp.where(row == 2, lo, 0.0)))
    extra = extra.astype(BF16)
    for c in range(n_space):
        cols_ref[c, :block, :] = own[:, c * cols : (c + 1) * cols]
        cols_ref[c, block:, :] = extra[:, c * cols : (c + 1) * cols]
    for k in range(n_space):
        out_refs[k][...] = cols_ref[me_ref[1] ^ k]


def out_sum_body(n, *refs):
    total = refs[0][...].astype(F32)
    for ref in refs[1:n]:
        total = total + ref[...].astype(F32)
    out_ref = refs[n]
    block = out_ref.shape[0] - 16
    out_ref[:block, :] = total[:block, :].astype(BF16)
    hi, mid, lo = parts3(jnp.sum(total[block:, :], axis=0, keepdims=True))
    row = iota((16, out_ref.shape[1]), 0)
    extra = jnp.where(row == 0, hi, jnp.where(row == 1, mid, jnp.where(row == 2, lo, 0.0)))
    out_ref[block:, :] = extra.astype(BF16)


def out_final_body(n, me_ref, *refs):
    ins, (grad_ref, gain_ref) = refs[:n], refs[n:]
    block = ins[0].shape[0] - 16
    gain = 0.0
    for k in range(n):
        start = pl.multiple_of((me_ref[0] ^ k) * block, block)
        grad_ref[pl.ds(start, block), :] = ins[k][:block, :].astype(F32)
        gain = gain + jnp.sum(ins[k][block:, :].astype(F32), axis=0, keepdims=True)
    gain_ref[...] = gain


def packet_sum_body(n_out, n_in, *refs):
    width = refs[0].shape[1] - LANES
    for i in range(n_out):
        ins, out = refs[i * n_in : (i + 1) * n_in], refs[n_out * n_in + i]
        out[:, :width] = sum(ref[:, :width].astype(F32) for ref in ins).astype(BF16)
        out[:, width:] = pack(sum(unpack(ref[:, width:]) for ref in ins))


def packet_split_body(n_in, n_space, me_ref, *refs):
    ins, small_ref = refs[:n_in], refs[n_in]
    out_refs, (cols_ref,) = refs[n_in + 1 : n_in + 1 + n_space], refs[n_in + 1 + n_space :]
    width = ins[0].shape[1] - LANES
    total = sum(ref[:, :width].astype(F32) for ref in ins).astype(BF16)
    small_ref[...] = pack(sum(unpack(ref[:, width:]) for ref in ins))
    half = n_space // 2
    cols = cols_ref.shape[2]
    for c in range(half):
        cols_ref[c] = total[:, c * cols : (c + 1) * cols]
    for k in range(n_space):
        out_refs[k][...] = cols_ref[jnp.maximum((me_ref[1] ^ k) - half, 0)]


def space_sum_body(n, *refs):
    small, large, (small_ref, large_ref) = refs[:n], refs[n : 2 * n], refs[2 * n :]
    small_ref[...] = pack(sum(unpack(ref[...]) for ref in small))
    large_ref[...] = sum(ref[...].astype(F32) for ref in large).astype(BF16)


def final_body(n_var, n_space, scale, me_ref, *refs):
    small, large = refs[:n_var], refs[n_var : 2 * n_var]
    query_ref, wk_ref, kv_ref, gq_ref = refs[2 * n_var :]
    me_v, me_s = me_ref[0], me_ref[1]
    half = n_space // 2
    width = wk_ref.shape[1]
    size = width // HEADS
    cols, qcols = kv_ref.shape[1], gq_ref.shape[1]
    place = pl.multiple_of(jnp.minimum(me_s, half - 1) * cols, LANES)
    spread_kv = spread_matrix(cols, size, place)
    qplace = pl.multiple_of(me_s * qcols, LANES)
    spread_q = spread_matrix(qcols, size, qplace)
    query = query_ref[:, pl.ds(place, cols)] * scale
    block = small[0].shape[0]
    total = 0.0
    for k in range(n_var):
        start = pl.multiple_of((me_v ^ k) * block, block)
        packed = small[k][...]
        key_grad = mm(packed, spread_kv) * query
        kv_ref[pl.ds(start, block), :] = jnp.where(me_s < half, key_grad, large[k][...].astype(F32))
        keys = wk_ref[pl.ds(start, block), pl.ds(qplace, qcols)].astype(F32)
        total = total + jnp.sum(mm(packed, spread_q) * keys, axis=0, keepdims=True)
    gq_ref[...] = total * scale


def shards(
    patches, embed_weight, var_embed, agg_query, agg_kv, agg_out, norm_gain, qkv_weight, out_weight, cotangent
):
    n_var, n_space = lax.axis_size("var"), lax.axis_size("space")
    count, rows, pixels = patches.shape
    width = agg_out.shape[0]
    size = width // HEADS
    scale = 1.0 / math.sqrt(size)
    block = rows // n_var
    cols = width // n_space
    group = out_weight.shape[0]
    drows = width // n_var
    positions = rows * n_space
    kv_cols = 2 * width // n_space
    me = jnp.stack([lax.axis_index("var"), lax.axis_index("space")]).astype(jnp.int32)
    gain = norm_gain.reshape(1, width)

    dattn, cot_own, w_heads, *cot_cols = call(
        functools.partial(early_body, n_var, n_space),
        [struct((rows, group), BF16), struct((block, width), BF16), struct(qkv_weight.shape, BF16)]
        + [struct((rows, cols), BF16)] * n_space,
        in_specs=[SMEM] + [pl.BlockSpec(memory_space=pltpu.VMEM)] * 3,
        scratch_shapes=[pltpu.VMEM((rows, width), BF16), pltpu.VMEM((n_space, rows, cols), BF16)],
        cost_estimate=cost(2e8, 4e6),
        name="early",
    )(me, cotangent, out_weight, qkv_weight)
    dattn_all = gather_direct(dattn, "space")
    cot_all = exchange_direct(cot_cols, "space")

    whole = lambda shape: pl.BlockSpec(shape, lambda v: (0,) * len(shape))
    each = lambda shape: pl.BlockSpec((1,) + shape, lambda v: (v,) + (0,) * len(shape))
    packet = width + LANES
    tokens, value, scores, w_back, *sends = call(
        functools.partial(forward_body, n_var, scale),
        [
            struct((count, rows, width), BF16),
            struct((count, rows, width), F32),
            struct((count, rows, LANES), F32),
            struct((width, LANES), BF16),
        ]
        + [struct((block, packet), F32)] * n_var,
        limit=48,
        grid=(count,),
        in_specs=[
            SMEM,
            each((rows, pixels)),
            each((pixels, width)),
            each((1, width)),
            whole((width, 1)),
            pl.BlockSpec((width, width), lambda v: (0, 0)),
            pl.BlockSpec((width, width), lambda v: (0, 1)),
        ],
        out_specs=[each((rows, width)), each((rows, width)), each((rows, LANES)), whole((width, LANES))]
        + [whole((block, packet))] * n_var,
        scratch_shapes=[
            pltpu.VMEM((width, 3 * LANES), BF16),
            pltpu.VMEM((rows, LANES), F32),
            pltpu.VMEM((rows, LANES), F32),
            pltpu.VMEM((rows, width), F32),
            pltpu.VMEM((rows, pixels), BF16),
        ],
        cost_estimate=cost(6e9, 2e7),
        name="forward",
    )(me, patches, embed_weight, var_embed.reshape(count, 1, width), agg_query.reshape(width, 1), agg_kv, agg_kv)

    received = exchange_direct(sends, "var")
    mixed, pooled_packet = call(
        functools.partial(pool_body, n_var),
        [struct((block, width), F32), struct((block, packet), BF16)],
        cost_estimate=cost(1e8, 3e6),
        name="pool",
    )(*received)
    pooled_packets = gather_direct(pooled_packet, "var")

    vmem = pl.BlockSpec(memory_space=pltpu.VMEM)
    pooled, stats, qkv, centred, inv, *normed_cols = call(
        functools.partial(norm_body, n_var, n_space),
        [
            struct((rows, width), BF16),
            struct((rows, LANES), BF16),
            struct((rows, 3 * group), BF16),
            struct((block, width), F32),
            struct((block, LANES), F32),
        ]
        + [struct((rows, cols), BF16)] * n_space,
        in_specs=[SMEM] + [vmem] * (n_var + 3),
        scratch_shapes=[pltpu.VMEM((n_space, rows, cols), BF16)],
        cost_estimate=cost(8e8, 5e6),
        name="norm",
    )(me, *pooled_packets, agg_out, gain, w_heads)

    qkv_all = gather_direct(qkv, "space")
    normed_all = exchange_direct(normed_cols, "space")
    attn, dqkv, *dn_blocks = call(
        functools.partial(attention_body, n_var, n_space, size, scale),
        [struct((positions, group), BF16), struct((positions, 3 * group), BF16)]
        + [struct((block, width), BF16)] * n_var,
        limit=48,
        scratch_shapes=[pltpu.VMEM((positions, group), BF16)] * 2 + [pltpu.VMEM((positions, group), F32)] * 2,
        cost_estimate=cost(6e9, 4e6),
        name="attention",
    )(*qkv_all, *dattn_all, w_heads)

    dn_all = exchange_direct(dn_blocks, "var")
    grad_qkv, grad_out = call(
        functools.partial(head_grads_body, n_space),
        [struct((cols, 3 * group), F32), struct((group, cols), F32)],
        cost_estimate=cost(1e9, 3e6),
        name="head_grads",
    )(*normed_all, *cot_all, dqkv, attn)

    joined_packet, dgain = call(
        functools.partial(joined_body, n_var),
        [struct((block, packet), BF16), struct((8, width), F32)],
        cost_estimate=cost(2e8, 3e6),
        name="joined",
    )(*dn_all, centred, inv, gain, cot_own, mixed, agg_out)
    joined_packets = gather_direct(joined_packet, "var")

    d_joined, d_value, d_logit, *embed_blocks = call(
        functools.partial(backward_body, n_var, n_space),
        [
            struct((rows, width), BF16),
            struct((count, rows, width), BF16),
            struct((count, rows, 2 * LANES), BF16),
        ]
        + [struct((count, pixels + 16, cols), BF16)] * n_space,
        limit=48,
        grid=(count,),
        in_specs=[SMEM]
        + [whole((block, packet))] * n_var
        + [
            whole((rows, LANES)),
            each((rows, width)),
            each((rows, width)),
            each((rows, LANES)),
            each((rows, pixels)),
            pl.BlockSpec((width, width), lambda v: (0, 1)),
            whole((width, LANES)),
            whole((width, width)),
        ],
        out_specs=[whole((rows, width)), each((rows, width)), each((rows, 2 * LANES))]
        + [each((pixels + 16, cols))] * n_space,
        scratch_shapes=[
            pltpu.VMEM((rows, width), F32),
            pltpu.VMEM((3, rows, LANES), F32),
            pltpu.VMEM((rows, pixels), BF16),
            pltpu.VMEM((n_space, pixels + 16, cols), BF16),
        ],
        cost_estimate=cost(8e9, 2e7),
        name="backward",
    )(me, *joined_packets, stats, tokens, value, scores, patches, agg_kv, w_back, agg_out)

    blocks, bit = list(embed_blocks), 1
    mine = [blocks[0]]
    while bit < n_space:
        arrived = {k ^ bit: swap(blocks[k], "space", bit) for k in range(n_space) if k & bit and k % bit == 0}
        mine.append(arrived[0])
        for k in arrived:
            if k:
                blocks[k] = (blocks[k].astype(F32) + arrived[k].astype(F32)).astype(BF16)
        bit *= 2
    embed_sum = sum(part.astype(F32) for part in mine)
    grad_embed = embed_sum[:, :pixels, :]
    grad_var_embed = jnp.sum(embed_sum[:, pixels:, :], axis=1)

    kv_blocks = call(
        functools.partial(value_grad_body, n_var),
        [struct((drows, packet), BF16)] * n_var,
        limit=48,
        in_specs=[SMEM] + [vmem] * 3,
        scratch_shapes=[pltpu.VMEM((width, packet), BF16)],
        cost_estimate=cost(4e9, 1e7),
        name="value_grad",
    )(me, tokens, d_value, d_logit)
    pair = [swap(kv_blocks[k], "var", 1) for k in range(1, n_var, 2)]
    halves = call(
        functools.partial(packet_sum_body, n_var // 2, 2),
        [struct((drows, packet), BF16)] * (n_var // 2),
        cost_estimate=cost(1e7, 3e6),
        name="pair_sum",
    )(*[x for k in range(n_var // 2) for x in (kv_blocks[2 * k], pair[k])])
    kv_parts = [halves[0]] + [swap(halves[k], "var", 2 * k) for k in range(1, n_var // 2)]
    small, *large = call(
        functools.partial(packet_split_body, n_var // 2, n_space),
        [struct((drows, LANES), BF16)] + [struct((drows, kv_cols), BF16)] * n_space,
        in_specs=[SMEM] + [vmem] * (n_var // 2),
        scratch_shapes=[pltpu.VMEM((n_space // 2, drows, kv_cols), BF16)],
        cost_estimate=cost(1e7, 3e6),
        name="packet_split",
    )(me, *kv_parts)
    small_all = gather_direct(small, "space")
    large_all = [large[0]] + [
        swap(large[k], "space", k, lambda target: target >= n_space // 2) for k in range(1, n_space)
    ]
    small, large = call(
        functools.partial(space_sum_body, n_space),
        [struct((drows, LANES), BF16), struct((drows, kv_cols), BF16)],
        cost_estimate=cost(1e7, 1e6),
        name="space_sum",
    )(*small_all, *large_all)

    out_blocks = call(
        functools.partial(out_grad_body, n_space),
        [struct((drows + 16, cols), BF16)] * n_space,
        in_specs=[SMEM] + [vmem] * 3,
        scratch_shapes=[pltpu.VMEM((width, width), F32), pltpu.VMEM((n_space, drows + 16, cols), BF16)],
        cost_estimate=cost(6e8, 4e6),
        name="out_grad",
    )(me, pooled, d_joined, dgain)
    out_all = exchange_direct(out_blocks, "space")
    out_part = call(
        functools.partial(out_sum_body, n_space),
        struct((drows + 16, cols), BF16),
        cost_estimate=cost(1e6, 3e5),
        name="out_sum",
    )(*out_all)
    out_parts = gather_direct(out_part, "var")
    grad_agg_out, grad_gain = call(
        functools.partial(out_final_body, n_var),
        [struct((width, cols), F32), struct((1, cols), F32)],
        in_specs=[SMEM] + [vmem] * n_var,
        cost_estimate=cost(1e6, 2e6),
        name="out_final",
    )(me, *out_parts)

    smalls, larges = gather_pairs(small, "var"), gather_pairs(large, "var")
    grad_agg_kv, grad_query = call(
        functools.partial(final_body, n_var, n_space, scale),
        [struct((width, kv_cols), F32), struct((1, cols), F32)],
        grid=(1,),
        in_specs=[SMEM] + [vmem] * (2 * n_var + 1) + [pl.BlockSpec((width, width), lambda i: (0, 0))],
        cost_estimate=cost(2e8, 5e6),
        name="final",
    )(me, *smalls, *larges, agg_query.reshape(1, width), agg_kv)

    return (
        grad_embed,
        grad_var_embed,
        grad_query.reshape(cols),
        grad_agg_kv,
        grad_agg_out,
        grad_gain.reshape(cols),
        grad_qkv,
        grad_out,
    )


def solution(mesh):
    return jax.shard_map(
        shards,
        mesh=mesh,
        in_specs=(
            P("var", "space", None),
            P("var", None, None),
            P("var", None),
            P(),
            P(),
            P(),
            P(),
            P(None, "var"),
            P("var", None),
            P("space", None),
        ),
        out_specs=(
            P("var", None, "space"),
            P("var", "space"),
            P("space"),
            P(None, "space"),
            P(None, "space"),
            P("space"),
            P("space", "var"),
            P("var", "space"),
        ),
        check_vma=False,
    )
```

time: 636 us -> 263 us (0.41); the launches traced: 626 us -> 261 us
  waiting for transfers between devices: 352 us -> 104 us
  starting transfers between devices: 0.88 us -> 88 us
  local copies, waits for them, and re-layouts: 83.1 us -> 4.1 us
  matrix products: 69.8 us -> 0 us
  Pallas kernels: 0 us -> 62.8 us
  blocking collectives: 57.6 us -> 0 us
  other arithmetic: 47.1 us -> 1.24 us
  between operations: 15.6 us -> 0.99 us
    reduce_scatter x7 -> x0, waiting for transfers between devices: 211 us -> none  [the longest x1 59.8 us: shards(): lax.psum_scatter(grad_embed_part.astype(jnp.bfloat16), 'space', scatter_d...]
    ppermute x0 -> x80, waiting for transfers between devices: none -> 104 us  [swap(): return lax.ppermute(x, axis, pairs)]
    psum x2 -> x0, waiting for transfers between devices: 104 us -> none  [sum_over_var(): lax.psum(for_sending(operand), 'var')]
    ppermute x0 -> x80, starting transfers between devices: none -> 88 us  [swap(): return lax.ppermute(x, axis, pairs)]
    dot_general x18 -> x0, matrix products: 67.7 us -> none  [the longest x1 13.1 us: shards(): jnp.einsum('vte,de->vtd', d_proj, agg_kv, preferred_element_type=jnp.floa...]
    pallas_call x0 -> x16, Pallas kernels: none -> 62.8 us  [the longest x1 15.1 us: shards(): call(functools.partial(forward_body, n_var, scale), [struct((count, rows,...]
    all_gather x1 -> x0, waiting for transfers between devices: 36.9 us -> none  [combined_all(): gathered = jax.tree.map(lambda a: lax.all_gather(a, axis), part)]
    all_gather x3 -> x0, blocking collectives: 36.4 us -> none  [the longest x2 20.4 us: combined_all(): gathered = jax.tree.map(lambda a: lax.all_gather(a, axis), part)]
  transfers between devices with their start and end apart: 10 -> 80, of which waited for: 9 -> 36; matrix products, arithmetic and copies ran while one was open for 8% -> 0% of each run, Pallas kernels for 0% -> 12%
where the time goes in v1:
time: 263 us; the launch traced here: 261 us
  waiting for transfers between devices  104 us (40%)
  starting transfers between devices  88 us (33%)
  Pallas kernels  62.8 us (24%)
  local copies, waits for them, and re-layouts  4.1 us (2%)
    ppermute x80, waiting for transfers between devices, swap(): return lax.ppermute(x, axis, pairs)  104 us
    ppermute x80, starting transfers between devices, swap(): return lax.ppermute(x, axis, pairs)  88 us
    pallas_call x1, Pallas kernels, shards(): call(functools.partial(forward_body, n_var, scale), [struct((count, rows,...  15.1 us
    pallas_call x1, Pallas kernels, shards(): call(functools.partial(backward_body, n_var, n_space), [struct((rows, wid...  14.9 us
    pallas_call x1, Pallas kernels, shards(): call(functools.partial(attention_body, n_var, n_space, size, scale), [str...  11.7 us
    pallas_call x1, Pallas kernels, shards(): call(functools.partial(value_grad_body, n_var), [struct((drows, packet),...  7.31 us
  transfers between devices with their start and end apart: 80, of which 36 were waited for; matrix products, arithmetic and copies ran while one was open for 0% of the time, Pallas kernels for 12%

profile of v1, /device:TPU:0, one launch (start us, length us, event | category | flops | bytes accessed | tf_op | source)
XLA Modules:
  0.0 261.1 jit_solution(14499372334137635084)
XLA Ops:
  3.5 15.1 %forward.1 = (bf16[6,256,1024]{2,1,0:T(8,128)(2,1)}, f32[6,256,1024]{2,1,0:T(8,128)}, f32[6,256,128]{2,1,0:T(8,128)S(1)}, bf16[1024,128]{1,0:T(8,128)(2,1)S(1)},...) custom-call(s32[2]{0:T(128)S(1)} %pad_add_fusion.me_ref, ...), custom_call_target="tpu_custom_call" | custom-call | flops 6000000000 | bytes 20000000 | tf_op jit(solution)/shard_map/forward/pallas_call | solution.py:539
  19.2 2.6 collective-permute-start.1
  23.6 2.6 collective-permute-start.5
  29.1 7.6 %collective-permute-done.4.refs_5_ = f32[32,1152]{1,0:T(8,128)S(1)} collective-permute-done((f32[32,1152]{1,0:T(8,128)S(1)}, f32[32,1152]{1,0:T(8,128)S(1)}, u32[]{:S(2)}, u32[]{:S(2)}) %collective-permute-start.4) | collective-permute-done | bytes 147488 | tf_op jit(solution)/shard_map/ppermute | solution.py:105
  37.1 2.9 %collective-permute-start.13 = (bf16[32,1152]{1,0:T(8,128)(2,1)S(1)}, bf16[32,1152]{1,0:T(8,128)(2,1)S(1)}, u32[]{:S(2)}, u32[]{:S(2)}) collective-permute-start(bf16[32,1152]{1,0:T(8,128)(2,1)S(1)} %get-tuple-element.94.refs_0_), channel_id=1, source_target_pairs={{0,28},{4,24},{8,20},{12,16},{16,12},{20,8},{24,4},{28,0},{1,29},{... | collective-permute-start | bytes 221192 | tf_op jit(solution)/shard_map/ppermute | solution.py:105
  48.2 2.0 norm.1
  50.2 3.7 %collective-permute-start.16 = (bf16[256,384]{1,0:T(8,128)(2,1)S(1)}, bf16[256,384]{1,0:T(8,128)(2,1)S(1)}, u32[]{:S(2)}, u32[]{:S(2)}) collective-permute-start(bf16[256,384]{1,0:T(8,128)(2,1)S(1)} %get-tuple-element.96.refs_0_), channel_id=1, source_target_pairs={{0,3},{1,2},{2,1},{3,0},{4,7},{5,6},{6,5},{7,4},{8,11},{9,10},{10,... | collective-permute-start | bytes 589832 | tf_op jit(solution)/shard_map/ppermute | solution.py:105
  54.6 3.6 %collective-permute-start.19 = (bf16[256,128]{1,0:T(8,128)(2,1)S(1)}, bf16[256,128]{1,0:T(8,128)(2,1)S(1)}, u32[]{:S(2)}, u32[]{:S(2)}) collective-permute-start(bf16[256,128]{1,0:T(8,128)(2,1)S(1)} %get-tuple-element.97.refs_4_), channel_id=1, source_target_pairs={{0,3},{1,2},{2,1},{3,0},{4,7},{5,6},{6,5},{7,4},{8,11},{9,10},{10,... | collective-permute-start | bytes 196616 | tf_op jit(solution)/shard_map/ppermute | solution.py:105
  58.3 11.4 %collective-permute-done.19.refs_7_ = bf16[256,128]{1,0:T(8,128)(2,1)S(1)} collective-permute-done((bf16[256,128]{1,0:T(8,128)(2,1)S(1)}, bf16[256,128]{1,0:T(8,128)(2,1)S(1)}, u32[]{:S(2)}, u32[]{:S(2)}) %collective-permute-start.19) | collective-permute-done | bytes 65568 | tf_op jit(solution)/shard_map/ppermute | solution.py:105
  69.7 6.5 %collective-permute-start.17 = (bf16[256,128]{1,0:T(8,128)(2,1)S(1)}, bf16[256,128]{1,0:T(8,128)(2,1)S(1)}, u32[]{:S(2)}, u32[]{:S(2)}) collective-permute-start(bf16[256,128]{1,0:T(8,128)(2,1)S(1)} %get-tuple-element.97.refs_4_), channel_id=1, source_target_pairs={{0,1},{1,0},{2,3},{3,2},{4,5},{5,4},{6,7},{7,6},{8,9},{9,8},{10,11... | collective-permute-start | bytes 196616 | tf_op jit(solution)/shard_map/ppermute | solution.py:105
  76.5 2.0 collective-permute-done.17.refs_5_
  78.5 11.7 %attention.1 = (bf16[1024,128]{1,0:T(8,128)(2,1)S(1)}, bf16[1024,384]{1,0:T(8,128)(2,1)S(1)}, bf16[32,1024]{1,0:T(8,128)(2,1)S(1)}, bf16[32,1024]{1,0:T(8,128)(2...) custom-call(bf16[256,384]{1,0:T(8,128)(2,1)S(1)} %get-tuple-element., ...), custom_call_target="tpu_custom_call" | custom-call | flops 6000000000 | bytes 4000000 | tf_op jit(solution)/shard_map/attention/pallas_call | solution.py:600
  93.8 2.1 collective-permute-start.25
  110.6 2.0 collective-permute-start.77
  112.7 14.9 %backward.1 = (bf16[256,1024]{1,0:T(8,128)(2,1)S(1)}, bf16[6,256,1024]{2,1,0:T(8,128)(2,1)}, bf16[6,256,256]{2,1,0:T(8,128)(2,1)S(1)}, bf16[6,272,256]{2,1,0:T(8...) custom-call(s32[2]{0:T(128)S(1)} %pad_add_fusion.me_ref, ...), custom_call_target="tpu_custom_call" | custom-call | flops 8000000000 | bytes 20000000 | tf_op jit(solution)/shard_map/backward/pallas_call | solution.py:626
  127.6 1.9 collective-permute-start.35
  131.0 2.9 %collective-permute-start.65 = (bf16[144,256]{1,0:T(8,128)(2,1)S(1)}, bf16[144,256]{1,0:T(8,128)(2,1)S(1)}, u32[]{:S(2)}, u32[]{:S(2)}) collective-permute-start(bf16[144,256]{1,0:T(8,128)(2,1)S(1)} %get-tuple-element.148), channel_id=1, source_target_pairs={{0,2},{1,3},{2,0},{3,1},{4,6},{5,7},{6,4},{7,5},{8,10},{9,11},{10,... | collective-permute-start | bytes 221192 | tf_op jit(solution)/shard_map/ppermute | solution.py:105
  135.3 7.3 %value_grad.1 = (bf16[128,1152]{1,0:T(8,128)(2,1)S(1)}, bf16[128,1152]{1,0:T(8,128)(2,1)S(1)}, bf16[128,1152]{1,0:T(8,128)(2,1)S(1)}, bf16[128,1152]{1,0:T(8,128...) custom-call(s32[2]{0:T(128)S(1)} %pad_add_fusion.me_ref, ...), custom_call_target="tpu_custom_call" | custom-call | flops 4000000000 | bytes 10000000 | tf_op jit(solution)/shard_map/value_grad/pallas_call | solution.py:673
  142.7 8.7 %collective-permute-done.64.refs_1_ = bf16[144,256]{1,0:T(8,128)(2,1)S(1)} collective-permute-done((bf16[144,256]{1,0:T(8,128)(2,1)S(1)}, bf16[144,256]{1,0:T(8,128)(2,1)S(1)}, u32[]{:S(2)}, u32[]{:S(2)}) %collective-permute-start.64) | collective-permute-done | bytes 73760 | tf_op jit(solution)/shard_map/ppermute | solution.py:105
  151.9 3.3 %collective-permute-done.66.refs_3_ = bf16[144,256]{1,0:T(8,128)(2,1)S(1)} collective-permute-done((bf16[144,256]{1,0:T(8,128)(2,1)S(1)}, bf16[144,256]{1,0:T(8,128)(2,1)S(1)}, u32[]{:S(2)}, u32[]{:S(2)}) %collective-permute-start.66) | collective-permute-done | bytes 73760 | tf_op jit(solution)/shard_map/ppermute | solution.py:105
  155.4 2.5 collective-permute-start.79
  160.4 7.5 %collective-permute-done.78.refs_6_ = bf16[256,256]{1,0:T(8,128)(2,1)S(1)} collective-permute-done((bf16[256,256]{1,0:T(8,128)(2,1)S(1)}, bf16[256,256]{1,0:T(8,128)(2,1)S(1)}, u32[]{:S(2)}, u32[]{:S(2)}) %collective-permute-start.78) | collective-permute-done | bytes 131104 | tf_op jit(solution)/shard_map/ppermute | solution.py:105
  170.6 7.6 %collective-permute-done.75.refs_2_ = bf16[256,256]{1,0:T(8,128)(2,1)S(1)} collective-permute-done((bf16[256,256]{1,0:T(8,128)(2,1)S(1)}, bf16[256,256]{1,0:T(8,128)(2,1)S(1)}, u32[]{:S(2)}, u32[]{:S(2)}) %collective-permute-start.75) | collective-permute-done | bytes 131104 | tf_op jit(solution)/shard_map/ppermute | solution.py:105
  184.7 10.4 %collective-permute-done.42.refs_2_ = bf16[128,1152]{1,0:T(8,128)(2,1)S(1)} collective-permute-done((bf16[128,1152]{1,0:T(8,128)(2,1)S(1)}, bf16[128,1152]{1,0:T(8,128)(2,1)S(1)}, u32[]{:S(2)}, u32[]{:S(2)}) %collective-permute-start.42) | collective-permute-done | bytes 294944 | tf_op jit(solution)/shard_map/ppermute | solution.py:105
  196.8 2.0 collective-permute-start.46
  201.9 19.5 %collective-permute-done.46.refs_3_ = bf16[128,128]{1,0:T(8,128)(2,1)S(1)} collective-permute-done((bf16[128,128]{1,0:T(8,128)(2,1)S(1)}, bf16[128,128]{1,0:T(8,128)(2,1)S(1)}, u32[]{:S(2)}, u32[]{:S(2)}) %collective-permute-start.46) | collective-permute-done | bytes 32800 | tf_op jit(solution)/shard_map/ppermute | solution.py:105
  223.5 4.5 %collective-permute-start.48 = (bf16[128,512]{1,0:T(8,128)(2,1)S(1)}, bf16[128,512]{1,0:T(8,128)(2,1)S(1)}, u32[]{:S(2)}, u32[]{:S(2)}) collective-permute-start(bf16[128,512]{1,0:T(8,128)(2,1)S(1)} %get-tuple-element.137), channel_id=1, source_target_pairs={{0,2},{1,3},{4,6},{5,7},{8,10},{9,11},{12,14},{13,15},{16,18},{17,... | collective-permute-start | bytes 393224 | tf_op jit(solution)/shard_map/ppermute | solution.py:105
  228.0 2.7 %collective-permute-start.49 = (bf16[128,512]{1,0:T(8,128)(2,1)S(1)}, bf16[128,512]{1,0:T(8,128)(2,1)S(1)}, u32[]{:S(2)}, u32[]{:S(2)}) collective-permute-start(bf16[128,512]{1,0:T(8,128)(2,1)S(1)} %get-tuple-element.138), channel_id=1, source_target_pairs={{0,3},{1,2},{4,7},{5,6},{8,11},{9,10},{12,15},{13,14},{16,19},{17,... | collective-permute-start | bytes 393224 | tf_op jit(solution)/shard_map/ppermute | solution.py:105
  240.9 2.3 collective-permute-done.53.refs_4_
  247.9 3.2 %collective-permute-done.60.refs_12_ = bf16[128,512]{1,0:T(8,128)(2,1)S(1)} collective-permute-done((bf16[128,512]{1,0:T(8,128)(2,1)S(1)}, bf16[128,512]{1,0:T(8,128)(2,1)S(1)}, u32[]{:S(2)}, u32[]{:S(2)}) %collective-permute-start.60) | collective-permute-done | bytes 131104 | tf_op jit(solution)/shard_map/ppermute | solution.py:105
  252.9 2.0 head_grads.1
  256.5 2.4 final.1
  (171 shorter events, 78.7 us)
Async XLA Ops:
  23.6 13.1 %collective-permute-start.4 = (f32[32,1152]{1,0:T(8,128)S(1)}, f32[32,1152]{1,0:T(8,128)S(1)}, u32[]{:S(2)}, u32[]{:S(2)}) collective-permute-start(f32[32,1152]{1,0:T(8,128)S(1)} %get-tuple-element.91), channel_id=1, source_target_pairs={{0,20},{4,16},{8,28},{12,24},{16,4},{20,0},{24,12},{28,8},{1,21},{... | collective-permute-start | bytes 442376 | tf_op jit(solution)/shard_map/ppermute | solution.py:105
  23.6 13.1 %collective-permute-start.5 = (f32[32,1152]{1,0:T(8,128)S(1)}, f32[32,1152]{1,0:T(8,128)S(1)}, u32[]{:S(2)}, u32[]{:S(2)}) collective-permute-start(f32[32,1152]{1,0:T(8,128)S(1)} %get-tuple-element.92), channel_id=1, source_target_pairs={{0,24},{4,28},{8,16},{12,20},{16,8},{20,12},{24,0},{28,4},{1,25},{... | collective-permute-start | bytes 442376 | tf_op jit(solution)/shard_map/ppermute | solution.py:105
  26.4 10.2 %collective-permute-start.6 = (f32[32,1152]{1,0:T(8,128)S(1)}, f32[32,1152]{1,0:T(8,128)S(1)}, u32[]{:S(2)}, u32[]{:S(2)}) collective-permute-start(f32[32,1152]{1,0:T(8,128)S(1)} %get-tuple-element.93), channel_id=1, source_target_pairs={{0,28},{4,24},{8,20},{12,16},{16,12},{20,8},{24,4},{28,0},{1,29},{... | collective-permute-start | bytes 442376 | tf_op jit(solution)/shard_map/ppermute | solution.py:105
  50.2 28.3 %collective-permute-start.16 = (bf16[256,384]{1,0:T(8,128)(2,1)S(1)}, bf16[256,384]{1,0:T(8,128)(2,1)S(1)}, u32[]{:S(2)}, u32[]{:S(2)}) collective-permute-start(bf16[256,384]{1,0:T(8,128)(2,1)S(1)} %get-tuple-element.96.refs_0_), channel_id=1, source_target_pairs={{0,3},{1,2},{2,1},{3,0},{4,7},{5,6},{6,5},{7,4},{8,11},{9,10},{10,... | collective-permute-start | bytes 589832 | tf_op jit(solution)/shard_map/ppermute | solution.py:105
  53.9 24.6 %collective-permute-start.15 = (bf16[256,384]{1,0:T(8,128)(2,1)S(1)}, bf16[256,384]{1,0:T(8,128)(2,1)S(1)}, u32[]{:S(2)}, u32[]{:S(2)}) collective-permute-start(bf16[256,384]{1,0:T(8,128)(2,1)S(1)} %get-tuple-element.96.refs_0_), channel_id=1, source_target_pairs={{0,2},{1,3},{2,0},{3,1},{4,6},{5,7},{6,4},{7,5},{8,10},{9,11},{10,... | collective-permute-start | bytes 589832 | tf_op jit(solution)/shard_map/ppermute | solution.py:105
  53.9 24.6 %collective-permute-start.14 = (bf16[256,384]{1,0:T(8,128)(2,1)S(1)}, bf16[256,384]{1,0:T(8,128)(2,1)S(1)}, u32[]{:S(2)}, u32[]{:S(2)}) collective-permute-start(bf16[256,384]{1,0:T(8,128)(2,1)S(1)} %get-tuple-element.96.refs_0_), channel_id=1, source_target_pairs={{0,1},{1,0},{2,3},{3,2},{4,5},{5,4},{6,7},{7,6},{8,9},{9,8},{10,11... | collective-permute-start | bytes 589832 | tf_op jit(solution)/shard_map/ppermute | solution.py:105
  54.6 15.1 %collective-permute-start.19 = (bf16[256,128]{1,0:T(8,128)(2,1)S(1)}, bf16[256,128]{1,0:T(8,128)(2,1)S(1)}, u32[]{:S(2)}, u32[]{:S(2)}) collective-permute-start(bf16[256,128]{1,0:T(8,128)(2,1)S(1)} %get-tuple-element.97.refs_4_), channel_id=1, source_target_pairs={{0,3},{1,2},{2,1},{3,0},{4,7},{5,6},{6,5},{7,4},{8,11},{9,10},{10,... | collective-permute-start | bytes 196616 | tf_op jit(solution)/shard_map/ppermute | solution.py:105
  58.3 18.2 %collective-permute-start.18 = (bf16[256,128]{1,0:T(8,128)(2,1)S(1)}, bf16[256,128]{1,0:T(8,128)(2,1)S(1)}, u32[]{:S(2)}, u32[]{:S(2)}) collective-permute-start(bf16[256,128]{1,0:T(8,128)(2,1)S(1)} %get-tuple-element.97.refs_4_), channel_id=1, source_target_pairs={{0,2},{1,3},{2,0},{3,1},{4,6},{5,7},{6,4},{7,5},{8,10},{9,11},{10,... | collective-permute-start | bytes 196616 | tf_op jit(solution)/shard_map/ppermute | solution.py:105
  69.7 8.8 %collective-permute-start.17 = (bf16[256,128]{1,0:T(8,128)(2,1)S(1)}, bf16[256,128]{1,0:T(8,128)(2,1)S(1)}, u32[]{:S(2)}, u32[]{:S(2)}) collective-permute-start(bf16[256,128]{1,0:T(8,128)(2,1)S(1)} %get-tuple-element.97.refs_4_), channel_id=1, source_target_pairs={{0,1},{1,0},{2,3},{3,2},{4,5},{5,4},{6,7},{7,6},{8,9},{9,8},{10,11... | collective-permute-start | bytes 196616 | tf_op jit(solution)/shard_map/ppermute | solution.py:105
  110.6 32.0 %collective-permute-start.77 = (bf16[256,256]{1,0:T(8,128)(2,1)S(1)}, bf16[256,256]{1,0:T(8,128)(2,1)S(1)}, u32[]{:S(2)}, u32[]{:S(2)}) collective-permute-start(bf16[256,256]{1,0:T(8,128)(2,1)S(1)} %get-tuple-element.157), channel_id=1, source_target_pairs={{0,1},{1,0},{2,3},{3,2},{4,5},{5,4},{6,7},{7,6},{8,9},{9,8},{10,11... | collective-permute-start | bytes 393224 | tf_op jit(solution)/shard_map/ppermute | solution.py:105
  127.6 51.3 %collective-permute-start.35 = (bf16[6,272,256]{2,1,0:T(8,128)(2,1)}, bf16[6,272,256]{2,1,0:T(8,128)(2,1)S(1)}, u32[]{:S(2)}, u32[]{:S(2)}) collective-permute-start(bf16[6,272,256]{2,1,0:T(8,128)(2,1)} %get-tuple-element.119), channel_id=1, source_target_pairs={{0,1},{1,0},{2,3},{3,2},{4,5},{5,4},{6,7},{7,6},{8,9},{9,8},{10,11... | collective-permute-start | bytes 2506760 | tf_op jit(solution)/shard_map/ppermute | solution.py:105
  130.8 20.6 %collective-permute-start.64 = (bf16[144,256]{1,0:T(8,128)(2,1)S(1)}, bf16[144,256]{1,0:T(8,128)(2,1)S(1)}, u32[]{:S(2)}, u32[]{:S(2)}) collective-permute-start(bf16[144,256]{1,0:T(8,128)(2,1)S(1)} %get-tuple-element.147), channel_id=1, source_target_pairs={{0,1},{1,0},{2,3},{3,2},{4,5},{5,4},{6,7},{7,6},{8,9},{9,8},{10,11... | collective-permute-start | bytes 221192 | tf_op jit(solution)/shard_map/ppermute | solution.py:105
  131.0 20.4 %collective-permute-start.65 = (bf16[144,256]{1,0:T(8,128)(2,1)S(1)}, bf16[144,256]{1,0:T(8,128)(2,1)S(1)}, u32[]{:S(2)}, u32[]{:S(2)}) collective-permute-start(bf16[144,256]{1,0:T(8,128)(2,1)S(1)} %get-tuple-element.148), channel_id=1, source_target_pairs={{0,2},{1,3},{2,0},{3,1},{4,6},{5,7},{6,4},{7,5},{8,10},{9,11},{10,... | collective-permute-start | bytes 221192 | tf_op jit(solution)/shard_map/ppermute | solution.py:105
  133.9 21.3 %collective-permute-start.66 = (bf16[144,256]{1,0:T(8,128)(2,1)S(1)}, bf16[144,256]{1,0:T(8,128)(2,1)S(1)}, u32[]{:S(2)}, u32[]{:S(2)}) collective-permute-start(bf16[144,256]{1,0:T(8,128)(2,1)S(1)} %get-tuple-element.149), channel_id=1, source_target_pairs={{0,3},{1,2},{2,1},{3,0},{4,7},{5,6},{6,5},{7,4},{8,11},{9,10},{10,... | collective-permute-start | bytes 221192 | tf_op jit(solution)/shard_map/ppermute | solution.py:105
  142.6 12.6 %collective-permute-start.37 = (bf16[128,1152]{1,0:T(8,128)(2,1)S(1)}, bf16[128,1152]{1,0:T(8,128)(2,1)S(1)}, u32[]{:S(2)}, u32[]{:S(2)}) collective-permute-start(bf16[128,1152]{1,0:T(8,128)(2,1)S(1)} %get-tuple-element.123), channel_id=1, source_target_pairs={{0,4},{4,0},{8,12},{12,8},{16,20},{20,16},{24,28},{28,24},{1,5},{5... | collective-permute-start | bytes 884744 | tf_op jit(solution)/shard_map/ppermute | solution.py:105
  155.2 12.7 %collective-permute-start.78 = (bf16[256,256]{1,0:T(8,128)(2,1)S(1)}, bf16[256,256]{1,0:T(8,128)(2,1)S(1)}, u32[]{:S(2)}, u32[]{:S(2)}) collective-permute-start(bf16[256,256]{1,0:T(8,128)(2,1)S(1)} %get-tuple-element.158), channel_id=1, source_target_pairs={{0,2},{1,3},{2,0},{3,1},{4,6},{5,7},{6,4},{7,5},{8,10},{9,11},{10,... | collective-permute-start | bytes 393224 | tf_op jit(solution)/shard_map/ppermute | solution.py:105
  155.4 13.8 %collective-permute-start.79 = (bf16[256,256]{1,0:T(8,128)(2,1)S(1)}, bf16[256,256]{1,0:T(8,128)(2,1)S(1)}, u32[]{:S(2)}, u32[]{:S(2)}) collective-permute-start(bf16[256,256]{1,0:T(8,128)(2,1)S(1)} %get-tuple-element.159), channel_id=1, source_target_pairs={{0,3},{1,2},{2,1},{3,0},{4,7},{5,6},{6,5},{7,4},{8,11},{9,10},{10,... | collective-permute-start | bytes 393224 | tf_op jit(solution)/shard_map/ppermute | solution.py:105
  157.9 12.4 %collective-permute-start.74 = (bf16[256,256]{1,0:T(8,128)(2,1)S(1)}, bf16[256,256]{1,0:T(8,128)(2,1)S(1)}, u32[]{:S(2)}, u32[]{:S(2)}) collective-permute-start(bf16[256,256]{1,0:T(8,128)(2,1)S(1)} %get-tuple-element.153), channel_id=1, source_target_pairs={{0,1},{1,0},{2,3},{3,2},{4,5},{5,4},{6,7},{7,6},{8,9},{9,8},{10,11... | collective-permute-start | bytes 393224 | tf_op jit(solution)/shard_map/ppermute | solution.py:105
  158.7 19.5 %collective-permute-start.75 = (bf16[256,256]{1,0:T(8,128)(2,1)S(1)}, bf16[256,256]{1,0:T(8,128)(2,1)S(1)}, u32[]{:S(2)}, u32[]{:S(2)}) collective-permute-start(bf16[256,256]{1,0:T(8,128)(2,1)S(1)} %get-tuple-element.154), channel_id=1, source_target_pairs={{0,2},{1,3},{2,0},{3,1},{4,6},{5,7},{6,4},{7,5},{8,10},{9,11},{10,... | collective-permute-start | bytes 393224 | tf_op jit(solution)/shard_map/ppermute | solution.py:105
  167.9 12.7 %collective-permute-start.76 = (bf16[256,256]{1,0:T(8,128)(2,1)S(1)}, bf16[256,256]{1,0:T(8,128)(2,1)S(1)}, u32[]{:S(2)}, u32[]{:S(2)}) collective-permute-start(bf16[256,256]{1,0:T(8,128)(2,1)S(1)} %get-tuple-element.155), channel_id=1, source_target_pairs={{0,3},{1,2},{2,1},{3,0},{4,7},{5,6},{6,5},{7,4},{8,11},{9,10},{10,... | collective-permute-start | bytes 393224 | tf_op jit(solution)/shard_map/ppermute | solution.py:105
  169.2 12.4 %collective-permute-start.73 = (bf16[144,256]{1,0:T(8,128)(2,1)S(1)}, bf16[144,256]{1,0:T(8,128)(2,1)S(1)}, u32[]{:S(2)}, u32[]{:S(2)}) collective-permute-start(bf16[144,256]{1,0:T(8,128)(2,1)S(1)} %out_sum.1.refs_0_), channel_id=1, source_target_pairs={{0,28},{4,24},{8,20},{12,16},{16,12},{20,8},{24,4},{28,0},{1,29},{... | collective-permute-start | bytes 221192 | tf_op jit(solution)/shard_map/ppermute | solution.py:105
  170.3 12.9 %collective-permute-start.41 = (bf16[128,1152]{1,0:T(8,128)(2,1)S(1)}, bf16[128,1152]{1,0:T(8,128)(2,1)S(1)}, u32[]{:S(2)}, u32[]{:S(2)}) collective-permute-start(bf16[128,1152]{1,0:T(8,128)(2,1)S(1)} %get-tuple-element.131), channel_id=1, source_target_pairs={{0,8},{4,12},{8,0},{12,4},{16,24},{20,28},{24,16},{28,20},{1,9},{5... | collective-permute-start | bytes 884744 | tf_op jit(solution)/shard_map/ppermute | solution.py:105
  178.2 16.8 %collective-permute-start.42 = (bf16[128,1152]{1,0:T(8,128)(2,1)S(1)}, bf16[128,1152]{1,0:T(8,128)(2,1)S(1)}, u32[]{:S(2)}, u32[]{:S(2)}) collective-permute-start(bf16[128,1152]{1,0:T(8,128)(2,1)S(1)} %get-tuple-element.132), channel_id=1, source_target_pairs={{0,16},{4,20},{8,24},{12,28},{16,0},{20,4},{24,8},{28,12},{1,17},{... | collective-permute-start | bytes 884744 | tf_op jit(solution)/shard_map/ppermute | solution.py:105
  179.0 16.1 %collective-permute-start.43 = (bf16[128,1152]{1,0:T(8,128)(2,1)S(1)}, bf16[128,1152]{1,0:T(8,128)(2,1)S(1)}, u32[]{:S(2)}, u32[]{:S(2)}) collective-permute-start(bf16[128,1152]{1,0:T(8,128)(2,1)S(1)} %get-tuple-element.133), channel_id=1, source_target_pairs={{0,24},{4,28},{8,16},{12,20},{16,8},{20,12},{24,0},{28,4},{1,25},{... | collective-permute-start | bytes 884744 | tf_op jit(solution)/shard_map/ppermute | solution.py:105
  180.6 78.3 %collective-permute-start.34 = (bf16[6,272,256]{2,1,0:T(8,128)(2,1)S(1)}, bf16[6,272,256]{2,1,0:T(8,128)(2,1)S(1)}, u32[]{:S(2)}, u32[]{:S(2)}) collective-permute-start(bf16[6,272,256]{2,1,0:T(8,128)(2,1)S(1)} %get-tuple-element.117), channel_id=1, source_target_pairs={{0,1},{1,0},{2,3},{3,2},{4,5},{5,4},{6,7},{7,6},{8,9},{9,8},{10,11... | collective-permute-start | bytes 2506760 | tf_op jit(solution)/shard_map/ppermute | solution.py:105
  181.6 77.3 %collective-permute-start.36 = (bf16[6,272,256]{2,1,0:T(8,128)(2,1)S(1)}, bf16[6,272,256]{2,1,0:T(8,128)(2,1)S(1)}, u32[]{:S(2)}, u32[]{:S(2)}) collective-permute-start(bf16[6,272,256]{2,1,0:T(8,128)(2,1)S(1)} %add_convert_fusion), channel_id=1, source_target_pairs={{0,2},{1,3},{2,0},{3,1},{4,6},{5,7},{6,4},{7,5},{8,10},{9,11},{10,... | collective-permute-start | bytes 2506760 | tf_op jit(solution)/shard_map/ppermute | solution.py:105
  183.1 13.6 %collective-permute-start.72 = (bf16[144,256]{1,0:T(8,128)(2,1)S(1)}, bf16[144,256]{1,0:T(8,128)(2,1)S(1)}, u32[]{:S(2)}, u32[]{:S(2)}) collective-permute-start(bf16[144,256]{1,0:T(8,128)(2,1)S(1)} %out_sum.1.refs_0_), channel_id=1, source_target_pairs={{0,24},{4,28},{8,16},{12,20},{16,8},{20,12},{24,0},{28,4},{1,25},{... | collective-permute-start | bytes 221192 | tf_op jit(solution)/shard_map/ppermute | solution.py:105
  196.8 24.6 %collective-permute-start.46 = (bf16[128,128]{1,0:T(8,128)(2,1)S(1)}, bf16[128,128]{1,0:T(8,128)(2,1)S(1)}, u32[]{:S(2)}, u32[]{:S(2)}) collective-permute-start(bf16[128,128]{1,0:T(8,128)(2,1)S(1)} %get-tuple-element.134.refs_0_), channel_id=1, source_target_pairs={{0,3},{1,2},{2,1},{3,0},{4,7},{5,6},{6,5},{7,4},{8,11},{9,10},{10,... | collective-permute-start | bytes 98312 | tf_op jit(solution)/shard_map/ppermute | solution.py:105
  199.4 24.1 %collective-permute-start.45 = (bf16[128,128]{1,0:T(8,128)(2,1)S(1)}, bf16[128,128]{1,0:T(8,128)(2,1)S(1)}, u32[]{:S(2)}, u32[]{:S(2)}) collective-permute-start(bf16[128,128]{1,0:T(8,128)(2,1)S(1)} %get-tuple-element.134.refs_0_), channel_id=1, source_target_pairs={{0,2},{1,3},{2,0},{3,1},{4,6},{5,7},{6,4},{7,5},{8,10},{9,11},{10,... | collective-permute-start | bytes 98312 | tf_op jit(solution)/shard_map/ppermute | solution.py:105
  200.2 27.8 %collective-permute-start.44 = (bf16[128,128]{1,0:T(8,128)(2,1)S(1)}, bf16[128,128]{1,0:T(8,128)(2,1)S(1)}, u32[]{:S(2)}, u32[]{:S(2)}) collective-permute-start(bf16[128,128]{1,0:T(8,128)(2,1)S(1)} %get-tuple-element.134.refs_0_), channel_id=1, source_target_pairs={{0,1},{1,0},{2,3},{3,2},{4,5},{5,4},{6,7},{7,6},{8,9},{9,8},{10,11... | collective-permute-start | bytes 98312 | tf_op jit(solution)/shard_map/ppermute | solution.py:105
  221.4 9.4 %collective-permute-start.47 = (bf16[128,512]{1,0:T(8,128)(2,1)S(1)}, bf16[128,512]{1,0:T(8,128)(2,1)S(1)}, u32[]{:S(2)}, u32[]{:S(2)}) collective-permute-start(bf16[128,512]{1,0:T(8,128)(2,1)S(1)} %get-tuple-element.136), channel_id=1, source_target_pairs={{2,3},{3,2},{6,7},{7,6},{10,11},{11,10},{14,15},{15,14},{18,19},{1... | collective-permute-start | bytes 393224 | tf_op jit(solution)/shard_map/ppermute | solution.py:105
  236.5 11.4 %collective-permute-start.62 = (bf16[128,512]{1,0:T(8,128)(2,1)S(1)}, bf16[128,512]{1,0:T(8,128)(2,1)S(1)}, u32[]{:S(2)}, u32[]{:S(2)}) collective-permute-start(bf16[128,512]{1,0:T(8,128)(2,1)S(1)} %get-tuple-element.140.refs_8_), channel_id=1, source_target_pairs={{0,24},{4,28},{8,16},{12,20},{16,8},{20,12},{24,0},{28,4},{1,25},{... | collective-permute-start | bytes 393224 | tf_op jit(solution)/shard_map/ppermute | solution.py:105
  (58 other events, 490.0 us)

commit v2 on v1

v2 whole, which is shorter than its diff:
```python
import functools
import math

import jax
import jax.numpy as jnp
from jax import lax
from jax.experimental import pallas as pl
from jax.experimental.pallas import tpu as pltpu
from jax.sharding import PartitionSpec as P

HEADS = 16
LANES = 128
EPSILON = 1e-05
MIB = 1 << 20

F32 = jnp.float32
BF16 = jnp.bfloat16

NN = (((1,), (0,)), ((), ()))
NT = (((1,), (1,)), ((), ()))
TN = (((0,), (0,)), ((), ()))


def mm(a, b, dims=NN):
    return lax.dot_general(a, b, dims, preferred_element_type=F32)


def iota(shape, axis):
    return lax.broadcasted_iota(jnp.int32, shape, axis)


def parts3(x):
    hi = x.astype(BF16).astype(F32)
    rest = x - hi
    mid = rest.astype(BF16).astype(F32)
    return hi, mid, rest - mid


def pack(x, y=None):
    group = iota(x.shape, 1) >> 4
    hi, mid, lo = parts3(x)
    out = jnp.where(group == 0, hi, jnp.where(group == 1, mid, jnp.where(group == 2, lo, 0.0)))
    if y is not None:
        hi, mid, lo = parts3(y)
        out = jnp.where(group == 3, hi, jnp.where(group == 4, mid, jnp.where(group == 5, lo, out)))
    return out.astype(BF16)


def unpack(packed, first_group=0):
    row, column = iota((LANES, LANES), 0), iota((LANES, LANES), 1)
    group = row >> 4
    take = ((row & 15) == (column & 15)) & (group >= first_group) & (group < first_group + 3)
    return mm(packed, jnp.where(take, 1.0, 0.0).astype(BF16))


def spread_matrix(width, size, first=0):
    row, column = iota((LANES, width), 0), iota((LANES, width), 1)
    shift = size.bit_length() - 1
    take = ((row & 15) == ((column + first) >> shift)) & (row < 48)
    return jnp.where(take, 1.0, 0.0).astype(BF16)


def fold_matrix(width, size):
    row, column = iota((width, LANES), 0), iota((width, LANES), 1)
    shift = size.bit_length() - 1
    return jnp.where((column & 15) == (row >> shift), 1.0, 0.0).astype(BF16)


def head_sums(x, fold):
    hi, mid, lo = parts3(x)
    return mm(hi.astype(BF16), fold) + mm(mid.astype(BF16), fold) + mm(lo.astype(BF16), fold)


def call(body, out_shape, limit=32, after=(), in_specs=None, **kw):
    def run(*args):
        n, m = len(args), len(after)
        specs = [pl.BlockSpec(memory_space=pltpu.VMEM)] * n if in_specs is None else list(in_specs)
        return pl.pallas_call(
            lambda *refs: body(*refs[:n], *refs[n + m :]),
            out_shape=out_shape,
            in_specs=specs + [pl.BlockSpec(memory_space=pl.ANY)] * m,
            compiler_params=pltpu.CompilerParams(vmem_limit_bytes=limit * MIB),
            **kw,
        )(*args, *after)

    return run


def struct(shape, dtype):
    return jax.ShapeDtypeStruct(shape, dtype)


def cost(flops, moved):
    return pl.CostEstimate(flops=int(flops), bytes_accessed=int(moved), transcendentals=0)


SMEM = pl.BlockSpec(memory_space=pltpu.SMEM)


def swap(x, axis, k, keep=None):
    pairs = [(i, i ^ k) for i in range(lax.axis_size(axis))]
    if keep is not None:
        pairs = [pair for pair in pairs if keep(pair[1])]
    return lax.ppermute(x, axis, pairs)


def gather_direct(x, axis):
    return [x] + [swap(x, axis, k) for k in range(1, lax.axis_size(axis))]


def exchange_direct(blocks, axis):
    return [blocks[0]] + [swap(blocks[k], axis, k) for k in range(1, len(blocks))]


def gather_pairs(x, axis):
    even = jnp.stack([x if k == 0 else swap(x, axis, k) for k in range(0, lax.axis_size(axis), 2)])
    return even, swap(even, axis, 1)


def exchange_all(x, axis):
    return lax.all_to_all(x, axis, split_axis=0, concat_axis=0, tiled=True)


def three_rows(x):
    hi, mid, lo = parts3(x)
    row = iota((16, x.shape[1]), 0)
    return jnp.where(row == 0, hi, jnp.where(row == 1, mid, jnp.where(row == 2, lo, 0.0))).astype(BF16)


def head_order(width, size=64):
    heads = width // (3 * size)
    row, column = iota((width, width), 0), iota((width, width), 1)
    take = jnp.zeros((width, width), jnp.bool_)
    for h in range(heads):
        for c in range(3):
            start, target = h * 3 * size + c * size, c * heads * size + h * size
            inside = (column >= target) & (column < target + size)
            take = take | (inside & ((row - start) == (column - target)))
    return jnp.where(take, 1.0, 0.0).astype(BF16)


def early_body(n_space, me_ref, cot_ref, outw_ref, qkvw_ref, dattn_ref, own_ref, wperm_ref, *rest):
    cot_refs, (cols_ref,) = rest[:n_space], rest[n_space:]
    dattn_ref[...] = mm(cot_ref[...], outw_ref[...], NT).astype(BF16)
    block = own_ref.shape[0]
    own_ref[...] = cot_ref[pl.ds(pl.multiple_of(me_ref[0] * block, block), block), :]
    width = cols_ref.shape[2]
    for c in range(n_space):
        cols_ref[c] = cot_ref[:, c * width : (c + 1) * width]
    for k in range(n_space):
        cot_refs[k][...] = cols_ref[me_ref[1] ^ k]
    wperm_ref[...] = mm(qkvw_ref[...], head_order(qkvw_ref.shape[1])).astype(BF16)


def forward_body(
    count, scale, patches_ref, embed_ref, offset_ref, query_ref, wk_ref, wv_ref,
    tokens_ref, value_ref, scores_ref, wback_ref, send_ref, wq_ref, held_ref, max_ref, spread_ref, acc_ref,
):
    i = pl.program_id(0)
    width = wv_ref.shape[1]
    size = width // HEADS

    @pl.when(i == 0)
    def _():
        row, column = iota((LANES, width), 0), iota((LANES, width), 1)
        own = (row & 15) == (column >> (size.bit_length() - 1))
        wq = jnp.zeros((width, LANES), F32)
        for part in parts3(query_ref[...]):
            wq = wq + mm(wk_ref[...], jnp.where(own, part, 0.0).astype(BF16), NT)
        hi, mid, lo = parts3(wq * scale)
        wq_ref[:, :LANES] = hi.astype(BF16)
        wq_ref[:, LANES : 2 * LANES] = mid.astype(BF16)
        wq_ref[:, 2 * LANES :] = lo.astype(BF16)
        group = iota((width, LANES), 1) >> 4
        back = jnp.where((group == 0) | (group == 2), hi, jnp.where(group == 1, mid, 0.0))
        wback_ref[...] = back.astype(BF16)
        spread_ref[...] = spread_matrix(width, size)

    @pl.when(i < count)
    def _():
        tokens = (mm(patches_ref[0], embed_ref[0]) + offset_ref[pl.ds(i, 1), :]).astype(BF16)
        tokens_ref[0] = tokens
        held_ref[i] = tokens
        pieces = mm(tokens, wq_ref[...])
        scores_ref[i] = pieces[:, :LANES] + pieces[:, LANES : 2 * LANES] + pieces[:, 2 * LANES :]

    @pl.when(i >= count)
    def _():
        j = i - count
        top = scores_ref[0]
        for v in range(1, count):
            top = jnp.maximum(top, scores_ref[v])
        max_ref[...] = top
        value = mm(held_ref[j], wv_ref[...])
        value_ref[0] = value
        term = mm(pack(jnp.exp(scores_ref[j] - top)), spread_ref[...]) * value

        @pl.when(j == 0)
        def _():
            acc_ref[...] = term

        @pl.when(j > 0)
        def _():
            acc_ref[...] += term

    @pl.when(i == 2 * count - 1)
    def _():
        top = max_ref[...]
        total = sum(jnp.exp(scores_ref[v] - top) for v in range(count))
        low = iota(top.shape, 1) < LANES // 2
        send_ref[:, :width] = acc_ref[...]
        send_ref[:, width:] = jnp.where(low, top, total)


def pool_body(n_var, in_ref, mixed_ref, packet_ref):
    block, width = mixed_ref.shape
    low = iota((block, LANES), 1) < LANES // 2
    maxima, sums = [], []
    for k in range(n_var):
        both = in_ref[k * block : (k + 1) * block, width:]
        turned = pltpu.roll(both, LANES // 2, 1)
        maxima.append(jnp.where(low, both, turned))
        sums.append(jnp.where(low, turned, both))
    top = functools.reduce(jnp.maximum, maxima)
    factors = [jnp.exp(m - top) for m in maxima]
    total = sum(s * f for s, f in zip(sums, factors))
    spread = spread_matrix(width, width // HEADS)
    mixed = jnp.zeros(mixed_ref.shape, F32)
    for k, factor in enumerate(factors):
        mixed = mixed + in_ref[k * block : (k + 1) * block, :width] * mm(pack(factor / total), spread)
    mixed_ref[...] = mixed
    pooled, stats = mixed.astype(BF16), pack(top, total)
    for k in range(n_var):
        packet_ref[k * block : (k + 1) * block, :width] = pooled
        packet_ref[k * block : (k + 1) * block, width:] = stats


def norm_body(me_ref, in_ref, agg_ref, gain_ref, w_ref, qkv_ref, normed_ref, centred_ref, inv_ref, all_ref, allinv_ref):
    width = agg_ref.shape[0]
    block = centred_ref.shape[0]
    joined = mm(in_ref[:, :width], agg_ref[...]).astype(BF16).astype(F32)
    mean = jnp.mean(joined, axis=-1, keepdims=True)
    spread_sq = jnp.mean((joined - mean) ** 2, axis=-1, keepdims=True)
    inv = lax.rsqrt(spread_sq + EPSILON)
    centred = (joined - mean) * inv
    normed = (centred * gain_ref[...]).astype(BF16)
    qkv_ref[...] = mm(normed, w_ref[...]).astype(BF16)
    normed_ref[...] = normed
    all_ref[...] = centred
    allinv_ref[...] = jnp.broadcast_to(inv, allinv_ref.shape)
    start = pl.multiple_of(me_ref[0] * block, block)
    centred_ref[...] = all_ref[pl.ds(start, block), :]
    inv_ref[...] = allinv_ref[pl.ds(start, block), :]


def attention_body(n_space, size, scale, me_ref, *refs):
    qkv_refs, dattn_refs = refs[:n_space], refs[n_space : 2 * n_space]
    w_ref, normed_ref, attn_ref, dqkv_ref, dn_ref = refs[2 * n_space : 2 * n_space + 5]
    normed_refs = refs[2 * n_space + 5 : 3 * n_space + 5]
    k_ref, v_ref, dk_ref, dv_ref, cols_ref = refs[3 * n_space + 5 :]
    rows, group = dattn_refs[0].shape
    heads = group // size
    for b in range(n_space):
        at = slice(b * rows, (b + 1) * rows)
        k_ref[at, :] = qkv_refs[b][:, group : 2 * group]
        v_ref[at, :] = qkv_refs[b][:, 2 * group :]
    lane_head = iota((rows, group), 1) // size if heads > 1 else None
    for b in range(n_space):
        at = slice(b * rows, (b + 1) * rows)
        queries, d_out = qkv_refs[b][:, :group], dattn_refs[b][...]
        attn = dq = None
        for h in range(heads):
            if heads > 1:
                q_h = jnp.where(lane_head == h, queries.astype(F32), 0.0).astype(BF16)
                do_h = jnp.where(lane_head == h, d_out.astype(F32), 0.0).astype(BF16)
            else:
                q_h, do_h = queries, d_out
            logits = mm(q_h, k_ref[...], NT) * scale
            shifted = jnp.exp(logits - jnp.max(logits, axis=-1, keepdims=True))
            probs = shifted * (1.0 / jnp.sum(shifted, axis=-1, keepdims=True))
            probs_b = probs.astype(BF16)
            attn_h = mm(probs_b, v_ref[...])
            dprob = mm(do_h, v_ref[...], NT)
            delta = jnp.sum(probs * dprob, axis=-1, keepdims=True)
            dscore = (probs * (dprob - delta) * scale).astype(BF16)
            dq_h = mm(dscore, k_ref[...])
            dk = mm(dscore, q_h, TN)
            dv = mm(probs_b, do_h, TN)
            if b == 0 and h == 0:
                dk_ref[...] = dk
                dv_ref[...] = dv
            else:
                dk_ref[...] += dk
                dv_ref[...] += dv
            attn = attn_h if attn is None else jnp.where(lane_head == h, attn_h, attn)
            dq = dq_h if dq is None else jnp.where(lane_head == h, dq_h, dq)
        attn_ref[at, :] = attn.astype(BF16)
        dqkv_ref[at, :group] = dq.astype(BF16)
    dqkv_ref[:, group : 2 * group] = dk_ref[...].astype(BF16)
    dqkv_ref[:, 2 * group :] = dv_ref[...].astype(BF16)
    dn_ref[...] = mm(dqkv_ref[:rows, :], w_ref[...], NT).astype(BF16)
    cols = cols_ref.shape[2]
    for c in range(n_space):
        cols_ref[c] = normed_ref[:, c * cols : (c + 1) * cols]
    for k in range(n_space):
        normed_refs[k][...] = cols_ref[me_ref[1] ^ k]


def head_grads_body(n_space, *refs):
    normed_refs, cot_refs = refs[:n_space], refs[n_space : 2 * n_space]
    dqkv_ref, attn_ref, gqkv_ref, gout_ref = refs[2 * n_space :]
    rows = normed_refs[0].shape[0]
    order = head_order(dqkv_ref.shape[1])
    natural = mm(dqkv_ref[...], order, NT).astype(BF16)
    gqkv, gout = 0.0, 0.0
    for b in range(n_space):
        at = slice(b * rows, (b + 1) * rows)
        gqkv = gqkv + mm(normed_refs[b][...], natural[at, :], TN)
        gout = gout + mm(attn_ref[at, :], cot_refs[b][...], TN)
    gqkv_ref[...] = gqkv
    gout_ref[...] = gout


def joined_body(n_var, in_ref, centred_ref, inv_ref, gain_ref, cot_ref, mixed_ref, agg_ref, packet_ref, dgain_ref):
    block, width = centred_ref.shape
    d_normed = in_ref[:block, :].astype(F32)
    for k in range(1, n_var):
        d_normed = d_normed + in_ref[k * block : (k + 1) * block, :].astype(F32)
    centred = centred_ref[...]
    dgain_ref[...] = jnp.broadcast_to(jnp.sum(d_normed * centred, axis=0, keepdims=True), dgain_ref.shape)
    gained = d_normed * gain_ref[...]
    inner = (
        gained
        - jnp.mean(gained, axis=-1, keepdims=True)
        - centred * jnp.mean(gained * centred, axis=-1, keepdims=True)
    )
    d_joined = (cot_ref[...].astype(F32) + inner * inv_ref[:, :1]).astype(BF16)
    d_pooled = mm(d_joined, agg_ref[...], NT)
    center = pack(head_sums(d_pooled * mixed_ref[...], fold_matrix(width, width // HEADS)))
    for k in range(n_var):
        packet_ref[k * block : (k + 1) * block, :width] = d_joined
        packet_ref[k * block : (k + 1) * block, width:] = center


def out_grad_body(n_space, me_ref, pooled_ref, djoined_ref, dgain_ref, agg_ref, dpool_ref, stat_ref, *refs):
    out_refs, (all_ref, cols_ref) = refs[:n_space], refs[n_space:]
    width = agg_ref.shape[0]
    all_ref[...] = mm(pooled_ref[:, :width], djoined_ref[:, :width], TN)
    cols = cols_ref.shape[2]
    block = out_refs[0].shape[0] - 16
    start = pl.multiple_of(me_ref[0] * block, block)
    own = all_ref[pl.ds(start, block), :].astype(BF16)
    extra = three_rows(dgain_ref[:1, :])
    for c in range(n_space):
        cols_ref[c, :block, :] = own[:, c * cols : (c + 1) * cols]
        cols_ref[c, block:, :] = extra[:, c * cols : (c + 1) * cols]
    for k in range(n_space):
        out_refs[k][...] = cols_ref[me_ref[1] ^ k]
    dpool_ref[...] = mm(djoined_ref[:, :width], agg_ref[...], NT)
    stat_ref[0] = unpack(djoined_ref[:, width:])
    stat_ref[1] = unpack(pooled_ref[:, width:])
    stat_ref[2] = 1.0 / unpack(pooled_ref[:, width:], 3)


def backward_body(
    n_space, me_ref, dpool_ref, stat_ref, tokens_ref, value_ref, scores_ref, patches_ref, wv_ref, wback_ref,
    dvalue_ref, dlogit_ref, keep_ref, send_ref, spread_ref, fold_ref, cols_ref,
):
    width = wv_ref.shape[0]
    size = width // HEADS

    @pl.when(pl.program_id(0) == 0)
    def _():
        spread_ref[...] = spread_matrix(width, size)
        fold_ref[...] = fold_matrix(width, size)

    weight = jnp.exp(scores_ref[0] - stat_ref[1]) * stat_ref[2]
    d_value = (mm(pack(weight), spread_ref[...]) * dpool_ref[...]).astype(BF16)
    dvalue_ref[0] = d_value
    dweight = head_sums(dpool_ref[...] * value_ref[0], fold_ref[...])
    dlogit = weight * (dweight - stat_ref[0])
    hi = dlogit.astype(BF16).astype(F32)
    lo = (dlogit - hi).astype(BF16)
    dlogit_ref[0, :, :LANES] = hi.astype(BF16)
    dlogit_ref[0, :, LANES:] = lo
    group = iota(dlogit.shape, 1) >> 4
    mixed = jnp.where(group < 2, hi, jnp.where(group == 2, lo.astype(F32), 0.0)).astype(BF16)
    d_tokens = (mm(d_value, wv_ref[...], NT) + mm(mixed, wback_ref[...], NT)).astype(BF16)
    grad = mm(patches_ref[0], d_tokens, TN).astype(BF16)
    extra = three_rows(jnp.sum(d_tokens.astype(F32), axis=0, keepdims=True))
    cols = cols_ref.shape[2]
    pixels = patches_ref.shape[2]
    for c in range(n_space):
        cols_ref[c, :pixels, :] = grad[:, c * cols : (c + 1) * cols]
        cols_ref[c, pixels:, :] = extra[:, c * cols : (c + 1) * cols]
    for k in range(0, n_space, 2):
        keep_ref[k // 2, 0] = cols_ref[me_ref[1] ^ k]
        send_ref[k // 2, 0] = cols_ref[me_ref[1] ^ (k + 1)]


def embed_final_body(parts, *refs):
    ins, (grad_ref, offset_ref) = refs[:-2], refs[-2:]
    pixels = grad_ref.shape[1]
    base = 0
    for half in range(2):
        mine = ins[half * parts : (half + 1) * parts]
        for v in range(mine[0].shape[1]):
            total = 0.0
            for ref in mine:
                total = total + (ref[0, v] if len(ref.shape) == 4 else ref[v]).astype(F32)
            grad_ref[base + v] = total[:pixels, :]
            offset_ref[base + v : base + v + 1, :] = jnp.sum(total[pixels:, :], axis=0, keepdims=True)
        base += mine[0].shape[1]


def value_grad_body(n_var, me_ref, tokens_ref, dv0_ref, dv1_ref, dl0_ref, dl1_ref, keep_ref, send_ref, all_ref):
    width = dv0_ref.shape[2]
    flat = lambda ref: ref[...].reshape(ref.shape[0] * ref.shape[1], ref.shape[2])
    tokens = flat(tokens_ref)
    middle = dv0_ref.shape[0] * dv0_ref.shape[1]
    first, second = tokens[:middle, :], tokens[middle:, :]
    all_ref[:, :width] = (mm(first, flat(dv0_ref), TN) + mm(second, flat(dv1_ref), TN)).astype(BF16)
    both = mm(first, flat(dl0_ref), TN) + mm(second, flat(dl1_ref), TN)
    all_ref[:, width:] = pack(both[:, :LANES] + both[:, LANES:])
    block = keep_ref.shape[1]
    count = all_ref.shape[0] // block
    for r in range(count):
        target = pl.program_id(0) * count + r
        same = (target & 1) == (me_ref[0] & 1)
        slot = target >> 1

        @pl.when(same)
        def _():
            keep_ref[slot] = all_ref[r * block : (r + 1) * block, :]

        @pl.when(jnp.logical_not(same))
        def _():
            send_ref[slot] = all_ref[r * block : (r + 1) * block, :]


def pair_sum_body(n_chip, me_ref, keep_ref, got_ref, *out_refs):
    width = keep_ref.shape[2] - LANES
    for k in range(n_chip):
        slot = (me_ref[0] >> 1) ^ k
        mine, other = keep_ref[slot], got_ref[slot]
        out_refs[k][:, :width] = (mine[:, :width].astype(F32) + other[:, :width].astype(F32)).astype(BF16)
        out_refs[k][:, width:] = pack(unpack(mine[:, width:]) + unpack(other[:, width:]))


def out_sum_body(n, *refs):
    total = refs[0][...].astype(F32)
    for ref in refs[1:n]:
        total = total + ref[...].astype(F32)
    out_ref = refs[n]
    block = out_ref.shape[0] - 16
    out_ref[:block, :] = total[:block, :].astype(BF16)
    out_ref[block:, :] = three_rows(jnp.sum(total[block:, :], axis=0, keepdims=True))


def out_final_body(n, me_ref, even_ref, odd_ref, grad_ref, gain_ref):
    block = even_ref.shape[1] - 16
    gain = 0.0
    for k in range(n):
        part = (odd_ref if k % 2 else even_ref)[k // 2].astype(F32)
        start = pl.multiple_of((me_ref[0] ^ k) * block, block)
        grad_ref[pl.ds(start, block), :] = part[:block, :]
        gain = gain + jnp.sum(part[block:, :], axis=0, keepdims=True)
    gain_ref[...] = gain


def packet_split_body(n_in, n_space, me_ref, *refs):
    ins, small_ref = refs[:n_in], refs[n_in]
    out_refs, (cols_ref,) = refs[n_in + 1 : n_in + 1 + n_space], refs[n_in + 1 + n_space :]
    width = ins[0].shape[1] - LANES
    total = sum(ref[:, :width].astype(F32) for ref in ins).astype(BF16)
    small_ref[...] = pack(sum(unpack(ref[:, width:]) for ref in ins))
    half = n_space // 2
    cols = cols_ref.shape[2]
    for c in range(half):
        cols_ref[c] = total[:, c * cols : (c + 1) * cols]
    for k in range(n_space):
        out_refs[k][...] = cols_ref[jnp.maximum((me_ref[1] ^ k) - half, 0)]


def space_sum_body(n, *refs):
    small, large, out_ref = refs[:n], refs[n : 2 * n], refs[2 * n]
    width = large[0].shape[1]
    out_ref[:, :width] = sum(ref[...].astype(F32) for ref in large).astype(BF16)
    out_ref[:, width:] = pack(sum(unpack(ref[...]) for ref in small))


def final_body(n_var, n_space, scale, me_ref, even_ref, odd_ref, query_ref, wk_ref, kv_ref, gq_ref):
    me_v, me_s = me_ref[0], me_ref[1]
    half = n_space // 2
    width = wk_ref.shape[1]
    size = width // HEADS
    cols, qcols = kv_ref.shape[1], gq_ref.shape[1]
    place = pl.multiple_of(jnp.minimum(me_s, half - 1) * cols, LANES)
    spread_kv = spread_matrix(cols, size, place)
    qplace = pl.multiple_of(me_s * qcols, LANES)
    spread_q = spread_matrix(qcols, size, qplace)
    query = query_ref[:, pl.ds(place, cols)] * scale
    block = even_ref.shape[1]
    total = 0.0
    for k in range(n_var):
        part = (odd_ref if k % 2 else even_ref)[k // 2]
        start = pl.multiple_of((me_v ^ k) * block, block)
        packed = part[:, cols:]
        key_grad = mm(packed, spread_kv) * query
        kv_ref[pl.ds(start, block), :] = jnp.where(me_s < half, key_grad, part[:, :cols].astype(F32))
        keys = wk_ref[pl.ds(start, block), pl.ds(qplace, qcols)].astype(F32)
        total = total + jnp.sum(mm(packed, spread_q) * keys, axis=0, keepdims=True)
    gq_ref[...] = total * scale


def shards(
    patches, embed_weight, var_embed, agg_query, agg_kv, agg_out, norm_gain, qkv_weight, out_weight, cotangent
):
    n_var, n_space = lax.axis_size("var"), lax.axis_size("space")
    count, rows, pixels = patches.shape
    width = agg_out.shape[0]
    size = width // HEADS
    scale = 1.0 / math.sqrt(size)
    block = rows // n_var
    cols = width // n_space
    group = out_weight.shape[0]
    drows = width // n_var
    positions = rows * n_space
    kv_cols = 2 * width // n_space
    me = jnp.stack([lax.axis_index("var"), lax.axis_index("space")]).astype(jnp.int32)
    gain = norm_gain.reshape(1, width)
    query = agg_query.reshape(1, width)
    vmem = pl.BlockSpec(memory_space=pltpu.VMEM)
    packet = width + LANES

    dattn, cot_own, w_heads, *cot_cols = call(
        functools.partial(early_body, n_space),
        [struct((rows, group), BF16), struct((block, width), BF16), struct(qkv_weight.shape, BF16)]
        + [struct((rows, cols), BF16)] * n_space,
        in_specs=[SMEM] + [vmem] * 3,
        scratch_shapes=[pltpu.VMEM((n_space, rows, cols), BF16)],
        cost_estimate=cost(2e8, 4e6),
        name="early",
    )(me, cotangent, out_weight, qkv_weight)
    dattn_all = gather_direct(dattn, "space")
    cot_all = exchange_direct(cot_cols, "space")

    whole = lambda shape: pl.BlockSpec(shape, lambda v: (0,) * len(shape))
    last = count - 1
    first_pass = lambda shape: pl.BlockSpec((1,) + shape, lambda i: (jnp.minimum(i, last),) + (0,) * len(shape))
    second_pass = lambda shape: pl.BlockSpec((1,) + shape, lambda i: (jnp.maximum(i - count, 0),) + (0,) * len(shape))
    tokens, value, scores, w_back, send = call(
        functools.partial(forward_body, count, scale),
        [
            struct((count, rows, width), BF16),
            struct((count, rows, width), F32),
            struct((count, rows, LANES), F32),
            struct((width, LANES), BF16),
            struct((rows, packet), F32),
        ],
        limit=48,
        grid=(2 * count,),
        in_specs=[
            first_pass((rows, pixels)),
            first_pass((pixels, width)),
            whole((count, width)),
            whole((1, width)),
            pl.BlockSpec((width, width), lambda v: (0, 0)),
            pl.BlockSpec((width, width), lambda v: (0, 1)),
        ],
        after=[dattn],
        out_specs=[
            first_pass((rows, width)),
            second_pass((rows, width)),
            whole((count, rows, LANES)),
            whole((width, LANES)),
            whole((rows, packet)),
        ],
        scratch_shapes=[
            pltpu.VMEM((width, 3 * LANES), BF16),
            pltpu.VMEM((count, rows, width), BF16),
            pltpu.VMEM((rows, LANES), F32),
            pltpu.VMEM((LANES, width), BF16),
            pltpu.VMEM((rows, width), F32),
        ],
        cost_estimate=cost(6e9, 2e7),
        name="forward",
    )(patches, embed_weight, var_embed, query, agg_kv, agg_kv)

    received = exchange_all(send, "var")
    mixed, pooled_copies = call(
        functools.partial(pool_body, n_var),
        [struct((block, width), F32), struct((rows, packet), BF16)],
        after=dattn_all[1:] + cot_all[1:],
        cost_estimate=cost(1e8, 3e6),
        name="pool",
    )(received)
    pooled_packets = exchange_all(pooled_copies, "var")

    qkv, normed, centred, inv = call(
        norm_body,
        [
            struct((rows, 3 * group), BF16),
            struct((rows, width), BF16),
            struct((block, width), F32),
            struct((block, LANES), F32),
        ],
        in_specs=[SMEM] + [vmem] * 4,
        scratch_shapes=[pltpu.VMEM((rows, width), F32), pltpu.VMEM((rows, LANES), F32)],
        cost_estimate=cost(8e8, 5e6),
        name="norm",
    )(me, pooled_packets, agg_out, gain, w_heads)

    qkv_all = gather_direct(qkv, "space")
    attn, dqkv, d_normed, *normed_cols = call(
        functools.partial(attention_body, n_space, size, scale),
        [struct((positions, group), BF16), struct((positions, 3 * group), BF16), struct((rows, width), BF16)]
        + [struct((rows, cols), BF16)] * n_space,
        limit=48,
        in_specs=[SMEM] + [vmem] * (2 * n_space + 2),
        scratch_shapes=[pltpu.VMEM((positions, group), BF16)] * 2
        + [pltpu.VMEM((positions, group), F32)] * 2
        + [pltpu.VMEM((n_space, rows, cols), BF16)],
        cost_estimate=cost(6e9, 4e6),
        name="attention",
    )(me, *qkv_all, *dattn_all, w_heads, normed)

    dn_received = exchange_all(d_normed, "var")
    normed_all = exchange_direct(normed_cols, "space")
    joined_copies, dgain = call(
        functools.partial(joined_body, n_var),
        [struct((rows, packet), BF16), struct((8, width), F32)],
        after=normed_all[1:],
        cost_estimate=cost(2e8, 3e6),
        name="joined",
    )(dn_received, centred, inv, gain, cot_own, mixed, agg_out)
    joined_packets = exchange_all(joined_copies, "var")

    d_pooled, stat, *out_blocks = call(
        functools.partial(out_grad_body, n_space),
        [struct((rows, width), F32), struct((3, rows, LANES), F32)] + [struct((drows + 16, cols), BF16)] * n_space,
        in_specs=[SMEM] + [vmem] * 4,
        scratch_shapes=[pltpu.VMEM((width, width), F32), pltpu.VMEM((n_space, drows + 16, cols), BF16)],
        cost_estimate=cost(1e9, 5e6),
        name="out_grad",
    )(me, pooled_packets, joined_packets, dgain, agg_out)
    out_all = exchange_direct(out_blocks, "space")

    def backward(start, size_here, after):
        each = lambda shape: pl.BlockSpec((1,) + shape, lambda v: (v + start,) + (0,) * len(shape))
        here = lambda shape: pl.BlockSpec((1,) + shape, lambda v: (v,) + (0,) * len(shape))
        blocks = pl.BlockSpec((n_space // 2, 1, pixels + 16, cols), lambda v: (0, v, 0, 0))
        return call(
            functools.partial(backward_body, n_space),
            [struct((size_here, rows, width), BF16), struct((size_here, rows, 2 * LANES), BF16)]
            + [struct((n_space // 2, size_here, pixels + 16, cols), BF16)] * 2,
            limit=40,
            grid=(size_here,),
            in_specs=[
                SMEM,
                whole((rows, width)),
                whole((3, rows, LANES)),
                each((rows, width)),
                each((rows, width)),
                each((rows, LANES)),
                each((rows, pixels)),
                pl.BlockSpec((width, width), lambda v: (0, 1)),
                whole((width, LANES)),
            ],
            after=after,
            out_specs=[here((rows, width)), here((rows, 2 * LANES)), blocks, blocks],
            scratch_shapes=[
                pltpu.VMEM((LANES, width), BF16),
                pltpu.VMEM((width, LANES), BF16),
                pltpu.VMEM((n_space, pixels + 16, cols), BF16),
            ],
            cost_estimate=cost(4e9, 1.5e7),
            name="backward",
        )(me, d_pooled, stat, tokens, value, scores, patches, agg_kv, w_back)

    def scatter_embed(keep, send):
        arrived = swap(send, "space", 1)
        blocks = {
            2 * j: (keep[j].astype(F32) + arrived[j].astype(F32)).astype(BF16) for j in range(1, n_space // 2)
        }
        sums = list(blocks.values())
        mine, bit = [keep, arrived], 2
        while bit < n_space:
            got = {k ^ bit: swap(blocks[k], "space", bit) for k in blocks if k & bit and k % bit == 0}
            mine.append(got[0])
            for k in got:
                if k:
                    blocks[k] = (blocks[k].astype(F32) + got[k].astype(F32)).astype(BF16)
            bit *= 2
        return mine, sums

    middle = count // 2
    dv0, dl0, keep0, send0 = backward(0, middle, [])
    out_part = call(
        functools.partial(out_sum_body, n_space),
        struct((drows + 16, cols), BF16),
        cost_estimate=cost(1e6, 3e5),
        name="out_sum",
    )(*out_all)
    dv1, dl1, keep1, send1 = backward(middle, count - middle, [out_part, dv0])
    mine0, sums0 = scatter_embed(keep0, send0)
    mine1, sums1 = scatter_embed(keep1, send1)
    out_even, out_odd = gather_pairs(out_part, "var")

    n_chip = n_var // 2
    step = max(drows, 256)
    half_whole = lambda arr: whole(arr.shape)
    kv_keep, kv_send = call(
        functools.partial(value_grad_body, n_var),
        [struct((n_chip, drows, packet), BF16)] * 2,
        limit=48,
        grid=(width // step,),
        in_specs=[SMEM, pl.BlockSpec((count, rows, step), lambda i: (0, 0, i))]
        + [half_whole(x) for x in (dv0, dv1, dl0, dl1)],
        out_specs=[whole((n_chip, drows, packet))] * 2,
        scratch_shapes=[pltpu.VMEM((step, packet), BF16)],
        cost_estimate=cost(4e9, 1e7),
        name="value_grad",
    )(me, tokens, dv0, dv1, dl0, dl1)
    kv_got = swap(kv_send, "var", 1)
    kv_blocks = call(
        functools.partial(pair_sum_body, n_chip),
        [struct((drows, packet), BF16)] * n_chip,
        after=[out_even],
        in_specs=[SMEM] + [vmem] * 2,
        cost_estimate=cost(1e6, 1e6),
        name="pair_sum",
    )(me, kv_keep, kv_got)
    kv_parts = [kv_blocks[0]] + [swap(kv_blocks[k], "var", 2 * k) for k in range(1, n_chip)]
    small, *large = call(
        functools.partial(packet_split_body, n_chip, n_space),
        [struct((drows, LANES), BF16)] + [struct((drows, kv_cols), BF16)] * n_space,
        after=sums0,
        in_specs=[SMEM] + [vmem] * n_chip,
        scratch_shapes=[pltpu.VMEM((n_space // 2, drows, kv_cols), BF16)],
        cost_estimate=cost(1e6, 1e6),
        name="packet_split",
    )(me, *kv_parts)
    small_all = gather_direct(small, "space")
    large_all = [large[0]] + [
        swap(large[k], "space", k, lambda target: target >= n_space // 2) for k in range(1, n_space)
    ]
    kv_sum = call(
        functools.partial(space_sum_body, n_space),
        struct((drows, kv_cols + LANES), BF16),
        after=sums1,
        cost_estimate=cost(1e6, 1e6),
        name="space_sum",
    )(*small_all, *large_all)

    grad_agg_out, grad_gain = call(
        functools.partial(out_final_body, n_var),
        [struct((width, cols), F32), struct((1, cols), F32)],
        in_specs=[SMEM] + [vmem] * 2,
        cost_estimate=cost(1e6, 1e6),
        name="out_final",
    )(me, out_even, out_odd)

    grad_qkv, grad_out = call(
        functools.partial(head_grads_body, n_space),
        [struct((cols, 3 * group), F32), struct((group, cols), F32)],
        cost_estimate=cost(1e9, 3e6),
        name="head_grads",
    )(*normed_all, *cot_all, dqkv, attn)

    kv_even, kv_odd = gather_pairs(kv_sum, "var")
    grad_agg_kv, grad_query = call(
        functools.partial(final_body, n_var, n_space, scale),
        [struct((width, kv_cols), F32), struct((1, cols), F32)],
        grid=(1,),
        in_specs=[SMEM] + [vmem] * 3 + [pl.BlockSpec((width, width), lambda i: (0, 0))],
        cost_estimate=cost(2e8, 5e6),
        name="final",
    )(me, kv_even, kv_odd, query, agg_kv)

    def first_block(x):
        if x.ndim == 4:
            return pl.BlockSpec((1,) + x.shape[1:], lambda i: (0, 0, 0, 0))
        return pl.BlockSpec(x.shape, lambda i: (0, 0, 0))

    grad_embed, grad_var_embed = call(
        functools.partial(embed_final_body, len(mine0)),
        [struct((count, pixels, cols), F32), struct((count, cols), F32)],
        grid=(1,),
        in_specs=[first_block(x) for x in mine0 + mine1],
        cost_estimate=cost(1e6, 1e6),
        name="embed_final",
    )(*mine0, *mine1)

    return (
        grad_embed,
        grad_var_embed,
        grad_query.reshape(cols),
        grad_agg_kv,
        grad_agg_out,
        grad_gain.reshape(cols),
        grad_qkv,
        grad_out,
    )


def solution(mesh):
    return jax.shard_map(
        shards,
        mesh=mesh,
        in_specs=(
            P("var", "space", None),
            P("var", None, None),
            P("var", None),
            P(),
            P(),
            P(),
            P(),
            P(None, "var"),
            P("var", None),
            P("space", None),
        ),
        out_specs=(
            P("var", None, "space"),
            P("var", "space"),
            P("space"),
            P(None, "space"),
            P(None, "space"),
            P("space"),
            P("space", "var"),
            P("var", "space"),
        ),
        check_vma=False,
    )
```

time: 263 us -> 296 us (1.13)
  blocking collectives: 0 us -> 28.3 us
  local copies, waits for them, and re-layouts: 4.1 us -> 31.4 us
  starting transfers between devices: 88 us -> 63.4 us
  Pallas kernels: 62.8 us -> 70.3 us
  waiting for transfers between devices: 104 us -> 100 us
    ppermute x80 -> x37, starting transfers between devices: 88 us -> 53.6 us  [swap(): return lax.ppermute(x, axis, pairs)]
    unnamed x20 -> x136, local copies, waits for them, and re-layouts: 1.17 us -> 31.4 us
    all_to_all x0 -> x2, blocking collectives: none -> 28.3 us  [exchange_all(): return lax.all_to_all(x, axis, split_axis=0, concat_axis=0, tiled=True)]
    all_to_all x0 -> x2, starting transfers between devices: none -> 9.8 us  [exchange_all(): return lax.all_to_all(x, axis, split_axis=0, concat_axis=0, tiled=True)]
    pallas_call x16 -> x18, Pallas kernels: 62.8 us -> 70.3 us  [run(): pl.pallas_call(lambda *refs: body(*refs[:n], *refs[n + m:]), out_shape=ou...]
    ppermute x80 -> x37, waiting for transfers between devices: 104 us -> 100 us  [swap(): return lax.ppermute(x, axis, pairs)]
  transfers between devices with their start and end apart: 80 -> 39, of which waited for: 36 -> 16; matrix products, arithmetic and copies ran while one was open for 0% -> 0% of each run, Pallas kernels for 12% -> 5%
where the time goes in v2:
time: 296 us; the launch traced here: 295 us
  waiting for transfers between devices  100 us (34%)
  Pallas kernels  70.3 us (24%)
  starting transfers between devices  63.4 us (21%)
  local copies, waits for them, and re-layouts  31.4 us (11%)
  blocking collectives  28.3 us (10%)
    ppermute x37, waiting for transfers between devices, swap(): return lax.ppermute(x, axis, pairs)  100 us
    pallas_call x18, Pallas kernels, run(): pl.pallas_call(lambda *refs: body(*refs[:n], *refs[n + m:]), out_shape=ou...  70.3 us
    ppermute x37, starting transfers between devices, swap(): return lax.ppermute(x, axis, pairs)  53.6 us
    unnamed x136, local copies, waits for them, and re-layouts  31.4 us
    all_to_all x2, blocking collectives, exchange_all(): return lax.all_to_all(x, axis, split_axis=0, concat_axis=0, tiled=True)  28.3 us
    all_to_all x2, starting transfers between devices, exchange_all(): return lax.all_to_all(x, axis, split_axis=0, concat_axis=0, tiled=True)  9.8 us
  transfers between devices with their start and end apart: 39, of which 16 were waited for; matrix products, arithmetic and copies ran while one was open for 0% of the time, Pallas kernels for 5%

profile of v2, /device:TPU:0, one launch (start us, length us, event | category | flops | bytes accessed | tf_op | source)
XLA Modules:
  0.0 295.2 jit_solution(992854517933766852)
XLA Ops:
  9.4 17.1 %forward.1 = (bf16[6,256,1024]{2,1,0:T(8,128)(2,1)}, f32[6,256,1024]{2,1,0:T(8,128)}, f32[6,256,128]{2,1,0:T(8,128)S(1)}, bf16[1024,128]{1,0:T(8,128)(2,1)S(1)}, f32[256,1152]{1,0:T(8,128)}) custom-call(bf16[6,256,256]{2,1,0:T(8,128)(2,1)S(1)} %copy-done.4, bf16[6,256,1024]{2,1,0:T(8,128)(2,1)} %refs_1_.3, f32[6,1024]{1,0:T(8,128)S(1)} %copy-done.61, ...), custom_call_target="tpu_custom_call" | custom-call | flops 6000000000 | bytes 20000000 | tf_op jit(solution)/shard_map/forward/pallas_call | solution.py:78
  28.1 5.3 %all-to-all-start = ((f32[8,32,1152]{2,1,0:T(8,128)}), f32[8,32,1152]{2,1,0:T(8,128)S(1)}, u32[]{:S(2)}, u32[]{:S(2)}) async-start(f32[8,32,1152]{2,1,0:T(8,128)} %bitcast.3), calls=%async_computation | async-start | bytes 2359296 | tf_op jit(solution)/shard_map/all_to_all | solution.py:121
  33.4 3.7 %collective-permute-start.2 = (bf16[256,128]{1,0:T(8,128)(2,1)}, bf16[256,128]{1,0:T(8,128)(2,1)S(1)}, u32[]{:S(2)}, u32[]{:S(2)}) collective-permute-start(bf16[256,128]{1,0:T(8,128)(2,1)} %get-tuple-element.68.refs_6_.refs_5_), channel_id=1, source_target_pairs={{0,3},{1,2},{2,1},{3,0},{4,7},{5,6},{6,5},{7,4},{8,11},{9,10},{10,... | collective-permute-start | bytes 196616 | tf_op jit(solution)/shard_map/ppermute | solution.py:104
  37.8 3.6 %collective-permute-start.5 = (bf16[256,256]{1,0:T(8,128)(2,1)}, bf16[256,256]{1,0:T(8,128)(2,1)S(1)}, u32[]{:S(2)}, u32[]{:S(2)}) collective-permute-start(bf16[256,256]{1,0:T(8,128)(2,1)} %copy-done.56), channel_id=1, source_target_pairs={{0,3},{1,2},{2,1},{3,0},{4,7},{5,6},{6,5},{7,4},{8,11},{9,10},{10,... | collective-permute-start | bytes 393224 | tf_op jit(solution)/shard_map/ppermute | solution.py:104
  42.9 12.2 %collective-permute-done.1.refs_2_.refs_7_ = bf16[256,128]{1,0:T(8,128)(2,1)S(1)} collective-permute-done((bf16[256,128]{1,0:T(8,128)(2,1)}, bf16[256,128]{1,0:T(8,128)(2,1)S(1)}, u32[]{:S(2)}, u32[]{:S(2)}) %collective-permute-start.1) | collective-permute-done | bytes 65568 | tf_op jit(solution)/shard_map/ppermute | solution.py:104
  61.1 14.0 %all_to_all.44 = bf16[8,32,1152]{2,1,0:T(8,128)(2,1)S(1)} all-to-all(bf16[8,32,1152]{2,1,0:T(8,128)(2,1)S(1)} %bitcast.33), channel_id=1, replica_groups=mesh['var'=8,'space'=4] {'var'}, dimensions={0} | all-to-all | bytes 1179648 | tf_op jit(solution)/shard_map/all_to_all | solution.py:121
  78.4 2.6 collective-permute-start.8
  82.8 5.3 %collective-permute-done.8.refs_4_ = bf16[256,384]{1,0:T(8,128)(2,1)S(1)} collective-permute-done((bf16[256,384]{1,0:T(8,128)(2,1)S(1)}, bf16[256,384]{1,0:T(8,128)(2,1)S(1)}, u32[]{:S(2)}, u32[]{:S(2)}) %collective-permute-start.8) | collective-permute-done | bytes 196640 | tf_op jit(solution)/shard_map/ppermute | solution.py:104
  88.1 8.8 %collective-permute-done.7.refs_3_ = bf16[256,384]{1,0:T(8,128)(2,1)S(1)} collective-permute-done((bf16[256,384]{1,0:T(8,128)(2,1)S(1)}, bf16[256,384]{1,0:T(8,128)(2,1)S(1)}, u32[]{:S(2)}, u32[]{:S(2)}) %collective-permute-start.7) | collective-permute-done | bytes 196640 | tf_op jit(solution)/shard_map/ppermute | solution.py:104
  96.9 12.5 %attention.1 = (bf16[1024,128]{1,0:T(8,128)(2,1)S(1)}, bf16[1024,384]{1,0:T(8,128)(2,1)S(1)}, bf16[256,1024]{1,0:T(8,128)(2,1)S(1)}, bf16[256,256]{1,0:T(8,128)(...) custom-call(s32[2]{0:T(128)S(1)} %pad_add_fusion.refs_0_, ...), custom_call_target="tpu_custom_call" | custom-call | flops 6000000000 | bytes 4000000 | tf_op jit(solution)/shard_map/attention/pallas_call | solution.py:78
  114.4 4.5 %all-to-all-start.2 = ((bf16[8,32,1024]{2,1,0:T(8,128)(2,1)}), bf16[8,32,1024]{2,1,0:T(8,128)(2,1)}, u32[]{:S(2)}, u32[]{:S(2)}) async-start(bf16[8,32,1024]{2,1,0:T(8,128)(2,1)} %bitcast.34), calls=%async_computation.2 | async-start | bytes 1048576 | tf_op jit(solution)/shard_map/all_to_all | solution.py:121
  120.8 2.5 collective-permute-start.11
  123.3 2.8 collective-permute-done.9.refs_7_.refs_1_
  126.8 5.3 %collective-permute-done.10.refs_8_.refs_2_ = bf16[256,256]{1,0:T(8,128)(2,1)S(1)} collective-permute-done((bf16[256,256]{1,0:T(8,128)(2,1)}, bf16[256,256]{1,0:T(8,128)(2,1)S(1)}, u32[]{:S(2)}, u32[]{:S(2)}) %collective-permute-start.10) | collective-permute-done | bytes 131104 | tf_op jit(solution)/shard_map/ppermute | solution.py:104
  138.7 2.2 joined.1
  141.0 14.2 %all_to_all.45 = bf16[8,32,1152]{2,1,0:T(8,128)(2,1)S(1)} all-to-all(bf16[8,32,1152]{2,1,0:T(8,128)(2,1)S(1)} %bitcast.32), channel_id=1, replica_groups=mesh['var'=8,'space'=4] {'var'}, dimensions={0} | all-to-all | bytes 1179648 | tf_op jit(solution)/shard_map/all_to_all | solution.py:121
  159.2 2.4 collective-permute-start.16
  162.6 7.2 %backward.2 = (bf16[3,256,1024]{2,1,0:T(8,128)(2,1)S(1)}, bf16[3,256,256]{2,1,0:T(8,128)(2,1)S(1)}, bf16[2,3,272,256]{3,2,1,0:T(8,128)(2,1)S(1)}, bf16[2,3,272,256]{3,2,1,0:T(8,128)(2,1)S(1)}) custom-call(s32[2]{0:T(128)S(1)} %pad_add_fusion.refs_0_, f32[256,1024]{1,0:T(8,128)S(1)} %get-tuple-element.87.refs_1_, ...), custom_call_target="tpu_custom_call" | custom-call | flops 4000000000 | bytes 15000000 | tf_op jit(solution)/shard_map/backward/pallas_call | solution.py:78
  169.9 8.4 %backward.3 = (bf16[3,256,1024]{2,1,0:T(8,128)(2,1)S(1)}, bf16[3,256,256]{2,1,0:T(8,128)(2,1)S(1)}, bf16[2,3,272,256]{3,2,1,0:T(8,128)(2,1)S(1)}, bf16[2,3,272,256]{3,2,1,0:T(8,128)(2,1)S(1)}) custom-call(s32[2]{0:T(128)S(1)} %pad_add_fusion.refs_0_, f32[256,1024]{1,0:T(8,128)S(1)} %get-tuple-element.87.refs_1_, ...), custom_call_target="tpu_custom_call" | custom-call | flops 4000000000 | bytes 15000000 | tf_op jit(solution)/shard_map/backward/pallas_call | solution.py:78
  180.8 7.0 %value_grad.1 = (bf16[4,128,1152]{2,1,0:T(8,128)(2,1)S(1)}, bf16[4,128,1152]{2,1,0:T(8,128)(2,1)S(1)}) custom-call(s32[2]{0:T(128)S(1)} %pad_add_fusion.refs_0_, bf16[6,256,1024]{2,1,0:T(8,128)(2,1)} %get-tuple-element.89.refs_3_.refs_1_, bf16[3,256,1024]{2,1,0:T(8,128)(2,1)S(1)} %copy-done.9, bf16[3,256,1024]{2,1,0:T(8,128)(2,1)} %copy-done.53, ...), custom_call_target="tpu_custom_call" | custom-call | flops 4000000000 | bytes 10000000 | tf_op jit(solution)/shard_map/value_grad/pallas_call | solution.py:78
  192.0 3.3 %collective-permute-done.22 = bf16[144,256]{1,0:T(8,128)(2,1)S(1)} collective-permute-done((bf16[144,256]{1,0:T(8,128)(2,1)S(1)}, bf16[144,256]{1,0:T(8,128)(2,1)S(1)}, u32[]{:S(2)}, u32[]{:S(2)}) %collective-permute-start.22) | collective-permute-done | bytes 73760 | tf_op jit(solution)/shard_map/ppermute | solution.py:104
  195.9 3.7 %collective-permute-done.20 = bf16[144,256]{1,0:T(8,128)(2,1)S(1)} collective-permute-done((bf16[144,256]{1,0:T(8,128)(2,1)S(1)}, bf16[144,256]{1,0:T(8,128)(2,1)S(1)}, u32[]{:S(2)}, u32[]{:S(2)}) %collective-permute-start.20) | collective-permute-done | bytes 73760 | tf_op jit(solution)/shard_map/ppermute | solution.py:104
  202.0 2.4 collective-permute-start.25
  204.4 5.0 %collective-permute-done.12.refs_1_ = bf16[2,3,272,256]{3,2,1,0:T(8,128)(2,1)S(1)} collective-permute-done((bf16[2,3,272,256]{3,2,1,0:T(8,128)(2,1)S(1)}, bf16[2,3,272,256]{3,2,1,0:T(8,128)(2,1)S(1)}, u32[]{:S(2)}, u32[]{:S(2)}) %collective-permute-start.12) | collective-permute-done | bytes 835616 | tf_op jit(solution)/shard_map/ppermute | solution.py:104
  210.8 3.4 %collective-permute-done.24.refs_3_ = bf16[128,1152]{1,0:T(8,128)(2,1)S(1)} collective-permute-done((bf16[128,1152]{1,0:T(8,128)(2,1)S(1)}, bf16[128,1152]{1,0:T(8,128)(2,1)S(1)}, u32[]{:S(2)}, u32[]{:S(2)}) %collective-permute-start.24) | collective-permute-done | bytes 294944 | tf_op jit(solution)/shard_map/ppermute | solution.py:104
  220.3 8.3 %collective-permute-done.17.refs_4_ = bf16[2,3,272,256]{3,2,1,0:T(8,128)(2,1)S(1)} collective-permute-done((bf16[2,3,272,256]{3,2,1,0:T(8,128)(2,1)S(1)}, bf16[2,3,272,256]{3,2,1,0:T(8,128)(2,1)S(1)}, u32[]{:S(2)}, u32[]{:S(2)}) %collective-permute-start.17) | collective-permute-done | bytes 835616 | tf_op jit(solution)/shard_map/ppermute | solution.py:104
  230.2 2.9 collective-permute-start.31
  239.2 4.1 %collective-permute-done.34 = bf16[128,640]{1,0:T(8,128)(2,1)S(1)} collective-permute-done((bf16[128,640]{1,0:T(8,128)(2,1)S(1)}, bf16[128,640]{1,0:T(8,128)(2,1)S(1)}, u32[]{:S(2)}, u32[]{:S(2)}) %collective-permute-start.34) | collective-permute-done | bytes 163872 | tf_op jit(solution)/shard_map/ppermute | solution.py:104
  244.5 9.7 %collective-permute-start.13 = (bf16[3,272,256]{2,1,0:T(8,128)(2,1)S(1)}, bf16[3,272,256]{2,1,0:T(8,128)(2,1)S(1)}, u32[]{:S(2)}, u32[]{:S(2)}) collective-permute-start(bf16[3,272,256]{2,1,0:T(8,128)(2,1)S(1)} %fusion.refs_5_), channel_id=1, source_target_pairs={{0,2},{1,3},{2,0},{3,1},{4,6},{5,7},{6,4},{7,5},{8,10},{9,11},{10,... | collective-permute-start | bytes 1253384 | tf_op jit(solution)/shard_map/ppermute | solution.py:104
  258.0 24.6 %collective-permute-done.13.refs_2_ = bf16[3,272,256]{2,1,0:T(8,128)(2,1)S(1)} collective-permute-done((bf16[3,272,256]{2,1,0:T(8,128)(2,1)S(1)}, bf16[3,272,256]{2,1,0:T(8,128)(2,1)S(1)}, u32[]{:S(2)}, u32[]{:S(2)}) %collective-permute-start.13) | collective-permute-done | bytes 417824 | tf_op jit(solution)/shard_map/ppermute | solution.py:104
  282.6 8.7 %collective-permute-done.18.refs_5_ = bf16[3,272,256]{2,1,0:T(8,128)(2,1)S(1)} collective-permute-done((bf16[3,272,256]{2,1,0:T(8,128)(2,1)S(1)}, bf16[3,272,256]{2,1,0:T(8,128)(2,1)S(1)}, u32[]{:S(2)}, u32[]{:S(2)}) %collective-permute-start.18) | collective-permute-done | bytes 417824 | tf_op jit(solution)/shard_map/ppermute | solution.py:104
  292.8 2.4 final.1
  (207 shorter events, 73.7 us)
Async XLA Ops:
  28.1 29.0 %all-to-all-start = ((f32[8,32,1152]{2,1,0:T(8,128)}), f32[8,32,1152]{2,1,0:T(8,128)S(1)}, u32[]{:S(2)}, u32[]{:S(2)}) async-start(f32[8,32,1152]{2,1,0:T(8,128)} %bitcast.3), calls=%async_computation | async-start | bytes 2359296 | tf_op jit(solution)/shard_map/all_to_all | solution.py:121
  33.4 8.1 %collective-permute-start.2 = (bf16[256,128]{1,0:T(8,128)(2,1)}, bf16[256,128]{1,0:T(8,128)(2,1)S(1)}, u32[]{:S(2)}, u32[]{:S(2)}) collective-permute-start(bf16[256,128]{1,0:T(8,128)(2,1)} %get-tuple-element.68.refs_6_.refs_5_), channel_id=1, source_target_pairs={{0,3},{1,2},{2,1},{3,0},{4,7},{5,6},{6,5},{7,4},{8,11},{9,10},{10,... | collective-permute-start | bytes 196616 | tf_op jit(solution)/shard_map/ppermute | solution.py:104
  37.1 19.3 %collective-permute-start.3 = (bf16[256,256]{1,0:T(8,128)(2,1)}, bf16[256,256]{1,0:T(8,128)(2,1)S(1)}, u32[]{:S(2)}, u32[]{:S(2)}) collective-permute-start(bf16[256,256]{1,0:T(8,128)(2,1)} %get-tuple-element.70), channel_id=1, source_target_pairs={{0,1},{1,0},{2,3},{3,2},{4,5},{5,4},{6,7},{7,6},{8,9},{9,8},{10,11... | collective-permute-start | bytes 393224 | tf_op jit(solution)/shard_map/ppermute | solution.py:104
  37.1 19.3 %collective-permute-start.4 = (bf16[256,256]{1,0:T(8,128)(2,1)}, bf16[256,256]{1,0:T(8,128)(2,1)S(1)}, u32[]{:S(2)}, u32[]{:S(2)}) collective-permute-start(bf16[256,256]{1,0:T(8,128)(2,1)} %copy-done.57), channel_id=1, source_target_pairs={{0,2},{1,3},{2,0},{3,1},{4,6},{5,7},{6,4},{7,5},{8,10},{9,11},{10,... | collective-permute-start | bytes 393224 | tf_op jit(solution)/shard_map/ppermute | solution.py:104
  37.8 18.5 %collective-permute-start.5 = (bf16[256,256]{1,0:T(8,128)(2,1)}, bf16[256,256]{1,0:T(8,128)(2,1)S(1)}, u32[]{:S(2)}, u32[]{:S(2)}) collective-permute-start(bf16[256,256]{1,0:T(8,128)(2,1)} %copy-done.56), channel_id=1, source_target_pairs={{0,3},{1,2},{2,1},{3,0},{4,7},{5,6},{6,5},{7,4},{8,11},{9,10},{10,... | collective-permute-start | bytes 393224 | tf_op jit(solution)/shard_map/ppermute | solution.py:104
  41.4 13.6 %collective-permute-start.1 = (bf16[256,128]{1,0:T(8,128)(2,1)}, bf16[256,128]{1,0:T(8,128)(2,1)S(1)}, u32[]{:S(2)}, u32[]{:S(2)}) collective-permute-start(bf16[256,128]{1,0:T(8,128)(2,1)} %get-tuple-element.68.refs_6_.refs_5_), channel_id=1, source_target_pairs={{0,2},{1,3},{2,0},{3,1},{4,6},{5,7},{6,4},{7,5},{8,10},{9,11},{10,... | collective-permute-start | bytes 196616 | tf_op jit(solution)/shard_map/ppermute | solution.py:104
  42.1 13.6 %collective-permute-start = (bf16[256,128]{1,0:T(8,128)(2,1)}, bf16[256,128]{1,0:T(8,128)(2,1)S(1)}, u32[]{:S(2)}, u32[]{:S(2)}) collective-permute-start(bf16[256,128]{1,0:T(8,128)(2,1)} %get-tuple-element.68.refs_6_.refs_5_), channel_id=1, source_target_pairs={{0,1},{1,0},{2,3},{3,2},{4,5},{5,4},{6,7},{7,6},{8,9},{9,8},{10,11... | collective-permute-start | bytes 196616 | tf_op jit(solution)/shard_map/ppermute | solution.py:104
  78.4 9.7 %collective-permute-start.8 = (bf16[256,384]{1,0:T(8,128)(2,1)S(1)}, bf16[256,384]{1,0:T(8,128)(2,1)S(1)}, u32[]{:S(2)}, u32[]{:S(2)}) collective-permute-start(bf16[256,384]{1,0:T(8,128)(2,1)S(1)} %get-tuple-element.75.refs_1_), channel_id=1, source_target_pairs={{0,3},{1,2},{2,1},{3,0},{4,7},{5,6},{6,5},{7,4},{8,11},{9,10},{10,... | collective-permute-start | bytes 589832 | tf_op jit(solution)/shard_map/ppermute | solution.py:104
  81.0 15.9 %collective-permute-start.7 = (bf16[256,384]{1,0:T(8,128)(2,1)S(1)}, bf16[256,384]{1,0:T(8,128)(2,1)S(1)}, u32[]{:S(2)}, u32[]{:S(2)}) collective-permute-start(bf16[256,384]{1,0:T(8,128)(2,1)S(1)} %get-tuple-element.75.refs_1_), channel_id=1, source_target_pairs={{0,2},{1,3},{2,0},{3,1},{4,6},{5,7},{6,4},{7,5},{8,10},{9,11},{10,... | collective-permute-start | bytes 589832 | tf_op jit(solution)/shard_map/ppermute | solution.py:104
  81.0 15.9 %collective-permute-start.6 = (bf16[256,384]{1,0:T(8,128)(2,1)S(1)}, bf16[256,384]{1,0:T(8,128)(2,1)S(1)}, u32[]{:S(2)}, u32[]{:S(2)}) collective-permute-start(bf16[256,384]{1,0:T(8,128)(2,1)S(1)} %get-tuple-element.75.refs_1_), channel_id=1, source_target_pairs={{0,1},{1,0},{2,3},{3,2},{4,5},{5,4},{6,7},{7,6},{8,9},{9,8},{10,11... | collective-permute-start | bytes 589832 | tf_op jit(solution)/shard_map/ppermute | solution.py:104
  114.4 19.1 %all-to-all-start.2 = ((bf16[8,32,1024]{2,1,0:T(8,128)(2,1)}), bf16[8,32,1024]{2,1,0:T(8,128)(2,1)}, u32[]{:S(2)}, u32[]{:S(2)}) async-start(bf16[8,32,1024]{2,1,0:T(8,128)(2,1)} %bitcast.34), calls=%async_computation.2 | async-start | bytes 1048576 | tf_op jit(solution)/shard_map/all_to_all | solution.py:121
  118.9 7.3 %collective-permute-start.9 = (bf16[256,256]{1,0:T(8,128)(2,1)}, bf16[256,256]{1,0:T(8,128)(2,1)S(1)}, u32[]{:S(2)}, u32[]{:S(2)}) collective-permute-start(bf16[256,256]{1,0:T(8,128)(2,1)} %copy-done.60), channel_id=1, source_target_pairs={{0,1},{1,0},{2,3},{3,2},{4,5},{5,4},{6,7},{7,6},{8,9},{9,8},{10,11... | collective-permute-start | bytes 393224 | tf_op jit(solution)/shard_map/ppermute | solution.py:104
  119.0 13.2 %collective-permute-start.10 = (bf16[256,256]{1,0:T(8,128)(2,1)}, bf16[256,256]{1,0:T(8,128)(2,1)S(1)}, u32[]{:S(2)}, u32[]{:S(2)}) collective-permute-start(bf16[256,256]{1,0:T(8,128)(2,1)} %copy-done.59), channel_id=1, source_target_pairs={{0,2},{1,3},{2,0},{3,1},{4,6},{5,7},{6,4},{7,5},{8,10},{9,11},{10,... | collective-permute-start | bytes 393224 | tf_op jit(solution)/shard_map/ppermute | solution.py:104
  120.8 12.0 %collective-permute-start.11 = (bf16[256,256]{1,0:T(8,128)(2,1)}, bf16[256,256]{1,0:T(8,128)(2,1)S(1)}, u32[]{:S(2)}, u32[]{:S(2)}) collective-permute-start(bf16[256,256]{1,0:T(8,128)(2,1)} %copy-done.58), channel_id=1, source_target_pairs={{0,3},{1,2},{2,1},{3,0},{4,7},{5,6},{6,5},{7,4},{8,11},{9,10},{10,... | collective-permute-start | bytes 393224 | tf_op jit(solution)/shard_map/ppermute | solution.py:104
  157.1 12.6 %collective-permute-start.14 = (bf16[144,256]{1,0:T(8,128)(2,1)S(1)}, bf16[144,256]{1,0:T(8,128)(2,1)S(1)}, u32[]{:S(2)}, u32[]{:S(2)}) collective-permute-start(bf16[144,256]{1,0:T(8,128)(2,1)S(1)} %get-tuple-element.96), channel_id=1, source_target_pairs={{0,1},{1,0},{2,3},{3,2},{4,5},{5,4},{6,7},{7,6},{8,9},{9,8},{10,11... | collective-permute-start | bytes 221192 | tf_op jit(solution)/shard_map/ppermute | solution.py:104
  159.1 10.7 %collective-permute-start.15 = (bf16[144,256]{1,0:T(8,128)(2,1)S(1)}, bf16[144,256]{1,0:T(8,128)(2,1)S(1)}, u32[]{:S(2)}, u32[]{:S(2)}) collective-permute-start(bf16[144,256]{1,0:T(8,128)(2,1)S(1)} %get-tuple-element.97), channel_id=1, source_target_pairs={{0,2},{1,3},{2,0},{3,1},{4,6},{5,7},{6,4},{7,5},{8,10},{9,11},{10,... | collective-permute-start | bytes 221192 | tf_op jit(solution)/shard_map/ppermute | solution.py:104
  159.2 10.6 %collective-permute-start.16 = (bf16[144,256]{1,0:T(8,128)(2,1)S(1)}, bf16[144,256]{1,0:T(8,128)(2,1)S(1)}, u32[]{:S(2)}, u32[]{:S(2)}) collective-permute-start(bf16[144,256]{1,0:T(8,128)(2,1)S(1)} %get-tuple-element.98), channel_id=1, source_target_pairs={{0,3},{1,2},{2,1},{3,0},{4,7},{5,6},{6,5},{7,4},{8,11},{9,10},{10,... | collective-permute-start | bytes 221192 | tf_op jit(solution)/shard_map/ppermute | solution.py:104
  187.8 11.9 %collective-permute-start.19 = (bf16[4,128,1152]{2,1,0:T(8,128)(2,1)S(1)}, bf16[4,128,1152]{2,1,0:T(8,128)(2,1)S(1)}, u32[]{:S(2)}, u32[]{:S(2)}) collective-permute-start(bf16[4,128,1152]{2,1,0:T(8,128)(2,1)S(1)} %get-tuple-element.108), channel_id=1, source_target_pairs={{0,4},{4,0},{8,12},{12,8},{16,20},{20,16},{24,28},{28,24},{1,5},{5... | collective-permute-start | bytes 3538952 | tf_op jit(solution)/shard_map/ppermute | solution.py:104
  187.9 21.5 %collective-permute-start.12 = (bf16[2,3,272,256]{3,2,1,0:T(8,128)(2,1)S(1)}, bf16[2,3,272,256]{3,2,1,0:T(8,128)(2,1)S(1)}, u32[]{:S(2)}, u32[]{:S(2)}) collective-permute-start(bf16[2,3,272,256]{3,2,1,0:T(8,128)(2,1)S(1)} %get-tuple-element.94), channel_id=1, source_target_pairs={{0,1},{1,0},{2,3},{3,2},{4,5},{5,4},{6,7},{7,6},{8,9},{9,8},{10,11... | collective-permute-start | bytes 2506760 | tf_op jit(solution)/shard_map/ppermute | solution.py:104
  189.0 39.6 %collective-permute-start.17 = (bf16[2,3,272,256]{3,2,1,0:T(8,128)(2,1)S(1)}, bf16[2,3,272,256]{3,2,1,0:T(8,128)(2,1)S(1)}, u32[]{:S(2)}, u32[]{:S(2)}) collective-permute-start(bf16[2,3,272,256]{3,2,1,0:T(8,128)(2,1)S(1)} %get-tuple-element.101), channel_id=1, source_target_pairs={{0,1},{1,0},{2,3},{3,2},{4,5},{5,4},{6,7},{7,6},{8,9},{9,8},{10,11... | collective-permute-start | bytes 2506760 | tf_op jit(solution)/shard_map/ppermute | solution.py:104
  200.8 10.0 %collective-permute-start.23 = (bf16[128,1152]{1,0:T(8,128)(2,1)S(1)}, bf16[128,1152]{1,0:T(8,128)(2,1)S(1)}, u32[]{:S(2)}, u32[]{:S(2)}) collective-permute-start(bf16[128,1152]{1,0:T(8,128)(2,1)S(1)} %get-tuple-element.110), channel_id=1, source_target_pairs={{0,8},{4,12},{8,0},{12,4},{16,24},{20,28},{24,16},{28,20},{1,9},{5... | collective-permute-start | bytes 884744 | tf_op jit(solution)/shard_map/ppermute | solution.py:104
  201.4 12.8 %collective-permute-start.24 = (bf16[128,1152]{1,0:T(8,128)(2,1)S(1)}, bf16[128,1152]{1,0:T(8,128)(2,1)S(1)}, u32[]{:S(2)}, u32[]{:S(2)}) collective-permute-start(bf16[128,1152]{1,0:T(8,128)(2,1)S(1)} %get-tuple-element.111), channel_id=1, source_target_pairs={{0,16},{4,20},{8,24},{12,28},{16,0},{20,4},{24,8},{28,12},{1,17},{... | collective-permute-start | bytes 884744 | tf_op jit(solution)/shard_map/ppermute | solution.py:104
  202.0 12.3 %collective-permute-start.25 = (bf16[128,1152]{1,0:T(8,128)(2,1)S(1)}, bf16[128,1152]{1,0:T(8,128)(2,1)S(1)}, u32[]{:S(2)}, u32[]{:S(2)}) collective-permute-start(bf16[128,1152]{1,0:T(8,128)(2,1)S(1)} %get-tuple-element.112), channel_id=1, source_target_pairs={{0,24},{4,28},{8,16},{12,20},{16,8},{20,12},{24,0},{28,4},{1,25},{... | collective-permute-start | bytes 884744 | tf_op jit(solution)/shard_map/ppermute | solution.py:104
  215.1 15.1 %collective-permute-start.28 = (bf16[128,128]{1,0:T(8,128)(2,1)S(1)}, bf16[128,128]{1,0:T(8,128)(2,1)S(1)}, u32[]{:S(2)}, u32[]{:S(2)}) collective-permute-start(bf16[128,128]{1,0:T(8,128)(2,1)S(1)} %get-tuple-element.113.refs_0_), channel_id=1, source_target_pairs={{0,3},{1,2},{2,1},{3,0},{4,7},{5,6},{6,5},{7,4},{8,11},{9,10},{10,... | collective-permute-start | bytes 98312 | tf_op jit(solution)/shard_map/ppermute | solution.py:104
  216.7 16.7 %collective-permute-start.27 = (bf16[128,128]{1,0:T(8,128)(2,1)S(1)}, bf16[128,128]{1,0:T(8,128)(2,1)S(1)}, u32[]{:S(2)}, u32[]{:S(2)}) collective-permute-start(bf16[128,128]{1,0:T(8,128)(2,1)S(1)} %get-tuple-element.113.refs_0_), channel_id=1, source_target_pairs={{0,2},{1,3},{2,0},{3,1},{4,6},{5,7},{6,4},{7,5},{8,10},{9,11},{10,... | collective-permute-start | bytes 98312 | tf_op jit(solution)/shard_map/ppermute | solution.py:104
  217.7 15.7 %collective-permute-start.26 = (bf16[128,128]{1,0:T(8,128)(2,1)S(1)}, bf16[128,128]{1,0:T(8,128)(2,1)S(1)}, u32[]{:S(2)}, u32[]{:S(2)}) collective-permute-start(bf16[128,128]{1,0:T(8,128)(2,1)S(1)} %get-tuple-element.113.refs_0_), channel_id=1, source_target_pairs={{0,1},{1,0},{2,3},{3,2},{4,5},{5,4},{6,7},{7,6},{8,9},{9,8},{10,11... | collective-permute-start | bytes 98312 | tf_op jit(solution)/shard_map/ppermute | solution.py:104
  219.6 13.8 %collective-permute-start.29 = (bf16[128,512]{1,0:T(8,128)(2,1)S(1)}, bf16[128,512]{1,0:T(8,128)(2,1)S(1)}, u32[]{:S(2)}, u32[]{:S(2)}) collective-permute-start(bf16[128,512]{1,0:T(8,128)(2,1)S(1)} %get-tuple-element.115), channel_id=1, source_target_pairs={{2,3},{3,2},{6,7},{7,6},{10,11},{11,10},{14,15},{15,14},{18,19},{1... | collective-permute-start | bytes 393224 | tf_op jit(solution)/shard_map/ppermute | solution.py:104
  235.7 7.7 %collective-permute-start.34 = (bf16[128,640]{1,0:T(8,128)(2,1)S(1)}, bf16[128,640]{1,0:T(8,128)(2,1)S(1)}, u32[]{:S(2)}, u32[]{:S(2)}) collective-permute-start(bf16[128,640]{1,0:T(8,128)(2,1)S(1)} %space_sum.1), channel_id=1, source_target_pairs={{0,24},{4,28},{8,16},{12,20},{16,8},{20,12},{24,0},{28,4},{1,25},{... | collective-permute-start | bytes 491528 | tf_op jit(solution)/shard_map/ppermute | solution.py:104
  236.3 8.0 %collective-permute-start.33 = (bf16[128,640]{1,0:T(8,128)(2,1)S(1)}, bf16[128,640]{1,0:T(8,128)(2,1)S(1)}, u32[]{:S(2)}, u32[]{:S(2)}) collective-permute-start(bf16[128,640]{1,0:T(8,128)(2,1)S(1)} %space_sum.1), channel_id=1, source_target_pairs={{0,16},{4,20},{8,24},{12,28},{16,0},{20,4},{24,8},{28,12},{1,17},{... | collective-permute-start | bytes 491528 | tf_op jit(solution)/shard_map/ppermute | solution.py:104
  244.5 48.3 %collective-permute-start.35 = (bf16[4,128,640]{2,1,0:T(8,128)(2,1)S(1)}, bf16[4,128,640]{2,1,0:T(8,128)(2,1)S(1)}, u32[]{:S(2)}, u32[]{:S(2)}) collective-permute-start(bf16[4,128,640]{2,1,0:T(8,128)(2,1)S(1)} %pad_maximum_fusion.refs_1_), channel_id=1, source_target_pairs={{0,4},{4,0},{8,12},{12,8},{16,20},{20,16},{24,28},{28,24},{1,5},{5... | collective-permute-start | bytes 1966088 | tf_op jit(solution)/shard_map/ppermute | solution.py:104
  244.5 38.1 %collective-permute-start.13 = (bf16[3,272,256]{2,1,0:T(8,128)(2,1)S(1)}, bf16[3,272,256]{2,1,0:T(8,128)(2,1)S(1)}, u32[]{:S(2)}, u32[]{:S(2)}) collective-permute-start(bf16[3,272,256]{2,1,0:T(8,128)(2,1)S(1)} %fusion.refs_5_), channel_id=1, source_target_pairs={{0,2},{1,3},{2,0},{3,1},{4,6},{5,7},{6,4},{7,5},{8,10},{9,11},{10,... | collective-permute-start | bytes 1253384 | tf_op jit(solution)/shard_map/ppermute | solution.py:104
  254.2 37.1 %collective-permute-start.18 = (bf16[3,272,256]{2,1,0:T(8,128)(2,1)S(1)}, bf16[3,272,256]{2,1,0:T(8,128)(2,1)S(1)}, u32[]{:S(2)}, u32[]{:S(2)}) collective-permute-start(bf16[3,272,256]{2,1,0:T(8,128)(2,1)S(1)} %fusion.1.refs_8_), channel_id=1, source_target_pairs={{0,2},{1,3},{2,0},{3,1},{4,6},{5,7},{6,4},{7,5},{8,10},{9,11},{10,... | collective-permute-start | bytes 1253384 | tf_op jit(solution)/shard_map/ppermute | solution.py:104
  (75 other events, 688.6 us)

commit v3 on v2

--- a/solution.py
+++ b/solution.py
@@ -12,6 +12,12 @@
 LANES = 128
 EPSILON = 1e-05
 MIB = 1 << 20
+
+LIMITS = {
+    "early": 16, "tokens": 20, "forward": 24, "columns": 8, "pool_pair": 16, "pool": 16, "norm": 16, "attention": 24, "dn_pair": 16, "joined": 16,
+    "out_grad": 16, "backward": 32, "out_sum": 16, "value_grad": 32, "pair_sum": 16, "packet_split": 16,
+    "space_sum": 16, "out_final": 16, "head_grads": 16, "final": 16, "embed_final": 24,
+}
 
 F32 = jnp.float32
 BF16 = jnp.bfloat16
@@ -71,19 +77,18 @@
     return mm(hi.astype(BF16), fold) + mm(mid.astype(BF16), fold) + mm(lo.astype(BF16), fold)
 
 
-def call(body, out_shape, limit=32, after=(), in_specs=None, **kw):
-    def run(*args):
-        n, m = len(args), len(after)
-        specs = [pl.BlockSpec(memory_space=pltpu.VMEM)] * n if in_specs is None else list(in_specs)
-        return pl.pallas_call(
-            lambda *refs: body(*refs[:n], *refs[n + m :]),
-            out_shape=out_shape,
-            in_specs=specs + [pl.BlockSpec(memory_space=pl.ANY)] * m,
-            compiler_params=pltpu.CompilerParams(vmem_limit_bytes=limit * MIB),
-            **kw,
-        )(*args, *after)
-
-    return run
+def call(body, out_shape, limit=16, **kw):
+    return pl.pallas_call(
+        body,
+        out_shape=out_shape,
+        compiler_params=pltpu.CompilerParams(vmem_limit_bytes=limit * MIB),
+        **kw,
+    )
+
+
+def hold(me, *arrays):
+    zero = sum(x[(0,) * x.ndim].astype(F32) * 0 for x in arrays)
+    return me + zero.astype(jnp.int32)
 
 
 def struct(shape, dtype):
@@ -112,13 +117,26 @@
     return [blocks[0]] + [swap(blocks[k], axis, k) for k in range(1, len(blocks))]
 
 
-def gather_pairs(x, axis):
-    even = jnp.stack([x if k == 0 else swap(x, axis, k) for k in range(0, lax.axis_size(axis), 2)])
+def gather_pairs(x, axis, after=()):
+    even = [x] + [swap(x, axis, k) for k in range(2, lax.axis_size(axis), 2)]
+    even = jnp.stack([late(even[0], *after)] + even[1:])
     return even, swap(even, axis, 1)
 
 
-def exchange_all(x, axis):
-    return lax.all_to_all(x, axis, split_axis=0, concat_axis=0, tiled=True)
+def late(x, *arrays):
+    for other in arrays:
+        x = x + other[(0,) * other.ndim].astype(x.dtype) * 0
+    return x
+
+
+def exchange_pairs(keep, send, combine, after=()):
+    parts = combine(keep, swap(late(send, *after), "var", 1))
+    return [parts[0]] + [swap(parts[k], "var", 2 * k) for k in range(1, len(parts))]
+
+
+def pair_rows(me_v, k, odd, block):
+    device = (((me_v >> 1) ^ k) << 1) + ((me_v & 1) ^ odd)
+    return pl.ds(pl.multiple_of(device * block, block), block)
 
 
 def three_rows(x):
@@ -152,12 +170,11 @@
     wperm_ref[...] = mm(qkvw_ref[...], head_order(qkvw_ref.shape[1])).astype(BF16)
 
 
-def forward_body(
-    count, scale, patches_ref, embed_ref, offset_ref, query_ref, wk_ref, wv_ref,
-    tokens_ref, value_ref, scores_ref, wback_ref, send_ref, wq_ref, held_ref, max_ref, spread_ref, acc_ref,
+def tokens_body(
+    scale, me_ref, patches_ref, embed_ref, offset_ref, query_ref, wk_ref, tokens_ref, scores_ref, wback_ref, wq_ref
 ):
     i = pl.program_id(0)
-    width = wv_ref.shape[1]
+    width = wk_ref.shape[1]
     size = width // HEADS
 
     @pl.when(i == 0)
@@ -174,71 +191,99 @@
         group = iota((width, LANES), 1) >> 4
         back = jnp.where((group == 0) | (group == 2), hi, jnp.where(group == 1, mid, 0.0))
         wback_ref[...] = back.astype(BF16)
-        spread_ref[...] = spread_matrix(width, size)
-
-    @pl.when(i < count)
+
+    tokens = (mm(patches_ref[0], embed_ref[0]) + offset_ref[pl.ds(i, 1), :]).astype(BF16)
+    tokens_ref[0] = tokens
+    pieces = mm(tokens, wq_ref[...])
+    scores_ref[0] = pieces[:, :LANES] + pieces[:, LANES : 2 * LANES] + pieces[:, 2 * LANES :]
+
+
+def forward_body(count, me_ref, tokens_ref, scores_ref, wv_ref, value_ref, keep_ref, send_ref, max_ref, spread_ref, acc_ref):
+    j = pl.program_id(0)
+    width = wv_ref.shape[1]
+
+    @pl.when(j == 0)
     def _():
-        tokens = (mm(patches_ref[0], embed_ref[0]) + offset_ref[pl.ds(i, 1), :]).astype(BF16)
-        tokens_ref[0] = tokens
-        held_ref[i] = tokens
-        pieces = mm(tokens, wq_ref[...])
-        scores_ref[i] = pieces[:, :LANES] + pieces[:, LANES : 2 * LANES] + pieces[:, 2 * LANES :]
-
-    @pl.when(i >= count)
-    def _():
-        j = i - count
+        spread_ref[...] = spread_matrix(width, width // HEADS)
         top = scores_ref[0]
         for v in range(1, count):
             top = jnp.maximum(top, scores_ref[v])
         max_ref[...] = top
-        value = mm(held_ref[j], wv_ref[...])
-        value_ref[0] = value
-        term = mm(pack(jnp.exp(scores_ref[j] - top)), spread_ref[...]) * value
-
-        @pl.when(j == 0)
-        def _():
-            acc_ref[...] = term
-
-        @pl.when(j > 0)
-        def _():
-            acc_ref[...] += term
-
-    @pl.when(i == 2 * count - 1)
+
+    value = mm(tokens_ref[0], wv_ref[...])
+    value_ref[0] = value
+    term = mm(pack(jnp.exp(scores_ref[j] - max_ref[...])), spread_ref[...]) * value
+
+    @pl.when(j == 0)
+    def _():
+        acc_ref[...] = term
+
+    @pl.when(j > 0)
+    def _():
+        acc_ref[...] += term
+
+    @pl.when(j == count - 1)
     def _():
         top = max_ref[...]
         total = sum(jnp.exp(scores_ref[v] - top) for v in range(count))
         low = iota(top.shape, 1) < LANES // 2
-        send_ref[:, :width] = acc_ref[...]
-        send_ref[:, width:] = jnp.where(low, top, total)
-
-
-def pool_body(n_var, in_ref, mixed_ref, packet_ref):
-    block, width = mixed_ref.shape
-    low = iota((block, LANES), 1) < LANES // 2
-    maxima, sums = [], []
-    for k in range(n_var):
-        both = in_ref[k * block : (k + 1) * block, width:]
-        turned = pltpu.roll(both, LANES // 2, 1)
-        maxima.append(jnp.where(low, both, turned))
-        sums.append(jnp.where(low, turned, both))
-    top = functools.reduce(jnp.maximum, maxima)
-    factors = [jnp.exp(m - top) for m in maxima]
-    total = sum(s * f for s, f in zip(sums, factors))
+        max_ref[...] = jnp.where(low, top, total)
+        block = keep_ref.shape[1]
+        core = me_ref[0] & 1
+        for c in range(keep_ref.shape[0]):
+            for ref, device in ((keep_ref, 2 * c + core), (send_ref, 2 * c + 1 - core)):
+                at = pl.ds(pl.multiple_of(device * block, block), block)
+                ref[c, :, :width] = acc_ref[at, :]
+                ref[c, :, width:] = max_ref[at, :]
+
+
+def halves_of(both):
+    low = iota(both.shape, 1) < LANES // 2
+    turned = pltpu.roll(both, LANES // 2, 1)
+    return jnp.where(low, both, turned), jnp.where(low, turned, both)
+
+
+def pool_pair_body(me_ref, keep_ref, got_ref, *out_refs):
+    width = keep_ref.shape[2] - LANES
+    spread = spread_matrix(width, width // HEADS)
+    low = iota((keep_ref.shape[1], LANES), 1) < LANES // 2
+    for k, out_ref in enumerate(out_refs):
+        slot = (me_ref[0] >> 1) ^ k
+        mine, other = keep_ref[slot], got_ref[slot]
+        max_a, sum_a = halves_of(mine[:, width:])
+        max_b, sum_b = halves_of(other[:, width:])
+        top = jnp.maximum(max_a, max_b)
+        factor_a, factor_b = jnp.exp(max_a - top), jnp.exp(max_b - top)
+        out_ref[:, :width] = mine[:, :width] * mm(pack(factor_a), spread) + other[:, :width] * mm(pack(factor_b), spread)
+        out_ref[:, width:] = jnp.where(low, top, sum_a * factor_a + sum_b * factor_b)
+
+
+def pool_body(n, *refs):
+    ins, (mixed_ref, packet_ref) = refs[:n], refs[n:]
+    width = mixed_ref.shape[1]
+    stats = [halves_of(ref[:, width:]) for ref in ins]
+    top = functools.reduce(jnp.maximum, [m for m, _ in stats])
+    factors = [jnp.exp(m - top) for m, _ in stats]
+    total = sum(s * f for (_, s), f in zip(stats, factors))
     spread = spread_matrix(width, width // HEADS)
     mixed = jnp.zeros(mixed_ref.shape, F32)
-    for k, factor in enumerate(factors):
-        mixed = mixed + in_ref[k * block : (k + 1) * block, :width] * mm(pack(factor / total), spread)
+    for ref, factor in zip(ins, factors):
+        mixed = mixed + ref[:, :width] * mm(pack(factor / total), spread)
     mixed_ref[...] = mixed
-    pooled, stats = mixed.astype(BF16), pack(top, total)
-    for k in range(n_var):
-        packet_ref[k * block : (k + 1) * block, :width] = pooled
-        packet_ref[k * block : (k + 1) * block, width:] = stats
-
-
-def norm_body(me_ref, in_ref, agg_ref, gain_ref, w_ref, qkv_ref, normed_ref, centred_ref, inv_ref, all_ref, allinv_ref):
+    packet_ref[:, :width] = mixed.astype(BF16)
+    packet_ref[:, width:] = pack(top, total)
+
+
+def norm_body(
+    me_ref, even_ref, odd_ref, agg_ref, gain_ref, w_ref, qkv_ref, normed_ref, packets_ref, centred_ref, inv_ref,
+    all_ref, allinv_ref,
+):
     width = agg_ref.shape[0]
     block = centred_ref.shape[0]
-    joined = mm(in_ref[:, :width], agg_ref[...]).astype(BF16).astype(F32)
+    for k in range(even_ref.shape[0]):
+        for odd, ref in ((0, even_ref), (1, odd_ref)):
+            packets_ref[pair_rows(me_ref[0], k, odd, block), :] = ref[k]
+    joined = mm(packets_ref[:, :width], agg_ref[...]).astype(BF16).astype(F32)
     mean = jnp.mean(joined, axis=-1, keepdims=True)
     spread_sq = jnp.mean((joined - mean) ** 2, axis=-1, keepdims=True)
     inv = lax.rsqrt(spread_sq + EPSILON)
@@ -255,9 +300,7 @@
 
 def attention_body(n_space, size, scale, me_ref, *refs):
     qkv_refs, dattn_refs = refs[:n_space], refs[n_space : 2 * n_space]
-    w_ref, normed_ref, attn_ref, dqkv_ref, dn_ref = refs[2 * n_space : 2 * n_space + 5]
-    normed_refs = refs[2 * n_space + 5 : 3 * n_space + 5]
-    k_ref, v_ref, dk_ref, dv_ref, cols_ref = refs[3 * n_space + 5 :]
+    w_ref, attn_ref, dqkv_ref, keep_ref, send_ref, k_ref, v_ref, dk_ref, dv_ref, dn_ref = refs[2 * n_space :]
     rows, group = dattn_refs[0].shape
     heads = group // size
     for b in range(n_space):
@@ -299,11 +342,20 @@
     dqkv_ref[:, group : 2 * group] = dk_ref[...].astype(BF16)
     dqkv_ref[:, 2 * group :] = dv_ref[...].astype(BF16)
     dn_ref[...] = mm(dqkv_ref[:rows, :], w_ref[...], NT).astype(BF16)
+    block = keep_ref.shape[1]
+    core = me_ref[0] & 1
+    for c in range(keep_ref.shape[0]):
+        for ref, device in ((keep_ref, 2 * c + core), (send_ref, 2 * c + 1 - core)):
+            ref[c] = dn_ref[pl.ds(pl.multiple_of(device * block, block), block), :]
+
+
+def columns_body(n_space, me_ref, in_ref, *refs):
+    out_refs, (cols_ref,) = refs[:n_space], refs[n_space:]
     cols = cols_ref.shape[2]
     for c in range(n_space):
-        cols_ref[c] = normed_ref[:, c * cols : (c + 1) * cols]
+        cols_ref[c] = in_ref[:, c * cols : (c + 1) * cols]
     for k in range(n_space):
-        normed_refs[k][...] = cols_ref[me_ref[1] ^ k]
+        out_refs[k][...] = cols_ref[me_ref[1] ^ k]
 
 
 def head_grads_body(n_space, *refs):
@@ -321,11 +373,17 @@
     gout_ref[...] = gout
 
 
-def joined_body(n_var, in_ref, centred_ref, inv_ref, gain_ref, cot_ref, mixed_ref, agg_ref, packet_ref, dgain_ref):
-    block, width = centred_ref.shape
-    d_normed = in_ref[:block, :].astype(F32)
-    for k in range(1, n_var):
-        d_normed = d_normed + in_ref[k * block : (k + 1) * block, :].astype(F32)
+def dn_pair_body(me_ref, keep_ref, got_ref, *out_refs):
+    for k, out_ref in enumerate(out_refs):
+        slot = (me_ref[0] >> 1) ^ k
+        out_ref[...] = (keep_ref[slot].astype(F32) + got_ref[slot].astype(F32)).astype(BF16)
+
+
+def joined_body(n, *refs):
+    ins = refs[:n]
+    centred_ref, inv_ref, gain_ref, cot_ref, mixed_ref, agg_ref, packet_ref, dgain_ref = refs[n:]
+    width = centred_ref.shape[1]
+    d_normed = sum(ref[...].astype(F32) for ref in ins)
     centred = centred_ref[...]
     dgain_ref[...] = jnp.broadcast_to(jnp.sum(d_normed * centred, axis=0, keepdims=True), dgain_ref.shape)
     gained = d_normed * gain_ref[...]
@@ -337,14 +395,16 @@
     d_joined = (cot_ref[...].astype(F32) + inner * inv_ref[:, :1]).astype(BF16)
     d_pooled = mm(d_joined, agg_ref[...], NT)
     center = pack(head_sums(d_pooled * mixed_ref[...], fold_matrix(width, width // HEADS)))
-    for k in range(n_var):
-        packet_ref[k * block : (k + 1) * block, :width] = d_joined
-        packet_ref[k * block : (k + 1) * block, width:] = center
-
-
-def out_grad_body(n_space, me_ref, pooled_ref, djoined_ref, dgain_ref, agg_ref, dpool_ref, stat_ref, *refs):
-    out_refs, (all_ref, cols_ref) = refs[:n_space], refs[n_space:]
+    packet_ref[:, :width] = d_joined
+    packet_ref[:, width:] = center
+
+
+def out_grad_body(n_space, me_ref, pooled_ref, even_ref, odd_ref, dgain_ref, agg_ref, dpool_ref, stat_ref, *refs):
+    out_refs, (all_ref, cols_ref, djoined_ref) = refs[:n_space], refs[n_space:]
     width = agg_ref.shape[0]
+    for k in range(even_ref.shape[0]):
+        for odd, ref in ((0, even_ref), (1, odd_ref)):
+            djoined_ref[pair_rows(me_ref[0], k, odd, even_ref.shape[1]), :] = ref[k]
     all_ref[...] = mm(pooled_ref[:, :width], djoined_ref[:, :width], TN)
     cols = cols_ref.shape[2]
     block = out_refs[0].shape[0] - 16
@@ -402,8 +462,8 @@
     ins, (grad_ref, offset_ref) = refs[:-2], refs[-2:]
     pixels = grad_ref.shape[1]
     base = 0
-    for half in range(2):
-        mine = ins[half * parts : (half + 1) * parts]
+    for chunk in range(len(ins) // parts):
+        mine = ins[chunk * parts : (chunk + 1) * parts]
         for v in range(mine[0].shape[1]):
             total = 0.0
             for ref in mine:
@@ -413,14 +473,17 @@
         base += mine[0].shape[1]
 
 
-def value_grad_body(n_var, me_ref, tokens_ref, dv0_ref, dv1_ref, dl0_ref, dl1_ref, keep_ref, send_ref, all_ref):
-    width = dv0_ref.shape[2]
-    flat = lambda ref: ref[...].reshape(ref.shape[0] * ref.shape[1], ref.shape[2])
-    tokens = flat(tokens_ref)
-    middle = dv0_ref.shape[0] * dv0_ref.shape[1]
-    first, second = tokens[:middle, :], tokens[middle:, :]
-    all_ref[:, :width] = (mm(first, flat(dv0_ref), TN) + mm(second, flat(dv1_ref), TN)).astype(BF16)
-    both = mm(first, flat(dl0_ref), TN) + mm(second, flat(dl1_ref), TN)
+def value_grad_body(chunks, me_ref, tokens_ref, *refs):
+    dv_refs, dl_refs, (keep_ref, send_ref, all_ref) = refs[:chunks], refs[chunks : 2 * chunks], refs[2 * chunks :]
+    width = dv_refs[0].shape[2]
+    total, both, base = 0.0, 0.0, 0
+    for dv_ref, dl_ref in zip(dv_refs, dl_refs):
+        for v in range(dv_ref.shape[0]):
+            tokens = tokens_ref[base + v]
+            total = total + mm(tokens, dv_ref[v], TN)
+            both = both + mm(tokens, dl_ref[v], TN)
+        base += dv_ref.shape[0]
+    all_ref[:, :width] = total.astype(BF16)
     all_ref[:, width:] = pack(both[:, :LANES] + both[:, LANES:])
     block = keep_ref.shape[1]
     count = all_ref.shape[0] // block
@@ -445,27 +508,6 @@
         mine, other = keep_ref[slot], got_ref[slot]
         out_refs[k][:, :width] = (mine[:, :width].astype(F32) + other[:, :width].astype(F32)).astype(BF16)
         out_refs[k][:, width:] = pack(unpack(mine[:, width:]) + unpack(other[:, width:]))
-
-
-def out_sum_body(n, *refs):
-    total = refs[0][...].astype(F32)
-    for ref in refs[1:n]:
-        total = total + ref[...].astype(F32)
-    out_ref = refs[n]
-    block = out_ref.shape[0] - 16
-    out_ref[:block, :] = total[:block, :].astype(BF16)
-    out_ref[block:, :] = three_rows(jnp.sum(total[block:, :], axis=0, keepdims=True))
-
-
-def out_final_body(n, me_ref, even_ref, odd_ref, grad_ref, gain_ref):
-    block = even_ref.shape[1] - 16
-    gain = 0.0
-    for k in range(n):
-        part = (odd_ref if k % 2 else even_ref)[k // 2].astype(F32)
-        start = pl.multiple_of((me_ref[0] ^ k) * block, block)
-        grad_ref[pl.ds(start, block), :] = part[:block, :]
-        gain = gain + jnp.sum(part[block:, :], axis=0, keepdims=True)
-    gain_ref[...] = gain
 
 
 def packet_split_body(n_in, n_space, me_ref, *refs):
@@ -482,14 +524,18 @@
         out_refs[k][...] = cols_ref[jnp.maximum((me_ref[1] ^ k) - half, 0)]
 
 
-def space_sum_body(n, *refs):
-    small, large, out_ref = refs[:n], refs[n : 2 * n], refs[2 * n]
-    width = large[0].shape[1]
-    out_ref[:, :width] = sum(ref[...].astype(F32) for ref in large).astype(BF16)
-    out_ref[:, width:] = pack(sum(unpack(ref[...]) for ref in small))
-
-
-def final_body(n_var, n_space, scale, me_ref, even_ref, odd_ref, query_ref, wk_ref, kv_ref, gq_ref):
+def space_sum_body(n, me_ref, *refs):
+    small, large, outs, out_ref = refs[:n], refs[n : 2 * n], refs[2 * n : 3 * n], refs[3 * n]
+    block, width = large[0].shape
+    out_ref[:block, :width] = sum(ref[...].astype(F32) for ref in large).astype(BF16)
+    out_ref[:block, width : width + LANES] = pack(sum(unpack(ref[...]) for ref in small))
+    out_ref[block:, : width + LANES] = jnp.zeros((out_ref.shape[0] - block, width + LANES), BF16)
+    total = sum(ref[...].astype(F32) for ref in outs)
+    out_ref[:block, width + LANES :] = total[:block, :].astype(BF16)
+    out_ref[block:, width + LANES :] = three_rows(jnp.sum(total[block:, :], axis=0, keepdims=True))
+
+
+def final_body(n_var, n_space, scale, me_ref, even_ref, odd_ref, query_ref, wk_ref, kv_ref, gq_ref, out_ref, gain_ref):
     me_v, me_s = me_ref[0], me_ref[1]
     half = n_space // 2
     width = wk_ref.shape[1]
@@ -500,17 +546,20 @@
     qplace = pl.multiple_of(me_s * qcols, LANES)
     spread_q = spread_matrix(qcols, size, qplace)
     query = query_ref[:, pl.ds(place, cols)] * scale
-    block = even_ref.shape[1]
-    total = 0.0
+    block = even_ref.shape[1] - 16
+    total, gain = 0.0, 0.0
     for k in range(n_var):
-        part = (odd_ref if k % 2 else even_ref)[k // 2]
-        start = pl.multiple_of((me_v ^ k) * block, block)
-        packed = part[:, cols:]
+        part_ref, slot = (odd_ref if k % 2 else even_ref), k // 2
+        at = pl.ds(pl.multiple_of((me_v ^ k) * block, block), block)
+        packed = part_ref[slot, :block, cols : cols + LANES]
         key_grad = mm(packed, spread_kv) * query
-        kv_ref[pl.ds(start, block), :] = jnp.where(me_s < half, key_grad, part[:, :cols].astype(F32))
-        keys = wk_ref[pl.ds(start, block), pl.ds(qplace, qcols)].astype(F32)
+        kv_ref[at, :] = jnp.where(me_s < half, key_grad, part_ref[slot, :block, :cols].astype(F32))
+        keys = wk_ref[at, pl.ds(qplace, qcols)].astype(F32)
         total = total + jnp.sum(mm(packed, spread_q) * keys, axis=0, keepdims=True)
+        out_ref[at, :] = part_ref[slot, :block, cols + LANES :].astype(F32)
+        gain = gain + jnp.sum(part_ref[slot, block:, cols + LANES :].astype(F32), axis=0, keepdims=True)
     gq_ref[...] = total * scale
+    gain_ref[...] = gain
 
 
 def shards(
@@ -539,6 +588,7 @@
         + [struct((rows, cols), BF16)] * n_space,
         in_specs=[SMEM] + [vmem] * 3,
         scratch_shapes=[pltpu.VMEM((n_space, rows, cols), BF16)],
+        limit=LIMITS["early"],
         cost_estimate=cost(2e8, 4e6),
         name="early",
     )(me, cotangent, out_weight, qkv_weight)
@@ -546,107 +596,143 @@
     cot_all = exchange_direct(cot_cols, "space")
 
     whole = lambda shape: pl.BlockSpec(shape, lambda v: (0,) * len(shape))
-    last = count - 1
-    first_pass = lambda shape: pl.BlockSpec((1,) + shape, lambda i: (jnp.minimum(i, last),) + (0,) * len(shape))
-    second_pass = lambda shape: pl.BlockSpec((1,) + shape, lambda i: (jnp.maximum(i - count, 0),) + (0,) * len(shape))
-    tokens, value, scores, w_back, send = call(
-        functools.partial(forward_body, count, scale),
-        [
-            struct((count, rows, width), BF16),
-            struct((count, rows, width), F32),
-            struct((count, rows, LANES), F32),
-            struct((width, LANES), BF16),
-            struct((rows, packet), F32),
-        ],
-        limit=48,
-        grid=(2 * count,),
+    every = lambda shape: pl.BlockSpec((1,) + shape, lambda v: (v,) + (0,) * len(shape))
+    n_chip = n_var // 2
+    tokens, scores, w_back = call(
+        functools.partial(tokens_body, scale),
+        [struct((count, rows, width), BF16), struct((count, rows, LANES), F32), struct((width, LANES), BF16)],
+        limit=LIMITS["tokens"],
+        grid=(count,),
         in_specs=[
-            first_pass((rows, pixels)),
-            first_pass((pixels, width)),
+            SMEM,
+            every((rows, pixels)),
+            every((pixels, width)),
             whole((count, width)),
             whole((1, width)),
             pl.BlockSpec((width, width), lambda v: (0, 0)),
+        ],
+        out_specs=[every((rows, width)), every((rows, LANES)), whole((width, LANES))],
+        scratch_shapes=[pltpu.VMEM((width, 3 * LANES), BF16)],
+        cost_estimate=cost(6e9, 2e7),
+        name="tokens",
+    )(hold(me, dattn), patches, embed_weight, var_embed, query, agg_kv)
+    value, keep, send = call(
+        functools.partial(forward_body, count),
+        [struct((count, rows, width), F32)] + [struct((n_chip, block, packet), F32)] * 2,
+        limit=LIMITS["forward"],
+        grid=(count,),
+        in_specs=[
+            SMEM,
+            every((rows, width)),
+            whole((count, rows, LANES)),
             pl.BlockSpec((width, width), lambda v: (0, 1)),
         ],
-        after=[dattn],
-        out_specs=[
-            first_pass((rows, width)),
-            second_pass((rows, width)),
-            whole((count, rows, LANES)),
-            whole((width, LANES)),
-            whole((rows, packet)),
-        ],
+        out_specs=[every((rows, width))] + [whole((n_chip, block, packet))] * 2,
         scratch_shapes=[
-            pltpu.VMEM((width, 3 * LANES), BF16),
-            pltpu.VMEM((count, rows, width), BF16),
             pltpu.VMEM((rows, LANES), F32),
             pltpu.VMEM((LANES, width), BF16),
             pltpu.VMEM((rows, width), F32),
         ],
-        cost_estimate=cost(6e9, 2e7),
+        cost_estimate=cost(4e9, 1e7),
         name="forward",
-    )(patches, embed_weight, var_embed, query, agg_kv, agg_kv)
-
-    received = exchange_all(send, "var")
-    mixed, pooled_copies = call(
-        functools.partial(pool_body, n_var),
-        [struct((block, width), F32), struct((rows, packet), BF16)],
-        after=dattn_all[1:] + cot_all[1:],
-        cost_estimate=cost(1e8, 3e6),
+    )(hold(me, scores, *dattn_all[1:], *cot_all[1:]), tokens, scores, agg_kv)
+
+    def pool_pairs(mine, got):
+        return call(
+            pool_pair_body,
+            [struct((block, packet), F32)] * n_chip,
+            limit=LIMITS["pool_pair"],
+            in_specs=[SMEM, vmem, vmem],
+            cost_estimate=cost(1e8, 3e6),
+            name="pool_pair",
+        )(me, mine, got)
+
+    received = exchange_pairs(keep, send, pool_pairs)
+    mixed, pooled_packet = call(
+        functools.partial(pool_body, n_chip),
+        [struct((block, width), F32), struct((block, packet), BF16)],
+        limit=LIMITS["pool"],
+        cost_estimate=cost(1e8, 2e6),
         name="pool",
-    )(received)
-    pooled_packets = exchange_all(pooled_copies, "var")
-
-    qkv, normed, centred, inv = call(
+    )(*received)
+    pooled_even, pooled_odd = gather_pairs(pooled_packet, "var")
+
+    qkv, normed, pooled_packets, centred, inv = call(
         norm_body,
         [
             struct((rows, 3 * group), BF16),
             struct((rows, width), BF16),
+            struct((rows, packet), BF16),
             struct((block, width), F32),
             struct((block, LANES), F32),
         ],
-        in_specs=[SMEM] + [vmem] * 4,
+        limit=LIMITS["norm"],
+        in_specs=[SMEM] + [vmem] * 5,
         scratch_shapes=[pltpu.VMEM((rows, width), F32), pltpu.VMEM((rows, LANES), F32)],
         cost_estimate=cost(8e8, 5e6),
         name="norm",
-    )(me, pooled_packets, agg_out, gain, w_heads)
+    )(me, pooled_even, pooled_odd, agg_out, gain, w_heads)
 
     qkv_all = gather_direct(qkv, "space")
-    attn, dqkv, d_normed, *normed_cols = call(
+    normed_cols = call(
+        functools.partial(columns_body, n_space),
+        [struct((rows, cols), BF16)] * n_space,
+        limit=LIMITS["columns"],
+        in_specs=[SMEM, vmem],
+        scratch_shapes=[pltpu.VMEM((n_space, rows, cols), BF16)],
+        cost_estimate=cost(1e6, 1e6),
+        name="columns",
+    )(hold(me, *qkv_all[1:]), normed)
+    normed_all = exchange_direct(normed_cols, "space")
+    attn, dqkv, dn_keep, dn_send = call(
         functools.partial(attention_body, n_space, size, scale),
-        [struct((positions, group), BF16), struct((positions, 3 * group), BF16), struct((rows, width), BF16)]
-        + [struct((rows, cols), BF16)] * n_space,
-        limit=48,
-        in_specs=[SMEM] + [vmem] * (2 * n_space + 2),
+        [struct((positions, group), BF16), struct((positions, 3 * group), BF16)]
+        + [struct((n_chip, block, width), BF16)] * 2,
+        limit=LIMITS["attention"],
+        in_specs=[SMEM] + [vmem] * (2 * n_space + 1),
         scratch_shapes=[pltpu.VMEM((positions, group), BF16)] * 2
         + [pltpu.VMEM((positions, group), F32)] * 2
-        + [pltpu.VMEM((n_space, rows, cols), BF16)],
+        + [pltpu.VMEM((rows, width), BF16)],
         cost_estimate=cost(6e9, 4e6),
         name="attention",
-    )(me, *qkv_all, *dattn_all, w_heads, normed)
-
-    dn_received = exchange_all(d_normed, "var")
-    normed_all = exchange_direct(normed_cols, "space")
-    joined_copies, dgain = call(
-        functools.partial(joined_body, n_var),
-        [struct((rows, packet), BF16), struct((8, width), F32)],
-        after=normed_all[1:],
+    )(hold(me, normed_cols[0]), *qkv_all, *dattn_all, w_heads)
+
+    def dn_pairs(mine, got):
+        return call(
+            dn_pair_body,
+            [struct((block, width), BF16)] * n_chip,
+            limit=LIMITS["dn_pair"],
+            in_specs=[SMEM, vmem, vmem],
+            cost_estimate=cost(1e6, 1e6),
+            name="dn_pair",
+        )(me, mine, got)
+
+    dn_received = exchange_pairs(dn_keep, dn_send, dn_pairs, normed_all[1:])
+    joined_packet, dgain = call(
+        functools.partial(joined_body, n_chip),
+        [struct((block, packet), BF16), struct((8, width), F32)],
+        limit=LIMITS["joined"],
         cost_estimate=cost(2e8, 3e6),
         name="joined",
-    )(dn_received, centred, inv, gain, cot_own, mixed, agg_out)
-    joined_packets = exchange_all(joined_copies, "var")
+    )(*dn_received, centred, inv, gain, cot_own, mixed, agg_out)
+    joined_even, joined_odd = gather_pairs(joined_packet, "var")
 
     d_pooled, stat, *out_blocks = call(
         functools.partial(out_grad_body, n_space),
         [struct((rows, width), F32), struct((3, rows, LANES), F32)] + [struct((drows + 16, cols), BF16)] * n_space,
-        in_specs=[SMEM] + [vmem] * 4,
-        scratch_shapes=[pltpu.VMEM((width, width), F32), pltpu.VMEM((n_space, drows + 16, cols), BF16)],
+        limit=LIMITS["out_grad"],
+        in_specs=[SMEM] + [vmem] * 5,
+        scratch_shapes=[
+            pltpu.VMEM((width, width), F32),
+            pltpu.VMEM((n_space, drows + 16, cols), BF16),
+            pltpu.VMEM((rows, packet), BF16),
+        ],
         cost_estimate=cost(1e9, 5e6),
         name="out_grad",
-    )(me, pooled_packets, joined_packets, dgain, agg_out)
+    )(me, pooled_packets, joined_even, joined_odd, dgain, agg_out)
     out_all = exchange_direct(out_blocks, "space")
 
-    def backward(start, size_here, after):
+    def backward(me, start, size_here, work):
         each = lambda shape: pl.BlockSpec((1,) + shape, lambda v: (v + start,) + (0,) * len(shape))
         here = lambda shape: pl.BlockSpec((1,) + shape, lambda v: (v,) + (0,) * len(shape))
         blocks = pl.BlockSpec((n_space // 2, 1, pixels + 16, cols), lambda v: (0, v, 0, 0))
@@ -654,7 +740,7 @@
             functools.partial(backward_body, n_space),
             [struct((size_here, rows, width), BF16), struct((size_here, rows, 2 * LANES), BF16)]
             + [struct((n_space // 2, size_here, pixels + 16, cols), BF16)] * 2,
-            limit=40,
+            limit=LIMITS["backward"],
             grid=(size_here,),
             in_specs=[
                 SMEM,
@@ -667,21 +753,20 @@
                 pl.BlockSpec((width, width), lambda v: (0, 1)),
                 whole((width, LANES)),
             ],
-            after=after,
             out_specs=[here((rows, width)), here((rows, 2 * LANES)), blocks, blocks],
             scratch_shapes=[
                 pltpu.VMEM((LANES, width), BF16),
                 pltpu.VMEM((width, LANES), BF16),
                 pltpu.VMEM((n_space, pixels + 16, cols), BF16),
             ],
-            cost_estimate=cost(4e9, 1.5e7),
+            cost_estimate=work,
             name="backward",
         )(me, d_pooled, stat, tokens, value, scores, patches, agg_kv, w_back)
 
-    def scatter_embed(keep, send):
-        arrived = swap(send, "space", 1)
+    def scatter_embed(keep, arrived, after=()):
         blocks = {
-            2 * j: (keep[j].astype(F32) + arrived[j].astype(F32)).astype(BF16) for j in range(1, n_space // 2)
+            2 * j: (keep[j].astype(F32) + late(arrived[j].astype(F32), *after)).astype(BF16)
+            for j in range(1, n_space // 2)
         }
         sums = list(blocks.values())
         mine, bit = [keep, arrived], 2
@@ -694,39 +779,31 @@
             bit *= 2
         return mine, sums
 
-    middle = count // 2
-    dv0, dl0, keep0, send0 = backward(0, middle, [])
-    out_part = call(
-        functools.partial(out_sum_body, n_space),
-        struct((drows + 16, cols), BF16),
-        cost_estimate=cost(1e6, 3e5),
-        name="out_sum",
-    )(*out_all)
-    dv1, dl1, keep1, send1 = backward(middle, count - middle, [out_part, dv0])
-    mine0, sums0 = scatter_embed(keep0, send0)
-    mine1, sums1 = scatter_embed(keep1, send1)
-    out_even, out_odd = gather_pairs(out_part, "var")
-
-    n_chip = n_var // 2
+    first = count // 3
+    dv0, dl0, keep0, send0 = backward(me, 0, first, cost(4e9, 1e7))
+    dv1, dl1, keep1, send1 = backward(hold(me, dv0), first, count - first, cost(1e6, 1e6))
+    mine0, sums0 = scatter_embed(keep0, swap(send0, "space", 1))
+    arrived1 = swap(send1, "space", 1)
+
     step = max(drows, 256)
-    half_whole = lambda arr: whole(arr.shape)
+    d_values, d_logits = (dv0, dv1), (dl0, dl1)
     kv_keep, kv_send = call(
-        functools.partial(value_grad_body, n_var),
+        functools.partial(value_grad_body, len(d_values)),
         [struct((n_chip, drows, packet), BF16)] * 2,
-        limit=48,
+        limit=LIMITS["value_grad"],
         grid=(width // step,),
         in_specs=[SMEM, pl.BlockSpec((count, rows, step), lambda i: (0, 0, i))]
-        + [half_whole(x) for x in (dv0, dv1, dl0, dl1)],
+        + [whole(x.shape) for x in d_values + d_logits],
         out_specs=[whole((n_chip, drows, packet))] * 2,
         scratch_shapes=[pltpu.VMEM((step, packet), BF16)],
-        cost_estimate=cost(4e9, 1e7),
+        cost_estimate=cost(1e6, 1e6),
         name="value_grad",
-    )(me, tokens, dv0, dv1, dl0, dl1)
+    )(hold(me, dv1, *sums0), tokens, *d_values, *d_logits)
     kv_got = swap(kv_send, "var", 1)
     kv_blocks = call(
         functools.partial(pair_sum_body, n_chip),
         [struct((drows, packet), BF16)] * n_chip,
-        after=[out_even],
+        limit=LIMITS["pair_sum"],
         in_specs=[SMEM] + [vmem] * 2,
         cost_estimate=cost(1e6, 1e6),
         name="pair_sum",
@@ -735,45 +812,41 @@
     small, *large = call(
         functools.partial(packet_split_body, n_chip, n_space),
         [struct((drows, LANES), BF16)] + [struct((drows, kv_cols), BF16)] * n_space,
-        after=sums0,
+        limit=LIMITS["packet_split"],
         in_specs=[SMEM] + [vmem] * n_chip,
         scratch_shapes=[pltpu.VMEM((n_space // 2, drows, kv_cols), BF16)],
         cost_estimate=cost(1e6, 1e6),
         name="packet_split",
-    )(me, *kv_parts)
+    )(hold(me, kv_parts[-1], *mine0[2:]), *kv_parts)
+    grad_qkv, grad_out = call(
+        functools.partial(head_grads_body, n_space),
+        [struct((cols, 3 * group), F32), struct((group, cols), F32)],
+        limit=LIMITS["head_grads"],
+        cost_estimate=cost(1e9, 3e6),
+        name="head_grads",
+    )(*normed_all, *cot_all, dqkv, attn)
+
+    mine1, sums1 = scatter_embed(keep1, arrived1, [small])
     small_all = gather_direct(small, "space")
     large_all = [large[0]] + [
         swap(large[k], "space", k, lambda target: target >= n_space // 2) for k in range(1, n_space)
     ]
     kv_sum = call(
         functools.partial(space_sum_body, n_space),
-        struct((drows, kv_cols + LANES), BF16),
-        after=sums1,
+        struct((drows + 16, kv_cols + LANES + cols), BF16),
+        limit=LIMITS["space_sum"],
+        in_specs=[SMEM] + [vmem] * (3 * n_space),
         cost_estimate=cost(1e6, 1e6),
         name="space_sum",
-    )(*small_all, *large_all)
-
-    grad_agg_out, grad_gain = call(
-        functools.partial(out_final_body, n_var),
-        [struct((width, cols), F32), struct((1, cols), F32)],
-        in_specs=[SMEM] + [vmem] * 2,
-        cost_estimate=cost(1e6, 1e6),
-        name="out_final",
-    )(me, out_even, out_odd)
-
-    grad_qkv, grad_out = call(
-        functools.partial(head_grads_body, n_space),
-        [struct((cols, 3 * group), F32), struct((group, cols), F32)],
-        cost_estimate=cost(1e9, 3e6),
-        name="head_grads",
-    )(*normed_all, *cot_all, dqkv, attn)
-
-    kv_even, kv_odd = gather_pairs(kv_sum, "var")
-    grad_agg_kv, grad_query = call(
+    )(hold(me, large_all[-1], grad_out, *sums1, *mine0[2:]), *small_all, *large_all, *out_all)
+
+    kv_even, kv_odd = gather_pairs(kv_sum, "var", mine1[2:])
+    grad_agg_kv, grad_query, grad_agg_out, grad_gain = call(
         functools.partial(final_body, n_var, n_space, scale),
-        [struct((width, kv_cols), F32), struct((1, cols), F32)],
+        [struct((width, kv_cols), F32), struct((1, cols), F32)] + [struct((width, cols), F32), struct((1, cols), F32)],
         grid=(1,),
         in_specs=[SMEM] + [vmem] * 3 + [pl.BlockSpec((width, width), lambda i: (0, 0))],
+        limit=LIMITS["final"],
         cost_estimate=cost(2e8, 5e6),
         name="final",
     )(me, kv_even, kv_odd, query, agg_kv)
@@ -788,6 +861,7 @@
         [struct((count, pixels, cols), F32), struct((count, cols), F32)],
         grid=(1,),
         in_specs=[first_block(x) for x in mine0 + mine1],
+        limit=LIMITS["embed_final"],
         cost_estimate=cost(1e6, 1e6),
         name="embed_final",
     )(*mine0, *mine1)

time: 296 us -> 288 us (0.973)
  blocking collectives: 28.3 us -> 0 us
  between operations: 1.25 us -> 17.8 us
  starting transfers between devices: 63.4 us -> 70.7 us
  waiting for transfers between devices: 100 us -> 93 us
  local copies, waits for them, and re-layouts: 31.4 us -> 37.9 us
  Pallas kernels: 70.3 us -> 66.1 us
    all_to_all x2 -> x0, blocking collectives: 28.3 us -> none  [exchange_all(): return lax.all_to_all(x, axis, split_axis=0, concat_axis=0, tiled=True)]
    slice x0 -> x25, local copies, waits for them, and re-layouts: none -> 17.2 us  [the longest x20 13.8 us: hold(): zero = sum((x[(0,) * x.ndim].astype(F32) * 0 for x in arrays))]
    ppermute x37 -> x49, starting transfers between devices: 53.6 us -> 70.7 us  [swap(): return lax.ppermute(x, axis, pairs)]
    unnamed x136 -> x112, local copies, waits for them, and re-layouts: 31.4 us -> 20.7 us
    all_to_all x2 -> x0, starting transfers between devices: 9.8 us -> none  [exchange_all(): return lax.all_to_all(x, axis, split_axis=0, concat_axis=0, tiled=True)]
    ppermute x37 -> x49, waiting for transfers between devices: 100 us -> 93 us  [swap(): return lax.ppermute(x, axis, pairs)]
    pallas_call x18 -> x20, Pallas kernels: 70.3 us -> 66.1 us  [the longest x2 13.4 us: backward(): call(functools.partial(backward_body, n_space), [struct((size_here, rows,...]
  transfers between devices with their start and end apart: 39 -> 49, of which waited for: 16 -> 26; matrix products, arithmetic and copies ran while one was open for 0% -> 5% of each run, Pallas kernels for 5% -> 13%
where the time goes in v3:
time: 288 us
  waiting for transfers between devices  93 us (32%)
  starting transfers between devices  70.7 us (25%)
  Pallas kernels  66.1 us (23%)
  local copies, waits for them, and re-layouts  37.9 us (13%)
  between operations  17.8 us (6%)
    ppermute x49, waiting for transfers between devices, swap(): return lax.ppermute(x, axis, pairs)  93 us
    ppermute x49, starting transfers between devices, swap(): return lax.ppermute(x, axis, pairs)  70.7 us
    unnamed x112, local copies, waits for them, and re-layouts  20.7 us
    slice x20, local copies, waits for them, and re-layouts, hold(): zero = sum((x[(0,) * x.ndim].astype(F32) * 0 for x in arrays))  13.8 us
    pallas_call x2, Pallas kernels, backward(): call(functools.partial(backward_body, n_space), [struct((size_here, rows,...  13.4 us
    pallas_call x1, Pallas kernels, shards(): call(functools.partial(attention_body, n_space, size, scale), [struct((po...  12.3 us
    pallas_call x1, Pallas kernels, shards(): call(functools.partial(forward_body, count), [struct((count, rows, width)...  6.8 us
    pallas_call x1, Pallas kernels, shards(): call(functools.partial(value_grad_body, len(d_values)), [struct((n_chip,...  6.05 us
  transfers between devices with their start and end apart: 49, of which 26 were waited for; matrix products, arithmetic and copies ran while one was open for 5% of the time, Pallas kernels for 13%

profile of v3, /device:TPU:0, one launch (start us, length us, event | category | flops | bytes accessed | tf_op | source)
XLA Modules:
  0.0 287.6 jit_solution(3072570374100398032)
XLA Ops:
  3.9 2.0 early.1
  7.5 5.1 %collective-permute-start.2 = (bf16[256,128]{1,0:T(8,128)(2,1)S(1)}, bf16[256,128]{1,0:T(8,128)(2,1)S(1)}, u32[]{:S(2)}, u32[]{:S(2)}) collective-permute-start(bf16[256,128]{1,0:T(8,128)(2,1)S(1)} %get-tuple-element.79.refs_4_), channel_id=1, source_target_pairs={{0,3},{1,2},{2,1},{3,0},{4,7},{5,6},{6,5},{7,4},{8,11},{9,10},{10,... | collective-permute-start | bytes 196616 | tf_op jit(solution)/shard_map/ppermute | solution.py:109
  14.6 2.9 %collective-permute-start.4 = (bf16[256,256]{1,0:T(8,128)(2,1)}, bf16[256,256]{1,0:T(8,128)(2,1)}, u32[]{:S(2)}, u32[]{:S(2)}) collective-permute-start(bf16[256,256]{1,0:T(8,128)(2,1)} %get-tuple-element.82), channel_id=1, source_target_pairs={{0,2},{1,3},{2,0},{3,1},{4,6},{5,7},{6,4},{7,5},{8,10},{9,11},{10,... | collective-permute-start | bytes 393224 | tf_op jit(solution)/shard_map/ppermute | solution.py:109
  19.4 2.2 copy-done
  23.4 5.9 %tokens.1 = (bf16[6,256,1024]{2,1,0:T(8,128)(2,1)S(1)}, f32[6,256,128]{2,1,0:T(8,128)S(1)}, bf16[1024,128]{1,0:T(8,128)(2,1)S(1)}) custom-call(s32[2]{0:T(128)S(1)} %broadcast_add_fusion.7.me_ref, bf16[6,256,256]{2,1,0:T(8,128)(2,1)S(1)} %copy-done.7, bf16[6,256,1024]{2,1,0:T(8,128)(2,1)S(1)} %copy-done.28, f32[6,1024]{1,0:T(8,128)S(1)} %copy-done.51, ...), custom_call_target="tpu_custom_call" | custom-call | flops 6000000000 | bytes 20000000 | tf_op jit(solution)/shard_map/tokens/pallas_call | solution.py:601
  41.8 2.2 copy-done.1
  45.2 6.8 %forward.1 = (f32[6,256,1024]{2,1,0:T(8,128)S(1)}, f32[4,32,1152]{2,1,0:T(8,128)S(1)}, f32[4,32,1152]{2,1,0:T(8,128)S(1)}) custom-call(s32[2]{0:T(128)S(1)} %broadcast_add_fusion.6.me_ref, bf16[6,256,1024]{2,1,0:T(8,128)(2,1)S(1)} %get-tuple-element.84.tokens_ref, f32[6,256,128]{2,1,0:T(8,128)S(1)} %copy-done.10, bf16[1024,2048]{1,0:T(8,128)(2,1)S(1)} %copy-done.1), custom_call_target="tpu_custom_call" | custom-call | flops 4000000000 | bytes 10000000 | tf_op jit(solution)/shard_map/forward/pallas_call | solution.py:619
  58.5 3.1 %collective-permute-done.7.refs_1_ = f32[32,1152]{1,0:T(8,128)S(1)} collective-permute-done((f32[32,1152]{1,0:T(8,128)S(1)}, f32[32,1152]{1,0:T(8,128)S(1)}, u32[]{:S(2)}, u32[]{:S(2)}) %collective-permute-start.7) | collective-permute-done | bytes 147488 | tf_op jit(solution)/shard_map/ppermute | solution.py:109
  61.6 3.7 %collective-permute-done.8.refs_2_ = f32[32,1152]{1,0:T(8,128)S(1)} collective-permute-done((f32[32,1152]{1,0:T(8,128)S(1)}, f32[32,1152]{1,0:T(8,128)S(1)}, u32[]{:S(2)}, u32[]{:S(2)}) %collective-permute-start.8) | collective-permute-done | bytes 147488 | tf_op jit(solution)/shard_map/ppermute | solution.py:109
  69.2 2.2 collective-permute-done.12
  77.4 2.9 %collective-permute-start.14 = (bf16[256,384]{1,0:T(8,128)(2,1)S(1)}, bf16[256,384]{1,0:T(8,128)(2,1)S(1)}, u32[]{:S(2)}, u32[]{:S(2)}) collective-permute-start(bf16[256,384]{1,0:T(8,128)(2,1)S(1)} %get-tuple-element.94.refs_0_), channel_id=1, source_target_pairs={{0,1},{1,0},{2,3},{3,2},{4,5},{5,4},{6,7},{7,6},{8,9},{9,8},{10,11... | collective-permute-start | bytes 589832 | tf_op jit(solution)/shard_map/ppermute | solution.py:109
  80.9 8.9 %collective-permute-done.15.refs_2_ = bf16[256,384]{1,0:T(8,128)(2,1)S(1)} collective-permute-done((bf16[256,384]{1,0:T(8,128)(2,1)S(1)}, bf16[256,384]{1,0:T(8,128)(2,1)S(1)}, u32[]{:S(2)}, u32[]{:S(2)}) %collective-permute-start.15) | collective-permute-done | bytes 196640 | tf_op jit(solution)/shard_map/ppermute | solution.py:109
  97.3 4.0 %collective-permute-start.17 = (bf16[256,256]{1,0:T(8,128)(2,1)S(1)}, bf16[256,256]{1,0:T(8,128)(2,1)S(1)}, u32[]{:S(2)}, u32[]{:S(2)}) collective-permute-start(bf16[256,256]{1,0:T(8,128)(2,1)S(1)} %get-tuple-element.99), channel_id=1, source_target_pairs={{0,1},{1,0},{2,3},{3,2},{4,5},{5,4},{6,7},{7,6},{8,9},{9,8},{10,11... | collective-permute-start | bytes 393224 | tf_op jit(solution)/shard_map/ppermute | solution.py:109
  103.8 12.3 %attention.1 = (bf16[1024,128]{1,0:T(8,128)(2,1)S(1)}, bf16[1024,384]{1,0:T(8,128)(2,1)S(1)}, bf16[4,32,1024]{2,1,0:T(8,128)(2,1)S(1)}, bf16[4,32,1024]{2,1,0:T(8,128)(2,1)S(1)}) custom-call(s32[2]{0:T(128)S(1)} %broadcast_add_fusion.4.me_ref, bf16[256,384]{1,0:T(8,128)(2,1)S(1)} %get-tuple-element.94.refs_0_, ...), custom_call_target="tpu_custom_call" | custom-call | flops 6000000000 | bytes 4000000 | tf_op jit(solution)/shard_map/attention/pallas_call | solution.py:687
  127.3 2.4 collective-permute-done.23.refs_3_
  138.9 2.4 out_grad.1
  142.5 4.4 %backward.2 = (bf16[2,256,1024]{2,1,0:T(8,128)(2,1)S(1)}, bf16[2,256,256]{2,1,0:T(8,128)(2,1)S(1)}, bf16[2,2,272,256]{3,2,1,0:T(8,128)(2,1)S(1)}, bf16[2,2,272,256]{3,2,1,0:T(8,128)(2,1)S(1)}) custom-call(s32[2]{0:T(128)S(1)} %pad_add_fusion.me_ref, f32[256,1024]{1,0:T(8,128)S(1)} %get-tuple-element.112.dpool_ref, ...), custom_call_target="tpu_custom_call" | custom-call | flops 4000000000 | bytes 10000000 | tf_op jit(solution)/shard_map/backward/pallas_call | solution.py:739
  149.4 2.8 copy-done.5
  152.2 8.9 %backward.3 = (bf16[4,256,1024]{2,1,0:T(8,128)(2,1)S(1)}, bf16[4,256,256]{2,1,0:T(8,128)(2,1)S(1)}, bf16[2,4,272,256]{3,2,1,0:T(8,128)(2,1)S(1)}, bf16[2,4,272,256]{3,2,1,0:T(8,128)(2,1)}) custom-call(s32[2]{0:T(128)S(1)} %broadcast_add_fusion.3.me_ref, f32[256,1024]{1,0:T(8,128)S(1)} %get-tuple-element.112.dpool_ref, ...), custom_call_target="tpu_custom_call" | custom-call | flops 1000000 | bytes 1000000 | tf_op jit(solution)/shard_map/backward/pallas_call | solution.py:739
  163.8 6.0 %value_grad.1 = (bf16[4,128,1152]{2,1,0:T(8,128)(2,1)S(1)}, bf16[4,128,1152]{2,1,0:T(8,128)(2,1)S(1)}) custom-call(s32[2]{0:T(128)S(1)} %broadcast_add_fusion.2.me_ref, bf16[6,256,1024]{2,1,0:T(8,128)(2,1)S(1)} %get-tuple-element.84.tokens_ref, bf16[2,256,1024]{2,1,0:T(8,128)(2,1)S(1)} %get-tuple-element.118.refs_0_, ...), custom_call_target="tpu_custom_call" | custom-call | flops 1000000 | bytes 1000000 | tf_op jit(solution)/shard_map/value_grad/pallas_call | solution.py:790
  179.6 22.1 %collective-permute-done.29.refs_2_ = bf16[2,272,256]{2,1,0:T(8,128)(2,1)S(1)} collective-permute-done((bf16[2,272,256]{2,1,0:T(8,128)(2,1)S(1)}, bf16[2,272,256]{2,1,0:T(8,128)(2,1)S(1)}, u32[]{:S(2)}, u32[]{:S(2)}) %collective-permute-start.29) | collective-permute-done | bytes 278560 | tf_op jit(solution)/shard_map/ppermute | solution.py:109
  209.3 3.4 %collective-permute-start.35 = (bf16[4,272,256]{2,1,0:T(8,128)(2,1)}, bf16[4,272,256]{2,1,0:T(8,128)(2,1)S(1)}, u32[]{:S(2)}, u32[]{:S(2)}) collective-permute-start(bf16[4,272,256]{2,1,0:T(8,128)(2,1)} %fusion), channel_id=1, source_target_pairs={{0,2},{1,3},{2,0},{3,1},{4,6},{5,7},{6,4},{7,5},{8,10},{9,11},{10,... | collective-permute-start | bytes 1671176 | tf_op jit(solution)/shard_map/ppermute | solution.py:109
  212.7 3.7 %collective-permute-start.36 = (bf16[128,512]{1,0:T(8,128)(2,1)S(1)}, bf16[128,512]{1,0:T(8,128)(2,1)S(1)}, u32[]{:S(2)}, u32[]{:S(2)}) collective-permute-start(bf16[128,512]{1,0:T(8,128)(2,1)S(1)} %get-tuple-element.133), channel_id=1, source_target_pairs={{0,3},{1,2},{4,7},{5,6},{8,11},{9,10},{12,15},{13,14},{16,19},{17,... | collective-permute-start | bytes 393224 | tf_op jit(solution)/shard_map/ppermute | solution.py:109
  216.7 4.3 %collective-permute-start.44 = (bf16[144,256]{1,0:T(8,128)(2,1)}, bf16[144,256]{1,0:T(8,128)(2,1)}, u32[]{:S(2)}, u32[]{:S(2)}) collective-permute-start(bf16[144,256]{1,0:T(8,128)(2,1)} %get-tuple-element.144), channel_id=1, source_target_pairs={{0,3},{1,2},{2,1},{3,0},{4,7},{5,6},{6,5},{7,4},{8,11},{9,10},{10,... | collective-permute-start | bytes 221192 | tf_op jit(solution)/shard_map/ppermute | solution.py:109
  220.9 9.4 %collective-permute-done.42.refs_9_ = bf16[144,256]{1,0:T(8,128)(2,1)S(1)} collective-permute-done((bf16[144,256]{1,0:T(8,128)(2,1)S(1)}, bf16[144,256]{1,0:T(8,128)(2,1)S(1)}, u32[]{:S(2)}, u32[]{:S(2)}) %collective-permute-start.42) | collective-permute-done | bytes 73760 | tf_op jit(solution)/shard_map/ppermute | solution.py:109
  230.4 13.4 %collective-permute-done.43.refs_10_ = bf16[144,256]{1,0:T(8,128)(2,1)S(1)} collective-permute-done((bf16[144,256]{1,0:T(8,128)(2,1)S(1)}, bf16[144,256]{1,0:T(8,128)(2,1)S(1)}, u32[]{:S(2)}, u32[]{:S(2)}) %collective-permute-start.43) | collective-permute-done | bytes 73760 | tf_op jit(solution)/shard_map/ppermute | solution.py:109
  244.5 11.4 %collective-permute-start.41 = (bf16[128,512]{1,0:T(8,128)(2,1)}, bf16[128,512]{1,0:T(8,128)(2,1)S(1)}, u32[]{:S(2)}, u32[]{:S(2)}) collective-permute-start(bf16[128,512]{1,0:T(8,128)(2,1)} %get-tuple-element.140), channel_id=1, source_target_pairs={{0,2},{1,3},{4,6},{5,7},{8,10},{9,11},{12,14},{13,15},{16,18},{17,... | collective-permute-start | bytes 393224 | tf_op jit(solution)/shard_map/ppermute | solution.py:109
  256.9 3.0 %head_grads.1 = (f32[256,384]{1,0:T(8,128)}, f32[128,256]{1,0:T(8,128)}) custom-call(bf16[256,256]{1,0:T(8,128)(2,1)S(1)} %copy-done.32, bf16[256,256]{1,0:T(8,128)(2,1)S(1)} %copy-done.34, bf16[256,256]{1,0:T(8,128)(2,1)S(1)} %copy-done.36, bf16[256,256]{1,0:T(8,128)(2,1)S(1)} %copy-done.38, bf16[256,256]{1,0:T(8,128)(2,1)S(1)} %copy-done.30, ...), custom_call_target="tpu_custom_call" | custom-call | flops 1000000000 | bytes 3000000 | tf_op jit(solution)/shard_map/head_grads/pallas_call | solution.py:821
  265.1 4.8 %collective-permute-done.38.refs_2_ = bf16[128,128]{1,0:T(8,128)(2,1)S(1)} collective-permute-done((bf16[128,128]{1,0:T(8,128)(2,1)}, bf16[128,128]{1,0:T(8,128)(2,1)S(1)}, u32[]{:S(2)}, u32[]{:S(2)}) %collective-permute-start.38) | collective-permute-done | bytes 32800 | tf_op jit(solution)/shard_map/ppermute | solution.py:109
  275.9 3.3 %collective-permute-done.47 = bf16[144,896]{1,0:T(8,128)(2,1)S(1)} collective-permute-done((bf16[144,896]{1,0:T(8,128)(2,1)S(1)}, bf16[144,896]{1,0:T(8,128)(2,1)S(1)}, u32[]{:S(2)}, u32[]{:S(2)}) %collective-permute-start.47) | collective-permute-done | bytes 258080 | tf_op jit(solution)/shard_map/ppermute | solution.py:109
  279.3 2.6 collective-permute-done.46
  284.8 2.8 final.1
  (239 shorter events, 94.0 us)
Async XLA Ops:
  7.5 11.3 %collective-permute-start.2 = (bf16[256,128]{1,0:T(8,128)(2,1)S(1)}, bf16[256,128]{1,0:T(8,128)(2,1)S(1)}, u32[]{:S(2)}, u32[]{:S(2)}) collective-permute-start(bf16[256,128]{1,0:T(8,128)(2,1)S(1)} %get-tuple-element.79.refs_4_), channel_id=1, source_target_pairs={{0,3},{1,2},{2,1},{3,0},{4,7},{5,6},{6,5},{7,4},{8,11},{9,10},{10,... | collective-permute-start | bytes 196616 | tf_op jit(solution)/shard_map/ppermute | solution.py:109
  12.6 19.9 %collective-permute-start.1 = (bf16[256,128]{1,0:T(8,128)(2,1)S(1)}, bf16[256,128]{1,0:T(8,128)(2,1)S(1)}, u32[]{:S(2)}, u32[]{:S(2)}) collective-permute-start(bf16[256,128]{1,0:T(8,128)(2,1)S(1)} %get-tuple-element.79.refs_4_), channel_id=1, source_target_pairs={{0,2},{1,3},{2,0},{3,1},{4,6},{5,7},{6,4},{7,5},{8,10},{9,11},{10,... | collective-permute-start | bytes 196616 | tf_op jit(solution)/shard_map/ppermute | solution.py:109
  12.6 21.8 %collective-permute-start = (bf16[256,128]{1,0:T(8,128)(2,1)S(1)}, bf16[256,128]{1,0:T(8,128)(2,1)S(1)}, u32[]{:S(2)}, u32[]{:S(2)}) collective-permute-start(bf16[256,128]{1,0:T(8,128)(2,1)S(1)} %get-tuple-element.79.refs_4_), channel_id=1, source_target_pairs={{0,1},{1,0},{2,3},{3,2},{4,5},{5,4},{6,7},{7,6},{8,9},{9,8},{10,11... | collective-permute-start | bytes 196616 | tf_op jit(solution)/shard_map/ppermute | solution.py:109
  13.1 23.1 %collective-permute-start.3 = (bf16[256,256]{1,0:T(8,128)(2,1)}, bf16[256,256]{1,0:T(8,128)(2,1)}, u32[]{:S(2)}, u32[]{:S(2)}) collective-permute-start(bf16[256,256]{1,0:T(8,128)(2,1)} %get-tuple-element.81), channel_id=1, source_target_pairs={{0,1},{1,0},{2,3},{3,2},{4,5},{5,4},{6,7},{7,6},{8,9},{9,8},{10,11... | collective-permute-start | bytes 393224 | tf_op jit(solution)/shard_map/ppermute | solution.py:109
  14.6 23.5 %collective-permute-start.4 = (bf16[256,256]{1,0:T(8,128)(2,1)}, bf16[256,256]{1,0:T(8,128)(2,1)}, u32[]{:S(2)}, u32[]{:S(2)}) collective-permute-start(bf16[256,256]{1,0:T(8,128)(2,1)} %get-tuple-element.82), channel_id=1, source_target_pairs={{0,2},{1,3},{2,0},{3,1},{4,6},{5,7},{6,4},{7,5},{8,10},{9,11},{10,... | collective-permute-start | bytes 393224 | tf_op jit(solution)/shard_map/ppermute | solution.py:109
  18.8 21.1 %collective-permute-start.5 = (bf16[256,256]{1,0:T(8,128)(2,1)}, bf16[256,256]{1,0:T(8,128)(2,1)}, u32[]{:S(2)}, u32[]{:S(2)}) collective-permute-start(bf16[256,256]{1,0:T(8,128)(2,1)} %get-tuple-element.83), channel_id=1, source_target_pairs={{0,3},{1,2},{2,1},{3,0},{4,7},{5,6},{6,5},{7,4},{8,11},{9,10},{10,... | collective-permute-start | bytes 393224 | tf_op jit(solution)/shard_map/ppermute | solution.py:109
  55.0 6.7 %collective-permute-start.7 = (f32[32,1152]{1,0:T(8,128)S(1)}, f32[32,1152]{1,0:T(8,128)S(1)}, u32[]{:S(2)}, u32[]{:S(2)}) collective-permute-start(f32[32,1152]{1,0:T(8,128)S(1)} %get-tuple-element.88), channel_id=1, source_target_pairs={{0,8},{4,12},{8,0},{12,4},{16,24},{20,28},{24,16},{28,20},{1,9},{5... | collective-permute-start | bytes 442376 | tf_op jit(solution)/shard_map/ppermute | solution.py:109
  56.5 8.8 %collective-permute-start.8 = (f32[32,1152]{1,0:T(8,128)S(1)}, f32[32,1152]{1,0:T(8,128)S(1)}, u32[]{:S(2)}, u32[]{:S(2)}) collective-permute-start(f32[32,1152]{1,0:T(8,128)S(1)} %get-tuple-element.89), channel_id=1, source_target_pairs={{0,16},{4,20},{8,24},{12,28},{16,0},{20,4},{24,8},{28,12},{1,17},{... | collective-permute-start | bytes 442376 | tf_op jit(solution)/shard_map/ppermute | solution.py:109
  58.0 7.3 %collective-permute-start.9 = (f32[32,1152]{1,0:T(8,128)S(1)}, f32[32,1152]{1,0:T(8,128)S(1)}, u32[]{:S(2)}, u32[]{:S(2)}) collective-permute-start(f32[32,1152]{1,0:T(8,128)S(1)} %get-tuple-element.90), channel_id=1, source_target_pairs={{0,24},{4,28},{8,16},{12,20},{16,8},{20,12},{24,0},{28,4},{1,25},{... | collective-permute-start | bytes 442376 | tf_op jit(solution)/shard_map/ppermute | solution.py:109
  76.4 13.4 %collective-permute-start.15 = (bf16[256,384]{1,0:T(8,128)(2,1)S(1)}, bf16[256,384]{1,0:T(8,128)(2,1)S(1)}, u32[]{:S(2)}, u32[]{:S(2)}) collective-permute-start(bf16[256,384]{1,0:T(8,128)(2,1)S(1)} %get-tuple-element.94.refs_0_), channel_id=1, source_target_pairs={{0,2},{1,3},{2,0},{3,1},{4,6},{5,7},{6,4},{7,5},{8,10},{9,11},{10,... | collective-permute-start | bytes 589832 | tf_op jit(solution)/shard_map/ppermute | solution.py:109
  77.4 12.9 %collective-permute-start.14 = (bf16[256,384]{1,0:T(8,128)(2,1)S(1)}, bf16[256,384]{1,0:T(8,128)(2,1)S(1)}, u32[]{:S(2)}, u32[]{:S(2)}) collective-permute-start(bf16[256,384]{1,0:T(8,128)(2,1)S(1)} %get-tuple-element.94.refs_0_), channel_id=1, source_target_pairs={{0,1},{1,0},{2,3},{3,2},{4,5},{5,4},{6,7},{7,6},{8,9},{9,8},{10,11... | collective-permute-start | bytes 589832 | tf_op jit(solution)/shard_map/ppermute | solution.py:109
  80.3 13.2 %collective-permute-start.16 = (bf16[256,384]{1,0:T(8,128)(2,1)S(1)}, bf16[256,384]{1,0:T(8,128)(2,1)S(1)}, u32[]{:S(2)}, u32[]{:S(2)}) collective-permute-start(bf16[256,384]{1,0:T(8,128)(2,1)S(1)} %get-tuple-element.94.refs_0_), channel_id=1, source_target_pairs={{0,3},{1,2},{2,1},{3,0},{4,7},{5,6},{6,5},{7,4},{8,11},{9,10},{10,... | collective-permute-start | bytes 589832 | tf_op jit(solution)/shard_map/ppermute | solution.py:109
  97.3 18.9 %collective-permute-start.17 = (bf16[256,256]{1,0:T(8,128)(2,1)S(1)}, bf16[256,256]{1,0:T(8,128)(2,1)S(1)}, u32[]{:S(2)}, u32[]{:S(2)}) collective-permute-start(bf16[256,256]{1,0:T(8,128)(2,1)S(1)} %get-tuple-element.99), channel_id=1, source_target_pairs={{0,1},{1,0},{2,3},{3,2},{4,5},{5,4},{6,7},{7,6},{8,9},{9,8},{10,11... | collective-permute-start | bytes 393224 | tf_op jit(solution)/shard_map/ppermute | solution.py:109
  101.4 16.1 %collective-permute-start.18 = (bf16[256,256]{1,0:T(8,128)(2,1)S(1)}, bf16[256,256]{1,0:T(8,128)(2,1)S(1)}, u32[]{:S(2)}, u32[]{:S(2)}) collective-permute-start(bf16[256,256]{1,0:T(8,128)(2,1)S(1)} %get-tuple-element.100), channel_id=1, source_target_pairs={{0,2},{1,3},{2,0},{3,1},{4,6},{5,7},{6,4},{7,5},{8,10},{9,11},{10,... | collective-permute-start | bytes 393224 | tf_op jit(solution)/shard_map/ppermute | solution.py:109
  101.8 16.8 %collective-permute-start.19 = (bf16[256,256]{1,0:T(8,128)(2,1)S(1)}, bf16[256,256]{1,0:T(8,128)(2,1)S(1)}, u32[]{:S(2)}, u32[]{:S(2)}) collective-permute-start(bf16[256,256]{1,0:T(8,128)(2,1)S(1)} %get-tuple-element.101), channel_id=1, source_target_pairs={{0,3},{1,2},{2,1},{3,0},{4,7},{5,6},{6,5},{7,4},{8,11},{9,10},{10,... | collective-permute-start | bytes 393224 | tf_op jit(solution)/shard_map/ppermute | solution.py:109
  147.0 14.8 %collective-permute-start.28 = (bf16[2,2,272,256]{3,2,1,0:T(8,128)(2,1)S(1)}, bf16[2,2,272,256]{3,2,1,0:T(8,128)(2,1)S(1)}, u32[]{:S(2)}, u32[]{:S(2)}) collective-permute-start(bf16[2,2,272,256]{3,2,1,0:T(8,128)(2,1)S(1)} %get-tuple-element.117), channel_id=1, source_target_pairs={{0,1},{1,0},{2,3},{3,2},{4,5},{5,4},{6,7},{7,6},{8,9},{9,8},{10,11... | collective-permute-start | bytes 1671176 | tf_op jit(solution)/shard_map/ppermute | solution.py:109
  170.0 38.4 %collective-permute-start.30 = (bf16[2,4,272,256]{3,2,1,0:T(8,128)(2,1)}, bf16[2,4,272,256]{3,2,1,0:T(8,128)(2,1)S(1)}, u32[]{:S(2)}, u32[]{:S(2)}) collective-permute-start(bf16[2,4,272,256]{3,2,1,0:T(8,128)(2,1)} %get-tuple-element.120), channel_id=1, source_target_pairs={{0,1},{1,0},{2,3},{3,2},{4,5},{5,4},{6,7},{7,6},{8,9},{9,8},{10,11... | collective-permute-start | bytes 3342344 | tf_op jit(solution)/shard_map/ppermute | solution.py:109
  174.6 29.0 %collective-permute-start.32 = (bf16[128,1152]{1,0:T(8,128)(2,1)S(1)}, bf16[128,1152]{1,0:T(8,128)(2,1)S(1)}, u32[]{:S(2)}, u32[]{:S(2)}) collective-permute-start(bf16[128,1152]{1,0:T(8,128)(2,1)S(1)} %get-tuple-element.126), channel_id=1, source_target_pairs={{0,24},{4,28},{8,16},{12,20},{16,8},{20,12},{24,0},{28,4},{1,25},{... | collective-permute-start | bytes 884744 | tf_op jit(solution)/shard_map/ppermute | solution.py:109
  176.1 25.6 %collective-permute-start.29 = (bf16[2,272,256]{2,1,0:T(8,128)(2,1)S(1)}, bf16[2,272,256]{2,1,0:T(8,128)(2,1)S(1)}, u32[]{:S(2)}, u32[]{:S(2)}) collective-permute-start(bf16[2,272,256]{2,1,0:T(8,128)(2,1)S(1)} %fusion.1), channel_id=1, source_target_pairs={{0,2},{1,3},{2,0},{3,1},{4,6},{5,7},{6,4},{7,5},{8,10},{9,11},{10,... | collective-permute-start | bytes 835592 | tf_op jit(solution)/shard_map/ppermute | solution.py:109
  177.5 27.4 %collective-permute-start.33 = (bf16[128,1152]{1,0:T(8,128)(2,1)}, bf16[128,1152]{1,0:T(8,128)(2,1)S(1)}, u32[]{:S(2)}, u32[]{:S(2)}) collective-permute-start(bf16[128,1152]{1,0:T(8,128)(2,1)} %get-tuple-element.128), channel_id=1, source_target_pairs={{0,8},{4,12},{8,0},{12,4},{16,24},{20,28},{24,16},{28,20},{1,9},{5... | collective-permute-start | bytes 884744 | tf_op jit(solution)/shard_map/ppermute | solution.py:109
  178.7 26.2 %collective-permute-start.34 = (bf16[128,1152]{1,0:T(8,128)(2,1)}, bf16[128,1152]{1,0:T(8,128)(2,1)S(1)}, u32[]{:S(2)}, u32[]{:S(2)}) collective-permute-start(bf16[128,1152]{1,0:T(8,128)(2,1)} %get-tuple-element.129), channel_id=1, source_target_pairs={{0,16},{4,20},{8,24},{12,28},{16,0},{20,4},{24,8},{28,12},{1,17},{... | collective-permute-start | bytes 884744 | tf_op jit(solution)/shard_map/ppermute | solution.py:109
  209.3 65.4 %collective-permute-start.35 = (bf16[4,272,256]{2,1,0:T(8,128)(2,1)}, bf16[4,272,256]{2,1,0:T(8,128)(2,1)S(1)}, u32[]{:S(2)}, u32[]{:S(2)}) collective-permute-start(bf16[4,272,256]{2,1,0:T(8,128)(2,1)} %fusion), channel_id=1, source_target_pairs={{0,2},{1,3},{2,0},{3,1},{4,6},{5,7},{6,4},{7,5},{8,10},{9,11},{10,... | collective-permute-start | bytes 1671176 | tf_op jit(solution)/shard_map/ppermute | solution.py:109
  212.7 31.7 %collective-permute-start.36 = (bf16[128,512]{1,0:T(8,128)(2,1)S(1)}, bf16[128,512]{1,0:T(8,128)(2,1)S(1)}, u32[]{:S(2)}, u32[]{:S(2)}) collective-permute-start(bf16[128,512]{1,0:T(8,128)(2,1)S(1)} %get-tuple-element.133), channel_id=1, source_target_pairs={{0,3},{1,2},{4,7},{5,6},{8,11},{9,10},{12,15},{13,14},{16,19},{17,... | collective-permute-start | bytes 393224 | tf_op jit(solution)/shard_map/ppermute | solution.py:109
  216.5 13.9 %collective-permute-start.42 = (bf16[144,256]{1,0:T(8,128)(2,1)S(1)}, bf16[144,256]{1,0:T(8,128)(2,1)S(1)}, u32[]{:S(2)}, u32[]{:S(2)}) collective-permute-start(bf16[144,256]{1,0:T(8,128)(2,1)S(1)} %copy-done.42), channel_id=1, source_target_pairs={{0,1},{1,0},{2,3},{3,2},{4,5},{5,4},{6,7},{7,6},{8,9},{9,8},{10,11... | collective-permute-start | bytes 221192 | tf_op jit(solution)/shard_map/ppermute | solution.py:109
  216.6 27.2 %collective-permute-start.43 = (bf16[144,256]{1,0:T(8,128)(2,1)S(1)}, bf16[144,256]{1,0:T(8,128)(2,1)S(1)}, u32[]{:S(2)}, u32[]{:S(2)}) collective-permute-start(bf16[144,256]{1,0:T(8,128)(2,1)S(1)} %copy-done.40), channel_id=1, source_target_pairs={{0,2},{1,3},{2,0},{3,1},{4,6},{5,7},{6,4},{7,5},{8,10},{9,11},{10,... | collective-permute-start | bytes 221192 | tf_op jit(solution)/shard_map/ppermute | solution.py:109
  216.7 48.1 %collective-permute-start.44 = (bf16[144,256]{1,0:T(8,128)(2,1)}, bf16[144,256]{1,0:T(8,128)(2,1)}, u32[]{:S(2)}, u32[]{:S(2)}) collective-permute-start(bf16[144,256]{1,0:T(8,128)(2,1)} %get-tuple-element.144), channel_id=1, source_target_pairs={{0,3},{1,2},{2,1},{3,0},{4,7},{5,6},{6,5},{7,4},{8,11},{9,10},{10,... | collective-permute-start | bytes 221192 | tf_op jit(solution)/shard_map/ppermute | solution.py:109
  230.4 34.5 %collective-permute-start.39 = (bf16[128,128]{1,0:T(8,128)(2,1)}, bf16[128,128]{1,0:T(8,128)(2,1)}, u32[]{:S(2)}, u32[]{:S(2)}) collective-permute-start(bf16[128,128]{1,0:T(8,128)(2,1)} %get-tuple-element.130.refs_0_), channel_id=1, source_target_pairs={{0,3},{1,2},{2,1},{3,0},{4,7},{5,6},{6,5},{7,4},{8,11},{9,10},{10,... | collective-permute-start | bytes 98312 | tf_op jit(solution)/shard_map/ppermute | solution.py:109
  243.8 26.1 %collective-permute-start.40 = (bf16[128,512]{1,0:T(8,128)(2,1)}, bf16[128,512]{1,0:T(8,128)(2,1)S(1)}, u32[]{:S(2)}, u32[]{:S(2)}) collective-permute-start(bf16[128,512]{1,0:T(8,128)(2,1)} %get-tuple-element.139), channel_id=1, source_target_pairs={{2,3},{3,2},{6,7},{7,6},{10,11},{11,10},{14,15},{15,14},{18,19},{1... | collective-permute-start | bytes 393224 | tf_op jit(solution)/shard_map/ppermute | solution.py:109
  244.5 25.4 %collective-permute-start.41 = (bf16[128,512]{1,0:T(8,128)(2,1)}, bf16[128,512]{1,0:T(8,128)(2,1)S(1)}, u32[]{:S(2)}, u32[]{:S(2)}) collective-permute-start(bf16[128,512]{1,0:T(8,128)(2,1)} %get-tuple-element.140), channel_id=1, source_target_pairs={{0,2},{1,3},{4,6},{5,7},{8,10},{9,11},{12,14},{13,15},{16,18},{17,... | collective-permute-start | bytes 393224 | tf_op jit(solution)/shard_map/ppermute | solution.py:109
  271.1 8.1 %collective-permute-start.47 = (bf16[144,896]{1,0:T(8,128)(2,1)S(1)}, bf16[144,896]{1,0:T(8,128)(2,1)S(1)}, u32[]{:S(2)}, u32[]{:S(2)}) collective-permute-start(bf16[144,896]{1,0:T(8,128)(2,1)S(1)} %space_sum.1), channel_id=1, source_target_pairs={{0,24},{4,28},{8,16},{12,20},{16,8},{20,12},{24,0},{28,4},{1,25},{... | collective-permute-start | bytes 774152 | tf_op jit(solution)/shard_map/ppermute | solution.py:109
  272.6 9.3 %collective-permute-start.46 = (bf16[144,896]{1,0:T(8,128)(2,1)S(1)}, bf16[144,896]{1,0:T(8,128)(2,1)S(1)}, u32[]{:S(2)}, u32[]{:S(2)}) collective-permute-start(bf16[144,896]{1,0:T(8,128)(2,1)S(1)} %space_sum.1), channel_id=1, source_target_pairs={{0,16},{4,20},{8,24},{12,28},{16,0},{20,4},{24,8},{28,12},{1,17},{... | collective-permute-start | bytes 774152 | tf_op jit(solution)/shard_map/ppermute | solution.py:109
  274.2 7.7 %collective-permute-start.45 = (bf16[144,896]{1,0:T(8,128)(2,1)S(1)}, bf16[144,896]{1,0:T(8,128)(2,1)S(1)}, u32[]{:S(2)}, u32[]{:S(2)}) collective-permute-start(bf16[144,896]{1,0:T(8,128)(2,1)S(1)} %space_sum.1), channel_id=1, source_target_pairs={{0,8},{4,12},{8,0},{12,4},{16,24},{20,28},{24,16},{28,20},{1,9},{5... | collective-permute-start | bytes 774152 | tf_op jit(solution)/shard_map/ppermute | solution.py:109
  (73 other events, 973.2 us)

commit v4 on v3

--- a/solution.py
+++ b/solution.py
@@ -14,9 +14,9 @@
 MIB = 1 << 20
 
 LIMITS = {
-    "early": 16, "tokens": 20, "forward": 24, "columns": 8, "pool_pair": 16, "pool": 16, "norm": 16, "attention": 24, "dn_pair": 16, "joined": 16,
-    "out_grad": 16, "backward": 32, "out_sum": 16, "value_grad": 32, "pair_sum": 16, "packet_split": 16,
-    "space_sum": 16, "out_final": 16, "head_grads": 16, "final": 16, "embed_final": 24,
+    "early": 16, "tokens": 56, "forward": 56, "columns": 8, "pool_pair": 16, "pool": 16, "norm": 16, "attention": 24,
+    "dn": 12, "dn_pair": 16, "joined": 16, "prepare": 16, "out_grad": 16, "dvalue": 24, "embed": 24, "value_grad": 32,
+    "add": 12, "pair_sum": 16, "packet_split": 16, "space_sum": 16, "head_grads": 16, "final": 16, "embed_final": 24,
 }
 
 F32 = jnp.float32
@@ -77,18 +77,19 @@
     return mm(hi.astype(BF16), fold) + mm(mid.astype(BF16), fold) + mm(lo.astype(BF16), fold)
 
 
-def call(body, out_shape, limit=16, **kw):
-    return pl.pallas_call(
-        body,
-        out_shape=out_shape,
-        compiler_params=pltpu.CompilerParams(vmem_limit_bytes=limit * MIB),
-        **kw,
-    )
-
-
-def hold(me, *arrays):
-    zero = sum(x[(0,) * x.ndim].astype(F32) * 0 for x in arrays)
-    return me + zero.astype(jnp.int32)
+def call(body, out_shape, limit=16, after=(), in_specs=None, **kw):
+    def run(*args):
+        n, m = len(args), len(after)
+        vmem = pl.BlockSpec(memory_space=pltpu.VMEM)
+        return pl.pallas_call(
+            lambda *refs: body(*refs[:n], *refs[n + m :]),
+            out_shape=out_shape,
+            in_specs=([vmem] * n if in_specs is None else list(in_specs)) + [vmem] * m,
+            compiler_params=pltpu.CompilerParams(vmem_limit_bytes=limit * MIB),
+            **kw,
+        )(*args, *after)
+
+    return run
 
 
 def struct(shape, dtype):
@@ -117,20 +118,14 @@
     return [blocks[0]] + [swap(blocks[k], axis, k) for k in range(1, len(blocks))]
 
 
-def gather_pairs(x, axis, after=()):
+def gather_pairs(x, axis, stack=jnp.stack):
     even = [x] + [swap(x, axis, k) for k in range(2, lax.axis_size(axis), 2)]
-    even = jnp.stack([late(even[0], *after)] + even[1:])
+    even = stack(even)
     return even, swap(even, axis, 1)
 
 
-def late(x, *arrays):
-    for other in arrays:
-        x = x + other[(0,) * other.ndim].astype(x.dtype) * 0
-    return x
-
-
-def exchange_pairs(keep, send, combine, after=()):
-    parts = combine(keep, swap(late(send, *after), "var", 1))
+def exchange_pairs(keep, send, combine):
+    parts = combine(keep, swap(send, "var", 1))
     return [parts[0]] + [swap(parts[k], "var", 2 * k) for k in range(1, len(parts))]
 
 
@@ -157,21 +152,15 @@
     return jnp.where(take, 1.0, 0.0).astype(BF16)
 
 
-def early_body(n_space, me_ref, cot_ref, outw_ref, qkvw_ref, dattn_ref, own_ref, wperm_ref, *rest):
-    cot_refs, (cols_ref,) = rest[:n_space], rest[n_space:]
+def early_body(me_ref, cot_ref, outw_ref, qkvw_ref, dattn_ref, own_ref, wperm_ref):
     dattn_ref[...] = mm(cot_ref[...], outw_ref[...], NT).astype(BF16)
     block = own_ref.shape[0]
     own_ref[...] = cot_ref[pl.ds(pl.multiple_of(me_ref[0] * block, block), block), :]
-    width = cols_ref.shape[2]
-    for c in range(n_space):
-        cols_ref[c] = cot_ref[:, c * width : (c + 1) * width]
-    for k in range(n_space):
-        cot_refs[k][...] = cols_ref[me_ref[1] ^ k]
     wperm_ref[...] = mm(qkvw_ref[...], head_order(qkvw_ref.shape[1])).astype(BF16)
 
 
 def tokens_body(
-    scale, me_ref, patches_ref, embed_ref, offset_ref, query_ref, wk_ref, tokens_ref, scores_ref, wback_ref, wq_ref
+    scale, patches_ref, embed_ref, offset_ref, query_ref, wk_ref, tokens_ref, scores_ref, wback_ref, wq_ref
 ):
     i = pl.program_id(0)
     width = wk_ref.shape[1]
@@ -298,9 +287,9 @@
     inv_ref[...] = allinv_ref[pl.ds(start, block), :]
 
 
-def attention_body(n_space, size, scale, me_ref, *refs):
+def attention_body(n_space, size, scale, *refs):
     qkv_refs, dattn_refs = refs[:n_space], refs[n_space : 2 * n_space]
-    w_ref, attn_ref, dqkv_ref, keep_ref, send_ref, k_ref, v_ref, dk_ref, dv_ref, dn_ref = refs[2 * n_space :]
+    attn_ref, dqkv_ref, k_ref, v_ref, dk_ref, dv_ref = refs[2 * n_space :]
     rows, group = dattn_refs[0].shape
     heads = group // size
     for b in range(n_space):
@@ -341,7 +330,10 @@
         dqkv_ref[at, :group] = dq.astype(BF16)
     dqkv_ref[:, group : 2 * group] = dk_ref[...].astype(BF16)
     dqkv_ref[:, 2 * group :] = dv_ref[...].astype(BF16)
-    dn_ref[...] = mm(dqkv_ref[:rows, :], w_ref[...], NT).astype(BF16)
+
+
+def dn_body(me_ref, dqkv_ref, w_ref, keep_ref, send_ref, dn_ref):
+    dn_ref[...] = mm(dqkv_ref[...], w_ref[...], NT).astype(BF16)
     block = keep_ref.shape[1]
     core = me_ref[0] & 1
     for c in range(keep_ref.shape[0]):
@@ -359,18 +351,13 @@
 
 
 def head_grads_body(n_space, *refs):
-    normed_refs, cot_refs = refs[:n_space], refs[n_space : 2 * n_space]
-    dqkv_ref, attn_ref, gqkv_ref, gout_ref = refs[2 * n_space :]
+    normed_refs, (dqkv_ref, gqkv_ref, flag_ref) = refs[:n_space], refs[n_space:]
+    flag_ref[...] = jnp.zeros(flag_ref.shape, F32)
     rows = normed_refs[0].shape[0]
-    order = head_order(dqkv_ref.shape[1])
-    natural = mm(dqkv_ref[...], order, NT).astype(BF16)
-    gqkv, gout = 0.0, 0.0
-    for b in range(n_space):
-        at = slice(b * rows, (b + 1) * rows)
-        gqkv = gqkv + mm(normed_refs[b][...], natural[at, :], TN)
-        gout = gout + mm(attn_ref[at, :], cot_refs[b][...], TN)
-    gqkv_ref[...] = gqkv
-    gout_ref[...] = gout
+    natural = mm(dqkv_ref[...], head_order(dqkv_ref.shape[1]), NT).astype(BF16)
+    gqkv_ref[...] = sum(
+        mm(ref[...], natural[b * rows : (b + 1) * rows, :], TN) for b, ref in enumerate(normed_refs)
+    )
 
 
 def dn_pair_body(me_ref, keep_ref, got_ref, *out_refs):
@@ -399,34 +386,34 @@
     packet_ref[:, width:] = center
 
 
-def out_grad_body(n_space, me_ref, pooled_ref, even_ref, odd_ref, dgain_ref, agg_ref, dpool_ref, stat_ref, *refs):
-    out_refs, (all_ref, cols_ref, djoined_ref) = refs[:n_space], refs[n_space:]
+def prepare_body(me_ref, pooled_ref, even_ref, odd_ref, agg_ref, djoined_ref, dpool_ref, stat_ref):
     width = agg_ref.shape[0]
     for k in range(even_ref.shape[0]):
         for odd, ref in ((0, even_ref), (1, odd_ref)):
             djoined_ref[pair_rows(me_ref[0], k, odd, even_ref.shape[1]), :] = ref[k]
+    dpool_ref[...] = mm(djoined_ref[:, :width], agg_ref[...], NT)
+    stat_ref[0] = unpack(djoined_ref[:, width:])
+    stat_ref[1] = unpack(pooled_ref[:, width:])
+    stat_ref[2] = 1.0 / unpack(pooled_ref[:, width:], 3)
+
+
+def out_grad_body(me_ref, pooled_ref, djoined_ref, dgain_ref, attn_ref, cot_ref, out_ref, all_ref):
+    width = dgain_ref.shape[1]
     all_ref[...] = mm(pooled_ref[:, :width], djoined_ref[:, :width], TN)
-    cols = cols_ref.shape[2]
-    block = out_refs[0].shape[0] - 16
+    weight_grad = mm(attn_ref[...], cot_ref[...], TN).astype(BF16)
+    n_space, height, cols = out_ref.shape
+    block = height - 16 - weight_grad.shape[0]
     start = pl.multiple_of(me_ref[0] * block, block)
     own = all_ref[pl.ds(start, block), :].astype(BF16)
     extra = three_rows(dgain_ref[:1, :])
     for c in range(n_space):
-        cols_ref[c, :block, :] = own[:, c * cols : (c + 1) * cols]
-        cols_ref[c, block:, :] = extra[:, c * cols : (c + 1) * cols]
-    for k in range(n_space):
-        out_refs[k][...] = cols_ref[me_ref[1] ^ k]
-    dpool_ref[...] = mm(djoined_ref[:, :width], agg_ref[...], NT)
-    stat_ref[0] = unpack(djoined_ref[:, width:])
-    stat_ref[1] = unpack(pooled_ref[:, width:])
-    stat_ref[2] = 1.0 / unpack(pooled_ref[:, width:], 3)
-
-
-def backward_body(
-    n_space, me_ref, dpool_ref, stat_ref, tokens_ref, value_ref, scores_ref, patches_ref, wv_ref, wback_ref,
-    dvalue_ref, dlogit_ref, keep_ref, send_ref, spread_ref, fold_ref, cols_ref,
-):
-    width = wv_ref.shape[0]
+        out_ref[c, :block, :] = own[:, c * cols : (c + 1) * cols]
+        out_ref[c, block : block + 16, :] = extra[:, c * cols : (c + 1) * cols]
+        out_ref[c, block + 16 :, :] = weight_grad[:, c * cols : (c + 1) * cols]
+
+
+def dvalue_body(dpool_ref, stat_ref, value_ref, scores_ref, dvalue_ref, dlogit_ref, spread_ref, fold_ref):
+    width = dpool_ref.shape[1]
     size = width // HEADS
 
     @pl.when(pl.program_id(0) == 0)
@@ -435,27 +422,52 @@
         fold_ref[...] = fold_matrix(width, size)
 
     weight = jnp.exp(scores_ref[0] - stat_ref[1]) * stat_ref[2]
-    d_value = (mm(pack(weight), spread_ref[...]) * dpool_ref[...]).astype(BF16)
-    dvalue_ref[0] = d_value
+    dvalue_ref[0] = (mm(pack(weight), spread_ref[...]) * dpool_ref[...]).astype(BF16)
     dweight = head_sums(dpool_ref[...] * value_ref[0], fold_ref[...])
     dlogit = weight * (dweight - stat_ref[0])
-    hi = dlogit.astype(BF16).astype(F32)
-    lo = (dlogit - hi).astype(BF16)
-    dlogit_ref[0, :, :LANES] = hi.astype(BF16)
-    dlogit_ref[0, :, LANES:] = lo
-    group = iota(dlogit.shape, 1) >> 4
-    mixed = jnp.where(group < 2, hi, jnp.where(group == 2, lo.astype(F32), 0.0)).astype(BF16)
-    d_tokens = (mm(d_value, wv_ref[...], NT) + mm(mixed, wback_ref[...], NT)).astype(BF16)
+    hi = dlogit.astype(BF16)
+    dlogit_ref[0, :, :LANES] = hi
+    dlogit_ref[0, :, LANES:] = (dlogit - hi.astype(F32)).astype(BF16)
+
+
+def embed_body(
+    n_space, me_ref, dvalue_ref, dlogit_ref, patches_ref, wv_ref, wback_ref, keep_ref, send_ref, cols_ref, extra_ref
+):
+    v = pl.program_id(0)
+    hi, lo = dlogit_ref[0, :, :LANES].astype(F32), dlogit_ref[0, :, LANES:].astype(F32)
+    group = iota(hi.shape, 1) >> 4
+    mixed = jnp.where(group < 2, hi, jnp.where(group == 2, lo, 0.0)).astype(BF16)
+    d_tokens = (mm(dvalue_ref[0], wv_ref[...], NT) + mm(mixed, wback_ref[...], NT)).astype(BF16)
     grad = mm(patches_ref[0], d_tokens, TN).astype(BF16)
-    extra = three_rows(jnp.sum(d_tokens.astype(F32), axis=0, keepdims=True))
+    hi, lo, _ = parts3(jnp.sum(d_tokens.astype(F32), axis=0, keepdims=True))
+    row = iota(extra_ref.shape, 0)
+    extra = jnp.where(row == 2 * v, hi, jnp.where(row == 2 * v + 1, lo, 0.0))
+
+    @pl.when(v == 0)
+    def _():
+        extra_ref[...] = extra
+
+    @pl.when(v > 0)
+    def _():
+        extra_ref[...] += extra
+
     cols = cols_ref.shape[2]
     pixels = patches_ref.shape[2]
     for c in range(n_space):
-        cols_ref[c, :pixels, :] = grad[:, c * cols : (c + 1) * cols]
-        cols_ref[c, pixels:, :] = extra[:, c * cols : (c + 1) * cols]
+        cols_ref[c] = grad[:, c * cols : (c + 1) * cols]
+    at = pl.ds(pl.multiple_of(v * pixels, pixels), pixels)
     for k in range(0, n_space, 2):
-        keep_ref[k // 2, 0] = cols_ref[me_ref[1] ^ k]
-        send_ref[k // 2, 0] = cols_ref[me_ref[1] ^ (k + 1)]
+        keep_ref[k // 2, at, :] = cols_ref[me_ref[1] ^ k]
+        send_ref[k // 2, at, :] = cols_ref[me_ref[1] ^ (k + 1)]
+
+    @pl.when(v == pl.num_programs(0) - 1)
+    def _():
+        tail = slice(keep_ref.shape[1] - 16, keep_ref.shape[1])
+        for c in range(n_space):
+            cols_ref[c, :16, :] = extra_ref[:, c * cols : (c + 1) * cols].astype(BF16)
+        for k in range(0, n_space, 2):
+            keep_ref[k // 2, tail, :] = cols_ref[me_ref[1] ^ k, :16, :]
+            send_ref[k // 2, tail, :] = cols_ref[me_ref[1] ^ (k + 1), :16, :]
 
 
 def embed_final_body(parts, *refs):
@@ -463,26 +475,28 @@
     pixels = grad_ref.shape[1]
     base = 0
     for chunk in range(len(ins) // parts):
-        mine = ins[chunk * parts : (chunk + 1) * parts]
-        for v in range(mine[0].shape[1]):
-            total = 0.0
-            for ref in mine:
-                total = total + (ref[0, v] if len(ref.shape) == 4 else ref[v]).astype(F32)
-            grad_ref[base + v] = total[:pixels, :]
-            offset_ref[base + v : base + v + 1, :] = jnp.sum(total[pixels:, :], axis=0, keepdims=True)
-        base += mine[0].shape[1]
-
-
-def value_grad_body(chunks, me_ref, tokens_ref, *refs):
-    dv_refs, dl_refs, (keep_ref, send_ref, all_ref) = refs[:chunks], refs[chunks : 2 * chunks], refs[2 * chunks :]
-    width = dv_refs[0].shape[2]
-    total, both, base = 0.0, 0.0, 0
-    for dv_ref, dl_ref in zip(dv_refs, dl_refs):
-        for v in range(dv_ref.shape[0]):
-            tokens = tokens_ref[base + v]
-            total = total + mm(tokens, dv_ref[v], TN)
-            both = both + mm(tokens, dl_ref[v], TN)
-        base += dv_ref.shape[0]
+        total = 0.0
+        for ref in ins[chunk * parts : (chunk + 1) * parts]:
+            total = total + (ref[0] if len(ref.shape) == 3 else ref[...]).astype(F32)
+        count = (total.shape[0] - 16) // pixels
+        for v in range(count):
+            grad_ref[base + v] = total[v * pixels : (v + 1) * pixels, :]
+            row = count * pixels + 2 * v
+            offset_ref[base + v : base + v + 1, :] = total[row : row + 1, :] + total[row + 1 : row + 2, :]
+        base += count
+
+
+def stack_body(*refs):
+    for k, ref in enumerate(refs[:-1]):
+        refs[-1][k] = ref[...]
+
+
+def value_grad_body(me_ref, tokens_ref, dv_ref, dl_ref, keep_ref, send_ref, all_ref):
+    width = dv_ref.shape[2]
+    total, both = 0.0, 0.0
+    for v in range(dv_ref.shape[0]):
+        total = total + mm(tokens_ref[v], dv_ref[v], TN)
+        both = both + mm(tokens_ref[v], dl_ref[v], TN)
     all_ref[:, :width] = total.astype(BF16)
     all_ref[:, width:] = pack(both[:, :LANES] + both[:, LANES:])
     block = keep_ref.shape[1]
@@ -511,28 +525,46 @@
 
 
 def packet_split_body(n_in, n_space, me_ref, *refs):
-    ins, small_ref = refs[:n_in], refs[n_in]
-    out_refs, (cols_ref,) = refs[n_in + 1 : n_in + 1 + n_space], refs[n_in + 1 + n_space :]
-    width = ins[0].shape[1] - LANES
+    ins, gathered_ref = refs[:n_in], refs[n_in]
+    small_refs, out_refs = refs[n_in + 1 : n_in + 1 + n_space], refs[n_in + 1 + n_space : n_in + 1 + 2 * n_space]
+    cols_ref = refs[-1]
+    block, width = ins[0].shape[0], ins[0].shape[1] - LANES
     total = sum(ref[:, :width].astype(F32) for ref in ins).astype(BF16)
-    small_ref[...] = pack(sum(unpack(ref[:, width:]) for ref in ins))
+    factor = pack(sum(unpack(ref[:, width:]) for ref in ins))
     half = n_space // 2
     cols = cols_ref.shape[2]
     for c in range(half):
         cols_ref[c] = total[:, c * cols : (c + 1) * cols]
+    height = gathered_ref.shape[1]
+    part = small_refs[0].shape[0] - height
     for k in range(n_space):
         out_refs[k][...] = cols_ref[jnp.maximum((me_ref[1] ^ k) - half, 0)]
-
-
-def space_sum_body(n, me_ref, *refs):
-    small, large, outs, out_ref = refs[:n], refs[n : 2 * n], refs[2 * n : 3 * n], refs[3 * n]
+        small_refs[k][:height, :] = gathered_ref[me_ref[1] ^ k]
+        for piece in range(block // part):
+            lanes = slice(piece * LANES, (piece + 1) * LANES)
+            small_refs[k][height:, lanes] = factor[piece * part : (piece + 1) * part, :]
+
+
+def space_sum_body(n, *refs):
+    small, large, (out_ref, weight_ref) = refs[:n], refs[n : 2 * n], refs[2 * n :]
     block, width = large[0].shape
     out_ref[:block, :width] = sum(ref[...].astype(F32) for ref in large).astype(BF16)
-    out_ref[:block, width : width + LANES] = pack(sum(unpack(ref[...]) for ref in small))
+    height = block + 16 + weight_ref.shape[0]
+    part = small[0].shape[0] - height
+    for piece in range(block // part):
+        lanes = slice(piece * LANES, (piece + 1) * LANES)
+        factor = pack(sum(unpack(ref[height:, lanes]) for ref in small))
+        out_ref[piece * part : (piece + 1) * part, width : width + LANES] = factor
     out_ref[block:, : width + LANES] = jnp.zeros((out_ref.shape[0] - block, width + LANES), BF16)
-    total = sum(ref[...].astype(F32) for ref in outs)
+    total = sum(ref[:height, :].astype(F32) for ref in small)
     out_ref[:block, width + LANES :] = total[:block, :].astype(BF16)
-    out_ref[block:, width + LANES :] = three_rows(jnp.sum(total[block:, :], axis=0, keepdims=True))
+    out_ref[block:, width + LANES :] = three_rows(jnp.sum(total[block : block + 16, :], axis=0, keepdims=True))
+    weight_ref[...] = total[block + 16 :, :]
+
+
+def add_body(n, keep_ref, got_ref, *refs):
+    for j, out_ref in enumerate(refs):
+        out_ref[...] = (keep_ref[j + 1].astype(F32) + got_ref[j + 1].astype(F32)).astype(BF16)
 
 
 def final_body(n_var, n_space, scale, me_ref, even_ref, odd_ref, query_ref, wk_ref, kv_ref, gq_ref, out_ref, gain_ref):
@@ -582,19 +614,6 @@
     vmem = pl.BlockSpec(memory_space=pltpu.VMEM)
     packet = width + LANES
 
-    dattn, cot_own, w_heads, *cot_cols = call(
-        functools.partial(early_body, n_space),
-        [struct((rows, group), BF16), struct((block, width), BF16), struct(qkv_weight.shape, BF16)]
-        + [struct((rows, cols), BF16)] * n_space,
-        in_specs=[SMEM] + [vmem] * 3,
-        scratch_shapes=[pltpu.VMEM((n_space, rows, cols), BF16)],
-        limit=LIMITS["early"],
-        cost_estimate=cost(2e8, 4e6),
-        name="early",
-    )(me, cotangent, out_weight, qkv_weight)
-    dattn_all = gather_direct(dattn, "space")
-    cot_all = exchange_direct(cot_cols, "space")
-
     whole = lambda shape: pl.BlockSpec(shape, lambda v: (0,) * len(shape))
     every = lambda shape: pl.BlockSpec((1,) + shape, lambda v: (v,) + (0,) * len(shape))
     n_chip = n_var // 2
@@ -604,7 +623,6 @@
         limit=LIMITS["tokens"],
         grid=(count,),
         in_specs=[
-            SMEM,
             every((rows, pixels)),
             every((pixels, width)),
             whole((count, width)),
@@ -615,7 +633,7 @@
         scratch_shapes=[pltpu.VMEM((width, 3 * LANES), BF16)],
         cost_estimate=cost(6e9, 2e7),
         name="tokens",
-    )(hold(me, dattn), patches, embed_weight, var_embed, query, agg_kv)
+    )(patches, embed_weight, var_embed, query, agg_kv)
     value, keep, send = call(
         functools.partial(forward_body, count),
         [struct((count, rows, width), F32)] + [struct((n_chip, block, packet), F32)] * 2,
@@ -635,7 +653,7 @@
         ],
         cost_estimate=cost(4e9, 1e7),
         name="forward",
-    )(hold(me, scores, *dattn_all[1:], *cot_all[1:]), tokens, scores, agg_kv)
+    )(me, tokens, scores, agg_kv)
 
     def pool_pairs(mine, got):
         return call(
@@ -648,10 +666,22 @@
         )(me, mine, got)
 
     received = exchange_pairs(keep, send, pool_pairs)
+    dattn, cot_own, w_heads = call(
+        early_body,
+        [struct((rows, group), BF16), struct((block, width), BF16), struct(qkv_weight.shape, BF16)],
+        limit=LIMITS["early"],
+        after=[received[0]],
+        in_specs=[SMEM] + [vmem] * 3,
+        cost_estimate=cost(2e8, 4e6),
+        name="early",
+    )(me, cotangent, out_weight, qkv_weight)
+    dattn_all = gather_direct(dattn, "space")
+
     mixed, pooled_packet = call(
         functools.partial(pool_body, n_chip),
         [struct((block, width), F32), struct((block, packet), BF16)],
         limit=LIMITS["pool"],
+        after=dattn_all[1:],
         cost_estimate=cost(1e8, 2e6),
         name="pool",
     )(*received)
@@ -678,24 +708,33 @@
         functools.partial(columns_body, n_space),
         [struct((rows, cols), BF16)] * n_space,
         limit=LIMITS["columns"],
+        after=qkv_all[1:],
         in_specs=[SMEM, vmem],
         scratch_shapes=[pltpu.VMEM((n_space, rows, cols), BF16)],
         cost_estimate=cost(1e6, 1e6),
         name="columns",
-    )(hold(me, *qkv_all[1:]), normed)
+    )(me, normed)
     normed_all = exchange_direct(normed_cols, "space")
-    attn, dqkv, dn_keep, dn_send = call(
+    attn, dqkv = call(
         functools.partial(attention_body, n_space, size, scale),
-        [struct((positions, group), BF16), struct((positions, 3 * group), BF16)]
-        + [struct((n_chip, block, width), BF16)] * 2,
+        [struct((positions, group), BF16), struct((positions, 3 * group), BF16)],
         limit=LIMITS["attention"],
-        in_specs=[SMEM] + [vmem] * (2 * n_space + 1),
-        scratch_shapes=[pltpu.VMEM((positions, group), BF16)] * 2
-        + [pltpu.VMEM((positions, group), F32)] * 2
-        + [pltpu.VMEM((rows, width), BF16)],
+        after=[normed_cols[0]],
+        scratch_shapes=[pltpu.VMEM((positions, group), BF16)] * 2 + [pltpu.VMEM((positions, group), F32)] * 2,
         cost_estimate=cost(6e9, 4e6),
         name="attention",
-    )(hold(me, normed_cols[0]), *qkv_all, *dattn_all, w_heads)
+    )(*qkv_all, *dattn_all)
+    dn_keep, dn_send = call(
+        dn_body,
+        [struct((n_chip, block, width), BF16)] * 2,
+        limit=LIMITS["dn"],
+        after=normed_all[1:],
+        grid=(1,),
+        in_specs=[SMEM, pl.BlockSpec((rows, 3 * group), lambda i: (0, 0)), vmem],
+        scratch_shapes=[pltpu.VMEM((rows, width), BF16)],
+        cost_estimate=cost(2e8, 1e6),
+        name="dn",
+    )(me, dqkv, w_heads)
 
     def dn_pairs(mine, got):
         return call(
@@ -707,7 +746,7 @@
             name="dn_pair",
         )(me, mine, got)
 
-    dn_received = exchange_pairs(dn_keep, dn_send, dn_pairs, normed_all[1:])
+    dn_received = exchange_pairs(dn_keep, dn_send, dn_pairs)
     joined_packet, dgain = call(
         functools.partial(joined_body, n_chip),
         [struct((block, packet), BF16), struct((8, width), F32)],
@@ -717,58 +756,92 @@
     )(*dn_received, centred, inv, gain, cot_own, mixed, agg_out)
     joined_even, joined_odd = gather_pairs(joined_packet, "var")
 
-    d_pooled, stat, *out_blocks = call(
-        functools.partial(out_grad_body, n_space),
-        [struct((rows, width), F32), struct((3, rows, LANES), F32)] + [struct((drows + 16, cols), BF16)] * n_space,
+    d_joined, d_pooled, stat = call(
+        prepare_body,
+        [struct((rows, packet), BF16), struct((rows, width), F32), struct((3, rows, LANES), F32)],
+        limit=LIMITS["prepare"],
+        in_specs=[SMEM] + [vmem] * 4,
+        cost_estimate=cost(6e8, 4e6),
+        name="prepare",
+    )(me, pooled_packets, joined_even, joined_odd, agg_out)
+    d_value, d_logit = call(
+        dvalue_body,
+        [struct((count, rows, width), BF16), struct((count, rows, 2 * LANES), BF16)],
+        limit=LIMITS["dvalue"],
+        grid=(count,),
+        in_specs=[whole((rows, width)), whole((3, rows, LANES)), every((rows, width)), every((rows, LANES))],
+        out_specs=[every((rows, width)), every((rows, 2 * LANES))],
+        scratch_shapes=[pltpu.VMEM((LANES, width), BF16), pltpu.VMEM((width, LANES), BF16)],
+        cost_estimate=cost(4e9, 1e7),
+        name="dvalue",
+    )(d_pooled, stat, value, scores)
+
+    step = max(drows, 256)
+    kv_keep, kv_send = call(
+        value_grad_body,
+        [struct((n_chip, drows, packet), BF16)] * 2,
+        limit=LIMITS["value_grad"],
+        grid=(width // step,),
+        in_specs=[
+            SMEM,
+            pl.BlockSpec((count, rows, step), lambda i: (0, 0, i)),
+            whole((count, rows, width)),
+            whole((count, rows, 2 * LANES)),
+        ],
+        out_specs=[whole((n_chip, drows, packet))] * 2,
+        scratch_shapes=[pltpu.VMEM((step, packet), BF16)],
+        cost_estimate=cost(4e9, 1e7),
+        name="value_grad",
+    )(me, tokens, d_value, d_logit)
+    kv_got = swap(kv_send, "var", 1)
+
+    out_block = call(
+        out_grad_body,
+        struct((n_space, drows + 16 + group, cols), BF16),
         limit=LIMITS["out_grad"],
-        in_specs=[SMEM] + [vmem] * 5,
-        scratch_shapes=[
-            pltpu.VMEM((width, width), F32),
-            pltpu.VMEM((n_space, drows + 16, cols), BF16),
-            pltpu.VMEM((rows, packet), BF16),
-        ],
-        cost_estimate=cost(1e9, 5e6),
+        after=[kv_keep],
+        grid=(1,),
+        in_specs=[SMEM] + [whole(x.shape) for x in (pooled_packets, d_joined, dgain)] + [whole((rows, group)), whole((rows, width))],
+        out_specs=whole((n_space, drows + 16 + group, cols)),
+        scratch_shapes=[pltpu.VMEM((width, width), F32)],
+        cost_estimate=cost(6e8, 3e6),
         name="out_grad",
-    )(me, pooled_packets, joined_even, joined_odd, dgain, agg_out)
-    out_all = exchange_direct(out_blocks, "space")
-
-    def backward(me, start, size_here, work):
-        each = lambda shape: pl.BlockSpec((1,) + shape, lambda v: (v + start,) + (0,) * len(shape))
-        here = lambda shape: pl.BlockSpec((1,) + shape, lambda v: (v,) + (0,) * len(shape))
-        blocks = pl.BlockSpec((n_space // 2, 1, pixels + 16, cols), lambda v: (0, v, 0, 0))
+    )(me, pooled_packets, d_joined, dgain, attn, cotangent)
+
+    def embed(start, here, after):
+        at = lambda shape: pl.BlockSpec((1,) + shape, lambda v: (v + start,) + (0,) * len(shape))
+        half = (n_space // 2, here * pixels + 16, cols)
         return call(
-            functools.partial(backward_body, n_space),
-            [struct((size_here, rows, width), BF16), struct((size_here, rows, 2 * LANES), BF16)]
-            + [struct((n_space // 2, size_here, pixels + 16, cols), BF16)] * 2,
-            limit=LIMITS["backward"],
-            grid=(size_here,),
+            functools.partial(embed_body, n_space),
+            [struct(half, BF16)] * 2,
+            limit=LIMITS["embed"],
+            after=after,
+            grid=(here,),
             in_specs=[
                 SMEM,
-                whole((rows, width)),
-                whole((3, rows, LANES)),
-                each((rows, width)),
-                each((rows, width)),
-                each((rows, LANES)),
-                each((rows, pixels)),
+                at((rows, width)),
+                at((rows, 2 * LANES)),
+                at((rows, pixels)),
                 pl.BlockSpec((width, width), lambda v: (0, 1)),
                 whole((width, LANES)),
             ],
-            out_specs=[here((rows, width)), here((rows, 2 * LANES)), blocks, blocks],
-            scratch_shapes=[
-                pltpu.VMEM((LANES, width), BF16),
-                pltpu.VMEM((width, LANES), BF16),
-                pltpu.VMEM((n_space, pixels + 16, cols), BF16),
-            ],
-            cost_estimate=work,
-            name="backward",
-        )(me, d_pooled, stat, tokens, value, scores, patches, agg_kv, w_back)
-
-    def scatter_embed(keep, arrived, after=()):
-        blocks = {
-            2 * j: (keep[j].astype(F32) + late(arrived[j].astype(F32), *after)).astype(BF16)
-            for j in range(1, n_space // 2)
-        }
-        sums = list(blocks.values())
+            out_specs=[whole(half)] * 2,
+            scratch_shapes=[pltpu.VMEM((n_space, pixels, cols), BF16), pltpu.VMEM((16, width), F32)],
+            cost_estimate=cost(1.5e9, 4e6),
+            name="embed",
+        )(me, d_value, d_logit, patches, agg_kv, w_back)
+
+    def scatter_embed(keep, arrived, after):
+        n = n_space // 2 - 1
+        sums = call(
+            functools.partial(add_body, n),
+            [struct(keep.shape[1:], BF16)] * n,
+            limit=LIMITS["add"],
+            after=after,
+            cost_estimate=cost(1e6, 1e6),
+            name="add",
+        )(keep, arrived)
+        blocks = {2 * (j + 1): sums[j] for j in range(n)}
         mine, bit = [keep, arrived], 2
         while bit < n_space:
             got = {k ^ bit: swap(blocks[k], "space", bit) for k in blocks if k & bit and k % bit == 0}
@@ -777,29 +850,14 @@
                 if k:
                     blocks[k] = (blocks[k].astype(F32) + got[k].astype(F32)).astype(BF16)
             bit *= 2
-        return mine, sums
-
-    first = count // 3
-    dv0, dl0, keep0, send0 = backward(me, 0, first, cost(4e9, 1e7))
-    dv1, dl1, keep1, send1 = backward(hold(me, dv0), first, count - first, cost(1e6, 1e6))
-    mine0, sums0 = scatter_embed(keep0, swap(send0, "space", 1))
+        return mine, list(sums)
+
+    half = count // 2
+    keep0, send0 = embed(0, half, [kv_keep])
+    arrived0 = swap(send0, "space", 1)
+    keep1, send1 = embed(half, count - half, [])
     arrived1 = swap(send1, "space", 1)
 
-    step = max(drows, 256)
-    d_values, d_logits = (dv0, dv1), (dl0, dl1)
-    kv_keep, kv_send = call(
-        functools.partial(value_grad_body, len(d_values)),
-        [struct((n_chip, drows, packet), BF16)] * 2,
-        limit=LIMITS["value_grad"],
-        grid=(width // step,),
-        in_specs=[SMEM, pl.BlockSpec((count, rows, step), lambda i: (0, 0, i))]
-        + [whole(x.shape) for x in d_values + d_logits],
-        out_specs=[whole((n_chip, drows, packet))] * 2,
-        scratch_shapes=[pltpu.VMEM((step, packet), BF16)],
-        cost_estimate=cost(1e6, 1e6),
-        name="value_grad",
-    )(hold(me, dv1, *sums0), tokens, *d_values, *d_logits)
-    kv_got = swap(kv_send, "var", 1)
     kv_blocks = call(
         functools.partial(pair_sum_body, n_chip),
         [struct((drows, packet), BF16)] * n_chip,
@@ -809,38 +867,51 @@
         name="pair_sum",
     )(me, kv_keep, kv_got)
     kv_parts = [kv_blocks[0]] + [swap(kv_blocks[k], "var", 2 * k) for k in range(1, n_chip)]
-    small, *large = call(
+    mine0, sums0 = scatter_embed(keep0, arrived0, [kv_parts[-1]])
+    height = drows + 16 + group
+    part = drows * LANES // cols
+    pieces = call(
         functools.partial(packet_split_body, n_chip, n_space),
-        [struct((drows, LANES), BF16)] + [struct((drows, kv_cols), BF16)] * n_space,
+        [struct((height + part, cols), BF16)] * n_space + [struct((drows, kv_cols), BF16)] * n_space,
         limit=LIMITS["packet_split"],
-        in_specs=[SMEM] + [vmem] * n_chip,
+        after=sums0,
+        in_specs=[SMEM] + [vmem] * (n_chip + 1),
         scratch_shapes=[pltpu.VMEM((n_space // 2, drows, kv_cols), BF16)],
         cost_estimate=cost(1e6, 1e6),
         name="packet_split",
-    )(hold(me, kv_parts[-1], *mine0[2:]), *kv_parts)
-    grad_qkv, grad_out = call(
+    )(me, *kv_parts, out_block)
+    small, large = pieces[:n_space], pieces[n_space:]
+    mine1, sums1 = scatter_embed(keep1, arrived1, [small[0]])
+    grad_qkv, head_flag = call(
         functools.partial(head_grads_body, n_space),
-        [struct((cols, 3 * group), F32), struct((group, cols), F32)],
+        [struct((cols, 3 * group), F32), struct((8, LANES), F32)],
         limit=LIMITS["head_grads"],
         cost_estimate=cost(1e9, 3e6),
         name="head_grads",
-    )(*normed_all, *cot_all, dqkv, attn)
-
-    mine1, sums1 = scatter_embed(keep1, arrived1, [small])
-    small_all = gather_direct(small, "space")
+    )(*normed_all, dqkv)
+    small_all = exchange_direct(small, "space")
     large_all = [large[0]] + [
         swap(large[k], "space", k, lambda target: target >= n_space // 2) for k in range(1, n_space)
     ]
-    kv_sum = call(
+    kv_sum, grad_out = call(
         functools.partial(space_sum_body, n_space),
-        struct((drows + 16, kv_cols + LANES + cols), BF16),
+        [struct((drows + 16, kv_cols + LANES + cols), BF16), struct((group, cols), F32)],
         limit=LIMITS["space_sum"],
-        in_specs=[SMEM] + [vmem] * (3 * n_space),
+        after=mine0[2:] + sums1 + [head_flag],
         cost_estimate=cost(1e6, 1e6),
         name="space_sum",
-    )(hold(me, large_all[-1], grad_out, *sums1, *mine0[2:]), *small_all, *large_all, *out_all)
-
-    kv_even, kv_odd = gather_pairs(kv_sum, "var", mine1[2:])
+    )(*small_all, *large_all)
+
+    def stack(parts):
+        return call(
+            stack_body,
+            struct((len(parts),) + parts[0].shape, BF16),
+            after=mine1[2:],
+            cost_estimate=cost(1e6, 1e6),
+            name="stack",
+        )(*parts)
+
+    kv_even, kv_odd = gather_pairs(kv_sum, "var", stack)
     grad_agg_kv, grad_query, grad_agg_out, grad_gain = call(
         functools.partial(final_body, n_var, n_space, scale),
         [struct((width, kv_cols), F32), struct((1, cols), F32)] + [struct((width, cols), F32), struct((1, cols), F32)],
@@ -852,9 +923,9 @@
     )(me, kv_even, kv_odd, query, agg_kv)
 
     def first_block(x):
-        if x.ndim == 4:
-            return pl.BlockSpec((1,) + x.shape[1:], lambda i: (0, 0, 0, 0))
-        return pl.BlockSpec(x.shape, lambda i: (0, 0, 0))
+        if x.ndim == 3:
+            return pl.BlockSpec((1,) + x.shape[1:], lambda i: (0, 0, 0))
+        return pl.BlockSpec(x.shape, lambda i: (0, 0))
 
     grad_embed, grad_var_embed = call(
         functools.partial(embed_final_body, len(mine0)),

time: 288 us -> 227 us (0.79)
  the two profiles are of different devices: /device:TPU:0 before, /device:TPU:17 now
where the time goes in v4:
time: 227 us; the launch traced here: 226 us
  waiting for transfers between devices  93.6 us (41%)
  Pallas kernels  70.1 us (31%)
  starting transfers between devices  59.7 us (26%)
    ppermute x43, waiting for transfers between devices, swap(): return lax.ppermute(x, axis, pairs)  93.6 us
    pallas_call x26, Pallas kernels, run(): pl.pallas_call(lambda *refs: body(*refs[:n], *refs[n + m:]), out_shape=ou...  70.1 us
    ppermute x43, starting transfers between devices, swap(): return lax.ppermute(x, axis, pairs)  59.7 us
  transfers between devices with their start and end apart: 43, of which 25 were waited for; matrix products, arithmetic and copies ran while one was open for 0% of the time, Pallas kernels for 13%

profile of v4, /device:TPU:17, one launch (start us, length us, event | category | flops | bytes accessed | tf_op | source)
XLA Modules:
  0.0 226.3 jit_solution(8194967710491550483)
XLA Ops:
  1.2 9.1 %tokens.1 = (bf16[6,256,1024]{2,1,0:T(8,128)(2,1)}, f32[6,256,128]{2,1,0:T(8,128)}, bf16[1024,128]{1,0:T(8,128)(2,1)}) custom-call(bf16[6,256,256]{2,1,0:T(8,128)(2,1)} %refs_3_.9, bf16[6,256,1024]{2,1,0:T(8,128)(2,1)} %refs_1_.2, f32[6,1024]{1,0:T(8,128)} %refs_2_.2, f32[1,1024]{1,0:T(1,128)} %bitcast.18, bf16[1024,2048]{1,0:T(8,128)(2,1)} %refs_4_.9), custom_call_target="tpu_custom_call" | custom-call | flops 6000000000 | bytes 20000000 | tf_op jit(solution)/shard_map/tokens/pallas_call | solution.py:84
  10.3 10.5 %forward.1 = (f32[6,256,1024]{2,1,0:T(8,128)}, f32[4,32,1152]{2,1,0:T(8,128)}, f32[4,32,1152]{2,1,0:T(8,128)}) custom-call(s32[2]{0:T(128)} %pad_add_fusion.refs_0_, bf16[6,256,1024]{2,1,0:T(8,128)(2,1)} %get-tuple-element.75.refs_1_, f32[6,256,128]{2,1,0:T(8,128)} %get-tuple-element.76.refs_2_.refs_3_, bf16[1024,2048]{1,0:T(8,128)(2,1)} %refs_4_.9), custom_call_target="tpu_custom_call" | custom-call | flops 4000000000 | bytes 10000000 | tf_op jit(solution)/shard_map/forward/pallas_call | solution.py:84
  21.5 1.8 collective-permute-done.refs_2_
  29.7 3.2 %collective-permute-start.5 = (bf16[256,128]{1,0:T(8,128)(2,1)S(1)}, bf16[256,128]{1,0:T(8,128)(2,1)S(1)}, u32[]{:S(2)}, u32[]{:S(2)}) collective-permute-start(bf16[256,128]{1,0:T(8,128)(2,1)S(1)} %get-tuple-element.83.refs_4_), channel_id=1, source_target_pairs={{0,2},{1,3},{2,0},{3,1},{4,6},{5,7},{6,4},{7,5},{8,10},{9,11},{10,... | collective-permute-start | bytes 196616 | tf_op jit(solution)/shard_map/ppermute | solution.py:110
  32.9 2.9 %collective-permute-start.4 = (bf16[256,128]{1,0:T(8,128)(2,1)S(1)}, bf16[256,128]{1,0:T(8,128)(2,1)S(1)}, u32[]{:S(2)}, u32[]{:S(2)}) collective-permute-start(bf16[256,128]{1,0:T(8,128)(2,1)S(1)} %get-tuple-element.83.refs_4_), channel_id=1, source_target_pairs={{0,1},{1,0},{2,3},{3,2},{4,5},{5,4},{6,7},{7,6},{8,9},{9,8},{10,11... | collective-permute-start | bytes 196616 | tf_op jit(solution)/shard_map/ppermute | solution.py:110
  35.8 1.9 collective-permute-done.4.refs_4_.refs_5_
  38.1 2.2 collective-permute-start.9
  43.8 5.3 %collective-permute-start.10 = (bf16[4,32,1152]{2,1,0:T(8,128)(2,1)S(1)}, bf16[4,32,1152]{2,1,0:T(8,128)(2,1)S(1)}, u32[]{:S(2)}, u32[]{:S(2)}) collective-permute-start(bf16[4,32,1152]{2,1,0:T(8,128)(2,1)S(1)} %pad_maximum_fusion.refs_1_), channel_id=1, source_target_pairs={{0,4},{4,0},{8,12},{12,8},{16,20},{20,16},{24,28},{28,24},{1,5},{5... | collective-permute-start | bytes 884744 | tf_op jit(solution)/shard_map/ppermute | solution.py:110
  50.3 2.0 norm.1
  52.3 3.8 %collective-permute-start.12 = (bf16[256,384]{1,0:T(8,128)(2,1)S(1)}, bf16[256,384]{1,0:T(8,128)(2,1)S(1)}, u32[]{:S(2)}, u32[]{:S(2)}) collective-permute-start(bf16[256,384]{1,0:T(8,128)(2,1)S(1)} %get-tuple-element.87.refs_0_), channel_id=1, source_target_pairs={{0,2},{1,3},{2,0},{3,1},{4,6},{5,7},{6,4},{7,5},{8,10},{9,11},{10,... | collective-permute-start | bytes 589832 | tf_op jit(solution)/shard_map/ppermute | solution.py:110
  56.2 10.7 %collective-permute-done.13.refs_4_.refs_3_ = bf16[256,384]{1,0:T(8,128)(2,1)S(1)} collective-permute-done((bf16[256,384]{1,0:T(8,128)(2,1)S(1)}, bf16[256,384]{1,0:T(8,128)(2,1)S(1)}, u32[]{:S(2)}, u32[]{:S(2)}) %collective-permute-start.13) | collective-permute-done | bytes 196640 | tf_op jit(solution)/shard_map/ppermute | solution.py:110
  66.9 2.3 %collective-permute-done.12.refs_3_.refs_2_ = bf16[256,384]{1,0:T(8,128)(2,1)S(1)} collective-permute-done((bf16[256,384]{1,0:T(8,128)(2,1)S(1)}, bf16[256,384]{1,0:T(8,128)(2,1)S(1)}, u32[]{:S(2)}, u32[]{:S(2)}) %collective-permute-start.12) | collective-permute-done | bytes 196640 | tf_op jit(solution)/shard_map/ppermute | solution.py:110
  69.8 3.1 %collective-permute-start.14 = (bf16[256,256]{1,0:T(8,128)(2,1)S(1)}, bf16[256,256]{1,0:T(8,128)(2,1)S(1)}, u32[]{:S(2)}, u32[]{:S(2)}) collective-permute-start(bf16[256,256]{1,0:T(8,128)(2,1)S(1)} %get-tuple-element.91), channel_id=1, source_target_pairs={{0,1},{1,0},{2,3},{3,2},{4,5},{5,4},{6,7},{7,6},{8,9},{9,8},{10,11... | collective-permute-start | bytes 393224 | tf_op jit(solution)/shard_map/ppermute | solution.py:110
  74.2 11.4 %attention.1 = (bf16[1024,128]{1,0:T(8,128)(2,1)S(1)}, bf16[1024,384]{1,0:T(8,128)(2,1)S(1)}) custom-call(bf16[256,384]{1,0:T(8,128)(2,1)S(1)} %get-tuple-element.87.refs_0_, bf16[256,384]{1,0:T(8,128)(2,1)S(1)} %collective-permute-done.11.refs_2_.refs_1_, bf16[256,384]{1,0:T(8,128)(2,1)S(1)} %collective-permute-done.12.refs_3_.refs_2_, ...), custom_call_target="tpu_custom_call" | custom-call | flops 6000000000 | bytes 4000000 | tf_op jit(solution)/shard_map/attention/pallas_call | solution.py:84
  94.1 1.9 collective-permute-done.20.refs_3_
  103.6 2.9 %collective-permute-start.24 = (bf16[4,32,1152]{2,1,0:T(8,128)(2,1)S(1)}, bf16[4,32,1152]{2,1,0:T(8,128)(2,1)S(1)}, u32[]{:S(2)}, u32[]{:S(2)}) collective-permute-start(bf16[4,32,1152]{2,1,0:T(8,128)(2,1)S(1)} %pad_maximum_fusion.1.refs_2_), channel_id=1, source_target_pairs={{0,4},{4,0},{8,12},{12,8},{16,20},{20,16},{24,28},{28,24},{1,5},{5... | collective-permute-start | bytes 884744 | tf_op jit(solution)/shard_map/ppermute | solution.py:110
  109.1 5.1 %dvalue.1 = (bf16[6,256,1024]{2,1,0:T(8,128)(2,1)S(1)}, bf16[6,256,256]{2,1,0:T(8,128)(2,1)S(1)}) custom-call(f32[256,1024]{1,0:T(8,128)S(1)} %get-tuple-element.105.refs_0_, f32[3,256,128]{2,1,0:T(8,128)S(1)} %get-tuple-element.106.refs_1_, f32[6,256,1024]{2,1,0:T(8,128)S(1)} %bitcast.21, f32[6,256,128]{2,1,0:T(8,128)S(1)} %copy-done.12), custom_call_target="tpu_custom_call" | custom-call | flops 4000000000 | bytes 10000000 | tf_op jit(solution)/shard_map/dvalue/pallas_call | solution.py:84
  114.3 6.1 %value_grad.1 = (bf16[4,128,1152]{2,1,0:T(8,128)(2,1)S(1)}, bf16[4,128,1152]{2,1,0:T(8,128)(2,1)S(1)}) custom-call(s32[2]{0:T(128)S(1)} %copy-done.8, bf16[6,256,1024]{2,1,0:T(8,128)(2,1)S(1)} %copy-done.11, bf16[6,256,1024]{2,1,0:T(8,128)(2,1)S(1)} %get-tuple-element.108.refs_2_.refs_1_, bf16[6,256,256]{2,1,0:T(8,128)(2,1)S(1)} %get-tuple-element.109.refs_3_.refs_2_), custom_call_target="tpu_custom_call" | custom-call | flops 4000000000 | bytes 10000000 | tf_op jit(solution)/shard_map/value_grad/pallas_call | solution.py:84
  120.8 4.1 %embed.2 = (bf16[2,784,256]{2,1,0:T(8,128)(2,1)S(1)}, bf16[2,784,256]{2,1,0:T(8,128)(2,1)S(1)}) custom-call(s32[2]{0:T(128)S(1)} %copy-done.8, bf16[6,256,1024]{2,1,0:T(8,128)(2,1)S(1)} %get-tuple-element.108.refs_2_.refs_1_, bf16[6,256,256]{2,1,0:T(8,128)(2,1)S(1)} %get-tuple-element.109.refs_3_.refs_2_, bf16[6,256,256]{2,1,0:T(8,128)(2,1)S(1)} %copy-done.2, ...), custom_call_target="tpu_custom_call" | custom-call | flops 1500000000 | bytes 4000000 | tf_op jit(solution)/shard_map/embed/pallas_call | solution.py:84
  124.9 2.6 %collective-permute-start.25 = (bf16[2,784,256]{2,1,0:T(8,128)(2,1)S(1)}, bf16[2,784,256]{2,1,0:T(8,128)(2,1)S(1)}, u32[]{:S(2)}, u32[]{:S(2)}) collective-permute-start(bf16[2,784,256]{2,1,0:T(8,128)(2,1)S(1)} %get-tuple-element.113), channel_id=1, source_target_pairs={{0,1},{1,0},{2,3},{3,2},{4,5},{5,4},{6,7},{7,6},{8,9},{9,8},{10,11... | collective-permute-start | bytes 2408456 | tf_op jit(solution)/shard_map/ppermute | solution.py:110
  127.5 4.1 %embed.3 = (bf16[2,784,256]{2,1,0:T(8,128)(2,1)S(1)}, bf16[2,784,256]{2,1,0:T(8,128)(2,1)S(1)}) custom-call(s32[2]{0:T(128)S(1)} %copy-done.8, bf16[6,256,1024]{2,1,0:T(8,128)(2,1)S(1)} %get-tuple-element.108.refs_2_.refs_1_, bf16[6,256,256]{2,1,0:T(8,128)(2,1)S(1)} %get-tuple-element.109.refs_3_.refs_2_, bf16[6,256,256]{2,1,0:T(8,128)(2,1)S(1)} %copy-done.2, ...), custom_call_target="tpu_custom_call" | custom-call | flops 1500000000 | bytes 4000000 | tf_op jit(solution)/shard_map/embed/pallas_call | solution.py:84
  135.5 10.2 %collective-permute-done.25.refs_1_ = bf16[2,784,256]{2,1,0:T(8,128)(2,1)S(1)} collective-permute-done((bf16[2,784,256]{2,1,0:T(8,128)(2,1)S(1)}, bf16[2,784,256]{2,1,0:T(8,128)(2,1)S(1)}, u32[]{:S(2)}, u32[]{:S(2)}) %collective-permute-start.25) | collective-permute-done | bytes 802848 | tf_op jit(solution)/shard_map/ppermute | solution.py:110
  149.9 3.3 %collective-permute-start.36 = (bf16[128,512]{1,0:T(8,128)(2,1)S(1)}, bf16[128,512]{1,0:T(8,128)(2,1)S(1)}, u32[]{:S(2)}, u32[]{:S(2)}) collective-permute-start(bf16[128,512]{1,0:T(8,128)(2,1)S(1)} %get-tuple-element.131), channel_id=1, source_target_pairs={{2,3},{3,2},{6,7},{7,6},{10,11},{11,10},{14,15},{15,14},{18,19},{1... | collective-permute-start | bytes 393224 | tf_op jit(solution)/shard_map/ppermute | solution.py:110
  156.1 17.1 %collective-permute-done.29.refs_1_.refs_4_ = bf16[2,784,256]{2,1,0:T(8,128)(2,1)S(1)} collective-permute-done((bf16[2,784,256]{2,1,0:T(8,128)(2,1)S(1)}, bf16[2,784,256]{2,1,0:T(8,128)(2,1)S(1)}, u32[]{:S(2)}, u32[]{:S(2)}) %collective-permute-start.29) | collective-permute-done | bytes 802848 | tf_op jit(solution)/shard_map/ppermute | solution.py:110
  173.2 2.3 %collective-permute-start.33 = (bf16[336,256]{1,0:T(8,128)(2,1)S(1)}, bf16[336,256]{1,0:T(8,128)(2,1)S(1)}, u32[]{:S(2)}, u32[]{:S(2)}) collective-permute-start(bf16[336,256]{1,0:T(8,128)(2,1)S(1)} %get-tuple-element.127), channel_id=1, source_target_pairs={{0,1},{1,0},{2,3},{3,2},{4,5},{5,4},{6,7},{7,6},{8,9},{9,8},{10,11... | collective-permute-start | bytes 516104 | tf_op jit(solution)/shard_map/ppermute | solution.py:110
  175.6 3.3 %collective-permute-done.36.refs_5_ = bf16[128,512]{1,0:T(8,128)(2,1)S(1)} collective-permute-done((bf16[128,512]{1,0:T(8,128)(2,1)S(1)}, bf16[128,512]{1,0:T(8,128)(2,1)S(1)}, u32[]{:S(2)}, u32[]{:S(2)}) %collective-permute-start.36) | collective-permute-done | bytes 131104 | tf_op jit(solution)/shard_map/ppermute | solution.py:110
  178.9 3.4 %collective-permute-start.35 = (bf16[336,256]{1,0:T(8,128)(2,1)S(1)}, bf16[336,256]{1,0:T(8,128)(2,1)S(1)}, u32[]{:S(2)}, u32[]{:S(2)}) collective-permute-start(bf16[336,256]{1,0:T(8,128)(2,1)S(1)} %get-tuple-element.129), channel_id=1, source_target_pairs={{0,3},{1,2},{2,1},{3,0},{4,7},{5,6},{6,5},{7,4},{8,11},{9,10},{10,... | collective-permute-start | bytes 516104 | tf_op jit(solution)/shard_map/ppermute | solution.py:110
  183.3 1.8 head_grads.1
  185.2 20.6 %collective-permute-done.35.refs_3_ = bf16[336,256]{1,0:T(8,128)(2,1)S(1)} collective-permute-done((bf16[336,256]{1,0:T(8,128)(2,1)S(1)}, bf16[336,256]{1,0:T(8,128)(2,1)S(1)}, u32[]{:S(2)}, u32[]{:S(2)}) %collective-permute-start.35) | collective-permute-done | bytes 172064 | tf_op jit(solution)/shard_map/ppermute | solution.py:110
  210.4 4.5 %collective-permute-done.41.refs_3_ = bf16[144,896]{1,0:T(8,128)(2,1)S(1)} collective-permute-done((bf16[144,896]{1,0:T(8,128)(2,1)S(1)}, bf16[144,896]{1,0:T(8,128)(2,1)S(1)}, u32[]{:S(2)}, u32[]{:S(2)}) %collective-permute-start.41) | collective-permute-done | bytes 258080 | tf_op jit(solution)/shard_map/ppermute | solution.py:110
  214.9 5.0 %collective-permute-done.40.refs_2_ = bf16[144,896]{1,0:T(8,128)(2,1)S(1)} collective-permute-done((bf16[144,896]{1,0:T(8,128)(2,1)S(1)}, bf16[144,896]{1,0:T(8,128)(2,1)S(1)}, u32[]{:S(2)}, u32[]{:S(2)}) %collective-permute-start.40) | collective-permute-done | bytes 258080 | tf_op jit(solution)/shard_map/ppermute | solution.py:110
  223.5 2.8 %final.1 = (f32[1024,512]{1,0:T(8,128)}, f32[1,256]{1,0:T(1,128)}, f32[1024,256]{1,0:T(8,128)}, f32[1,256]{1,0:T(1,128)}) custom-call(s32[2]{0:T(128)S(1)} %copy-done.8, bf16[4,144,896]{2,1,0:T(8,128)(2,1)S(1)} %stack.53.refs_1_, bf16[4,144,896]{2,1,0:T(8,128)(2,1)S(1)} %collective-permute-done.42.refs_2_, f32[1,1024]{1,0:T(1,128)S(1)} %bitcast.19, ...), custom_call_target="tpu_custom_call" | custom-call | flops 200000000 | bytes 5000000 | tf_op jit(solution)/shard_map/final/pallas_call | solution.py:84
  (114 shorter events, 53.7 us)
Async XLA Ops:
  25.4 12.4 %collective-permute-start.1 = (f32[32,1152]{1,0:T(8,128)S(1)}, f32[32,1152]{1,0:T(8,128)S(1)}, u32[]{:S(2)}, u32[]{:S(2)}) collective-permute-start(f32[32,1152]{1,0:T(8,128)S(1)} %get-tuple-element.80), channel_id=1, source_target_pairs={{0,8},{4,12},{8,0},{12,4},{16,24},{20,28},{24,16},{28,20},{1,9},{5... | collective-permute-start | bytes 442376 | tf_op jit(solution)/shard_map/ppermute | solution.py:110
  26.6 11.1 %collective-permute-start.2 = (f32[32,1152]{1,0:T(8,128)S(1)}, f32[32,1152]{1,0:T(8,128)S(1)}, u32[]{:S(2)}, u32[]{:S(2)}) collective-permute-start(f32[32,1152]{1,0:T(8,128)S(1)} %get-tuple-element.81), channel_id=1, source_target_pairs={{0,16},{4,20},{8,24},{12,28},{16,0},{20,4},{24,8},{28,12},{1,17},{... | collective-permute-start | bytes 442376 | tf_op jit(solution)/shard_map/ppermute | solution.py:110
  27.9 9.9 %collective-permute-start.3 = (f32[32,1152]{1,0:T(8,128)S(1)}, f32[32,1152]{1,0:T(8,128)S(1)}, u32[]{:S(2)}, u32[]{:S(2)}) collective-permute-start(f32[32,1152]{1,0:T(8,128)S(1)} %get-tuple-element.82), channel_id=1, source_target_pairs={{0,24},{4,28},{8,16},{12,20},{16,8},{20,12},{24,0},{28,4},{1,25},{... | collective-permute-start | bytes 442376 | tf_op jit(solution)/shard_map/ppermute | solution.py:110
  29.7 6.1 %collective-permute-start.5 = (bf16[256,128]{1,0:T(8,128)(2,1)S(1)}, bf16[256,128]{1,0:T(8,128)(2,1)S(1)}, u32[]{:S(2)}, u32[]{:S(2)}) collective-permute-start(bf16[256,128]{1,0:T(8,128)(2,1)S(1)} %get-tuple-element.83.refs_4_), channel_id=1, source_target_pairs={{0,2},{1,3},{2,0},{3,1},{4,6},{5,7},{6,4},{7,5},{8,10},{9,11},{10,... | collective-permute-start | bytes 196616 | tf_op jit(solution)/shard_map/ppermute | solution.py:110
  32.9 4.8 %collective-permute-start.4 = (bf16[256,128]{1,0:T(8,128)(2,1)S(1)}, bf16[256,128]{1,0:T(8,128)(2,1)S(1)}, u32[]{:S(2)}, u32[]{:S(2)}) collective-permute-start(bf16[256,128]{1,0:T(8,128)(2,1)S(1)} %get-tuple-element.83.refs_4_), channel_id=1, source_target_pairs={{0,1},{1,0},{2,3},{3,2},{4,5},{5,4},{6,7},{7,6},{8,9},{9,8},{10,11... | collective-permute-start | bytes 196616 | tf_op jit(solution)/shard_map/ppermute | solution.py:110
  38.1 4.2 %collective-permute-start.9 = (bf16[32,1152]{1,0:T(8,128)(2,1)S(1)}, bf16[32,1152]{1,0:T(8,128)(2,1)S(1)}, u32[]{:S(2)}, u32[]{:S(2)}) collective-permute-start(bf16[32,1152]{1,0:T(8,128)(2,1)S(1)} %get-tuple-element.84), channel_id=1, source_target_pairs={{0,24},{4,28},{8,16},{12,20},{16,8},{20,12},{24,0},{28,4},{1,25},{... | collective-permute-start | bytes 221192 | tf_op jit(solution)/shard_map/ppermute | solution.py:110
  43.8 6.5 %collective-permute-start.10 = (bf16[4,32,1152]{2,1,0:T(8,128)(2,1)S(1)}, bf16[4,32,1152]{2,1,0:T(8,128)(2,1)S(1)}, u32[]{:S(2)}, u32[]{:S(2)}) collective-permute-start(bf16[4,32,1152]{2,1,0:T(8,128)(2,1)S(1)} %pad_maximum_fusion.refs_1_), channel_id=1, source_target_pairs={{0,4},{4,0},{8,12},{12,8},{16,20},{20,16},{24,28},{28,24},{1,5},{5... | collective-permute-start | bytes 884744 | tf_op jit(solution)/shard_map/ppermute | solution.py:110
  52.3 14.6 %collective-permute-start.13 = (bf16[256,384]{1,0:T(8,128)(2,1)S(1)}, bf16[256,384]{1,0:T(8,128)(2,1)S(1)}, u32[]{:S(2)}, u32[]{:S(2)}) collective-permute-start(bf16[256,384]{1,0:T(8,128)(2,1)S(1)} %get-tuple-element.87.refs_0_), channel_id=1, source_target_pairs={{0,3},{1,2},{2,1},{3,0},{4,7},{5,6},{6,5},{7,4},{8,11},{9,10},{10,... | collective-permute-start | bytes 589832 | tf_op jit(solution)/shard_map/ppermute | solution.py:110
  52.3 16.9 %collective-permute-start.12 = (bf16[256,384]{1,0:T(8,128)(2,1)S(1)}, bf16[256,384]{1,0:T(8,128)(2,1)S(1)}, u32[]{:S(2)}, u32[]{:S(2)}) collective-permute-start(bf16[256,384]{1,0:T(8,128)(2,1)S(1)} %get-tuple-element.87.refs_0_), channel_id=1, source_target_pairs={{0,2},{1,3},{2,0},{3,1},{4,6},{5,7},{6,4},{7,5},{8,10},{9,11},{10,... | collective-permute-start | bytes 589832 | tf_op jit(solution)/shard_map/ppermute | solution.py:110
  56.2 13.1 %collective-permute-start.11 = (bf16[256,384]{1,0:T(8,128)(2,1)S(1)}, bf16[256,384]{1,0:T(8,128)(2,1)S(1)}, u32[]{:S(2)}, u32[]{:S(2)}) collective-permute-start(bf16[256,384]{1,0:T(8,128)(2,1)S(1)} %get-tuple-element.87.refs_0_), channel_id=1, source_target_pairs={{0,1},{1,0},{2,3},{3,2},{4,5},{5,4},{6,7},{7,6},{8,9},{9,8},{10,11... | collective-permute-start | bytes 589832 | tf_op jit(solution)/shard_map/ppermute | solution.py:110
  69.8 15.8 %collective-permute-start.14 = (bf16[256,256]{1,0:T(8,128)(2,1)S(1)}, bf16[256,256]{1,0:T(8,128)(2,1)S(1)}, u32[]{:S(2)}, u32[]{:S(2)}) collective-permute-start(bf16[256,256]{1,0:T(8,128)(2,1)S(1)} %get-tuple-element.91), channel_id=1, source_target_pairs={{0,1},{1,0},{2,3},{3,2},{4,5},{5,4},{6,7},{7,6},{8,9},{9,8},{10,11... | collective-permute-start | bytes 393224 | tf_op jit(solution)/shard_map/ppermute | solution.py:110
  73.0 12.7 %collective-permute-start.15 = (bf16[256,256]{1,0:T(8,128)(2,1)S(1)}, bf16[256,256]{1,0:T(8,128)(2,1)S(1)}, u32[]{:S(2)}, u32[]{:S(2)}) collective-permute-start(bf16[256,256]{1,0:T(8,128)(2,1)S(1)} %get-tuple-element.92), channel_id=1, source_target_pairs={{0,2},{1,3},{2,0},{3,1},{4,6},{5,7},{6,4},{7,5},{8,10},{9,11},{10,... | collective-permute-start | bytes 393224 | tf_op jit(solution)/shard_map/ppermute | solution.py:110
  73.1 12.6 %collective-permute-start.16 = (bf16[256,256]{1,0:T(8,128)(2,1)S(1)}, bf16[256,256]{1,0:T(8,128)(2,1)S(1)}, u32[]{:S(2)}, u32[]{:S(2)}) collective-permute-start(bf16[256,256]{1,0:T(8,128)(2,1)S(1)} %get-tuple-element.93), channel_id=1, source_target_pairs={{0,3},{1,2},{2,1},{3,0},{4,7},{5,6},{6,5},{7,4},{8,11},{9,10},{10,... | collective-permute-start | bytes 393224 | tf_op jit(solution)/shard_map/ppermute | solution.py:110
  97.0 4.2 %collective-permute-start.23 = (bf16[32,1152]{1,0:T(8,128)(2,1)S(1)}, bf16[32,1152]{1,0:T(8,128)(2,1)S(1)}, u32[]{:S(2)}, u32[]{:S(2)}) collective-permute-start(bf16[32,1152]{1,0:T(8,128)(2,1)S(1)} %get-tuple-element.104), channel_id=1, source_target_pairs={{0,24},{4,28},{8,16},{12,20},{16,8},{20,12},{24,0},{28,4},{1,25},{... | collective-permute-start | bytes 221192 | tf_op jit(solution)/shard_map/ppermute | solution.py:110
  99.4 4.2 %collective-permute-start.21 = (bf16[32,1152]{1,0:T(8,128)(2,1)S(1)}, bf16[32,1152]{1,0:T(8,128)(2,1)S(1)}, u32[]{:S(2)}, u32[]{:S(2)}) collective-permute-start(bf16[32,1152]{1,0:T(8,128)(2,1)S(1)} %get-tuple-element.104), channel_id=1, source_target_pairs={{0,8},{4,12},{8,0},{12,4},{16,24},{20,28},{24,16},{28,20},{1,9},{5... | collective-permute-start | bytes 221192 | tf_op jit(solution)/shard_map/ppermute | solution.py:110
  120.4 11.3 %collective-permute-start.26 = (bf16[4,128,1152]{2,1,0:T(8,128)(2,1)S(1)}, bf16[4,128,1152]{2,1,0:T(8,128)(2,1)S(1)}, u32[]{:S(2)}, u32[]{:S(2)}) collective-permute-start(bf16[4,128,1152]{2,1,0:T(8,128)(2,1)S(1)} %get-tuple-element.114), channel_id=1, source_target_pairs={{0,4},{4,0},{8,12},{12,8},{16,20},{20,16},{24,28},{28,24},{1,5},{5... | collective-permute-start | bytes 3538952 | tf_op jit(solution)/shard_map/ppermute | solution.py:110
  124.9 20.8 %collective-permute-start.25 = (bf16[2,784,256]{2,1,0:T(8,128)(2,1)S(1)}, bf16[2,784,256]{2,1,0:T(8,128)(2,1)S(1)}, u32[]{:S(2)}, u32[]{:S(2)}) collective-permute-start(bf16[2,784,256]{2,1,0:T(8,128)(2,1)S(1)} %get-tuple-element.113), channel_id=1, source_target_pairs={{0,1},{1,0},{2,3},{3,2},{4,5},{5,4},{6,7},{7,6},{8,9},{9,8},{10,11... | collective-permute-start | bytes 2408456 | tf_op jit(solution)/shard_map/ppermute | solution.py:110
  131.6 41.7 %collective-permute-start.29 = (bf16[2,784,256]{2,1,0:T(8,128)(2,1)S(1)}, bf16[2,784,256]{2,1,0:T(8,128)(2,1)S(1)}, u32[]{:S(2)}, u32[]{:S(2)}) collective-permute-start(bf16[2,784,256]{2,1,0:T(8,128)(2,1)S(1)} %get-tuple-element.117), channel_id=1, source_target_pairs={{0,1},{1,0},{2,3},{3,2},{4,5},{5,4},{6,7},{7,6},{8,9},{9,8},{10,11... | collective-permute-start | bytes 2408456 | tf_op jit(solution)/shard_map/ppermute | solution.py:110
  132.8 12.9 %collective-permute-start.27 = (bf16[128,1152]{1,0:T(8,128)(2,1)S(1)}, bf16[128,1152]{1,0:T(8,128)(2,1)S(1)}, u32[]{:S(2)}, u32[]{:S(2)}) collective-permute-start(bf16[128,1152]{1,0:T(8,128)(2,1)S(1)} %get-tuple-element.115), channel_id=1, source_target_pairs={{0,24},{4,28},{8,16},{12,20},{16,8},{20,12},{24,0},{28,4},{1,25},{... | collective-permute-start | bytes 884744 | tf_op jit(solution)/shard_map/ppermute | solution.py:110
  133.0 15.0 %collective-permute-start.30 = (bf16[128,1152]{1,0:T(8,128)(2,1)S(1)}, bf16[128,1152]{1,0:T(8,128)(2,1)S(1)}, u32[]{:S(2)}, u32[]{:S(2)}) collective-permute-start(bf16[128,1152]{1,0:T(8,128)(2,1)S(1)} %get-tuple-element.119), channel_id=1, source_target_pairs={{0,8},{4,12},{8,0},{12,4},{16,24},{20,28},{24,16},{28,20},{1,9},{5... | collective-permute-start | bytes 884744 | tf_op jit(solution)/shard_map/ppermute | solution.py:110
  134.3 14.7 %collective-permute-start.31 = (bf16[128,1152]{1,0:T(8,128)(2,1)S(1)}, bf16[128,1152]{1,0:T(8,128)(2,1)S(1)}, u32[]{:S(2)}, u32[]{:S(2)}) collective-permute-start(bf16[128,1152]{1,0:T(8,128)(2,1)S(1)} %get-tuple-element.120), channel_id=1, source_target_pairs={{0,16},{4,20},{8,24},{12,28},{16,0},{20,4},{24,8},{28,12},{1,17},{... | collective-permute-start | bytes 884744 | tf_op jit(solution)/shard_map/ppermute | solution.py:110
  145.8 59.9 %collective-permute-start.28 = (bf16[784,256]{1,0:T(8,128)(2,1)S(1)}, bf16[784,256]{1,0:T(8,128)(2,1)S(1)}, u32[]{:S(2)}, u32[]{:S(2)}) collective-permute-start(bf16[784,256]{1,0:T(8,128)(2,1)S(1)} %add.4.refs_6_), channel_id=1, source_target_pairs={{0,2},{1,3},{2,0},{3,1},{4,6},{5,7},{6,4},{7,5},{8,10},{9,11},{10,... | collective-permute-start | bytes 1204232 | tf_op jit(solution)/shard_map/ppermute | solution.py:110
  149.9 29.0 %collective-permute-start.36 = (bf16[128,512]{1,0:T(8,128)(2,1)S(1)}, bf16[128,512]{1,0:T(8,128)(2,1)S(1)}, u32[]{:S(2)}, u32[]{:S(2)}) collective-permute-start(bf16[128,512]{1,0:T(8,128)(2,1)S(1)} %get-tuple-element.131), channel_id=1, source_target_pairs={{2,3},{3,2},{6,7},{7,6},{10,11},{11,10},{14,15},{15,14},{18,19},{1... | collective-permute-start | bytes 393224 | tf_op jit(solution)/shard_map/ppermute | solution.py:110
  153.2 25.6 %collective-permute-start.37 = (bf16[128,512]{1,0:T(8,128)(2,1)S(1)}, bf16[128,512]{1,0:T(8,128)(2,1)S(1)}, u32[]{:S(2)}, u32[]{:S(2)}) collective-permute-start(bf16[128,512]{1,0:T(8,128)(2,1)S(1)} %get-tuple-element.132), channel_id=1, source_target_pairs={{0,2},{1,3},{4,6},{5,7},{8,10},{9,11},{12,14},{13,15},{16,18},{17,... | collective-permute-start | bytes 393224 | tf_op jit(solution)/shard_map/ppermute | solution.py:110
  154.5 27.8 %collective-permute-start.38 = (bf16[128,512]{1,0:T(8,128)(2,1)S(1)}, bf16[128,512]{1,0:T(8,128)(2,1)S(1)}, u32[]{:S(2)}, u32[]{:S(2)}) collective-permute-start(bf16[128,512]{1,0:T(8,128)(2,1)S(1)} %get-tuple-element.133), channel_id=1, source_target_pairs={{0,3},{1,2},{4,7},{5,6},{8,11},{9,10},{12,15},{13,14},{16,19},{17,... | collective-permute-start | bytes 393224 | tf_op jit(solution)/shard_map/ppermute | solution.py:110
  173.2 11.9 %collective-permute-start.33 = (bf16[336,256]{1,0:T(8,128)(2,1)S(1)}, bf16[336,256]{1,0:T(8,128)(2,1)S(1)}, u32[]{:S(2)}, u32[]{:S(2)}) collective-permute-start(bf16[336,256]{1,0:T(8,128)(2,1)S(1)} %get-tuple-element.127), channel_id=1, source_target_pairs={{0,1},{1,0},{2,3},{3,2},{4,5},{5,4},{6,7},{7,6},{8,9},{9,8},{10,11... | collective-permute-start | bytes 516104 | tf_op jit(solution)/shard_map/ppermute | solution.py:110
  178.9 6.3 %collective-permute-start.34 = (bf16[336,256]{1,0:T(8,128)(2,1)S(1)}, bf16[336,256]{1,0:T(8,128)(2,1)S(1)}, u32[]{:S(2)}, u32[]{:S(2)}) collective-permute-start(bf16[336,256]{1,0:T(8,128)(2,1)S(1)} %get-tuple-element.128), channel_id=1, source_target_pairs={{0,2},{1,3},{2,0},{3,1},{4,6},{5,7},{6,4},{7,5},{8,10},{9,11},{10,... | collective-permute-start | bytes 516104 | tf_op jit(solution)/shard_map/ppermute | solution.py:110
  178.9 26.9 %collective-permute-start.35 = (bf16[336,256]{1,0:T(8,128)(2,1)S(1)}, bf16[336,256]{1,0:T(8,128)(2,1)S(1)}, u32[]{:S(2)}, u32[]{:S(2)}) collective-permute-start(bf16[336,256]{1,0:T(8,128)(2,1)S(1)} %get-tuple-element.129), channel_id=1, source_target_pairs={{0,3},{1,2},{2,1},{3,0},{4,7},{5,6},{6,5},{7,4},{8,11},{9,10},{10,... | collective-permute-start | bytes 516104 | tf_op jit(solution)/shard_map/ppermute | solution.py:110
  182.4 28.0 %collective-permute-start.32 = (bf16[784,256]{1,0:T(8,128)(2,1)S(1)}, bf16[784,256]{1,0:T(8,128)(2,1)S(1)}, u32[]{:S(2)}, u32[]{:S(2)}) collective-permute-start(bf16[784,256]{1,0:T(8,128)(2,1)S(1)} %add.5.refs_9_), channel_id=1, source_target_pairs={{0,2},{1,3},{2,0},{3,1},{4,6},{5,7},{6,4},{7,5},{8,10},{9,11},{10,... | collective-permute-start | bytes 1204232 | tf_op jit(solution)/shard_map/ppermute | solution.py:110
  206.7 8.2 %collective-permute-start.41 = (bf16[144,896]{1,0:T(8,128)(2,1)S(1)}, bf16[144,896]{1,0:T(8,128)(2,1)S(1)}, u32[]{:S(2)}, u32[]{:S(2)}) collective-permute-start(bf16[144,896]{1,0:T(8,128)(2,1)S(1)} %get-tuple-element.135.refs_0_), channel_id=1, source_target_pairs={{0,24},{4,28},{8,16},{12,20},{16,8},{20,12},{24,0},{28,4},{1,25},{... | collective-permute-start | bytes 774152 | tf_op jit(solution)/shard_map/ppermute | solution.py:110
  206.9 12.9 %collective-permute-start.40 = (bf16[144,896]{1,0:T(8,128)(2,1)S(1)}, bf16[144,896]{1,0:T(8,128)(2,1)S(1)}, u32[]{:S(2)}, u32[]{:S(2)}) collective-permute-start(bf16[144,896]{1,0:T(8,128)(2,1)S(1)} %get-tuple-element.135.refs_0_), channel_id=1, source_target_pairs={{0,16},{4,20},{8,24},{12,28},{16,0},{20,4},{24,8},{28,12},{1,17},{... | collective-permute-start | bytes 774152 | tf_op jit(solution)/shard_map/ppermute | solution.py:110
  208.2 11.7 %collective-permute-start.39 = (bf16[144,896]{1,0:T(8,128)(2,1)S(1)}, bf16[144,896]{1,0:T(8,128)(2,1)S(1)}, u32[]{:S(2)}, u32[]{:S(2)}) collective-permute-start(bf16[144,896]{1,0:T(8,128)(2,1)S(1)} %get-tuple-element.135.refs_0_), channel_id=1, source_target_pairs={{0,8},{4,12},{8,0},{12,4},{16,24},{20,28},{24,16},{28,20},{1,9},{5... | collective-permute-start | bytes 774152 | tf_op jit(solution)/shard_map/ppermute | solution.py:110
  (26 other events, 271.7 us)

commit v5 on v4

--- a/solution.py
+++ b/solution.py
@@ -14,7 +14,7 @@
 MIB = 1 << 20
 
 LIMITS = {
-    "early": 16, "tokens": 56, "forward": 56, "columns": 8, "pool_pair": 16, "pool": 16, "norm": 16, "attention": 24,
+    "early": 60, "forward": 56, "columns": 8, "pool_pair": 16, "pool": 16, "norm": 16, "attention": 24,
     "dn": 12, "dn_pair": 16, "joined": 16, "prepare": 16, "out_grad": 16, "dvalue": 24, "embed": 24, "value_grad": 32,
     "add": 12, "pair_sum": 16, "packet_split": 16, "space_sum": 16, "head_grads": 16, "final": 16, "embed_final": 24,
 }
@@ -159,14 +159,41 @@
     wperm_ref[...] = mm(qkvw_ref[...], head_order(qkvw_ref.shape[1])).astype(BF16)
 
 
-def tokens_body(
-    scale, patches_ref, embed_ref, offset_ref, query_ref, wk_ref, tokens_ref, scores_ref, wback_ref, wq_ref
+def forward_step(fresh, patches_ref, embed_ref, offset, wq_ref, wv_ref, spread_ref, outs, state):
+    tokens_ref, value_ref, scores_ref = outs
+    acc_ref, max_ref, sum_ref = state
+    tokens = (mm(patches_ref[0], embed_ref[0]) + offset).astype(BF16)
+    tokens_ref[0] = tokens
+    pieces = mm(tokens, wq_ref[...])
+    scores = pieces[:, :LANES] + pieces[:, LANES : 2 * LANES] + pieces[:, 2 * LANES :]
+    scores_ref[0] = scores
+    value = mm(tokens, wv_ref[...])
+    value_ref[0] = value
+
+    @pl.when(fresh)
+    def _():
+        max_ref[...] = scores
+        sum_ref[...] = jnp.ones_like(scores)
+        acc_ref[...] = value
+
+    @pl.when(jnp.logical_not(fresh))
+    def _():
+        top = jnp.maximum(max_ref[...], scores)
+        old, new = jnp.exp(max_ref[...] - top), jnp.exp(scores - top)
+        max_ref[...] = top
+        sum_ref[...] = sum_ref[...] * old + new
+        acc_ref[...] = acc_ref[...] * mm(pack(old), spread_ref[...]) + value * mm(pack(new), spread_ref[...])
+
+
+def first_body(
+    scale, patches_ref, embed_ref, offset_ref, query_ref, wk_ref, wv_ref,
+    tokens_ref, value_ref, scores_ref, wq_ref, wback_ref, acc_ref, max_ref, sum_ref, spread_ref,
 ):
-    i = pl.program_id(0)
+    v = pl.program_id(0)
     width = wk_ref.shape[1]
     size = width // HEADS
 
-    @pl.when(i == 0)
+    @pl.when(v == 0)
     def _():
         row, column = iota((LANES, width), 0), iota((LANES, width), 1)
         own = (row & 15) == (column >> (size.bit_length() - 1))
@@ -180,43 +207,37 @@
         group = iota((width, LANES), 1) >> 4
         back = jnp.where((group == 0) | (group == 2), hi, jnp.where(group == 1, mid, 0.0))
         wback_ref[...] = back.astype(BF16)
-
-    tokens = (mm(patches_ref[0], embed_ref[0]) + offset_ref[pl.ds(i, 1), :]).astype(BF16)
-    tokens_ref[0] = tokens
-    pieces = mm(tokens, wq_ref[...])
-    scores_ref[0] = pieces[:, :LANES] + pieces[:, LANES : 2 * LANES] + pieces[:, 2 * LANES :]
-
-
-def forward_body(count, me_ref, tokens_ref, scores_ref, wv_ref, value_ref, keep_ref, send_ref, max_ref, spread_ref, acc_ref):
-    j = pl.program_id(0)
+        spread_ref[...] = spread_matrix(width, size)
+
+    forward_step(
+        v == 0, patches_ref, embed_ref, offset_ref[pl.ds(v, 1), :], wq_ref, wv_ref, spread_ref,
+        (tokens_ref, value_ref, scores_ref), (acc_ref, max_ref, sum_ref),
+    )
+
+
+def second_body(
+    start, me_ref, patches_ref, embed_ref, offset_ref, wq_ref, wv_ref, acc0_ref, max0_ref, sum0_ref,
+    tokens_ref, value_ref, scores_ref, keep_ref, send_ref, spread_ref, acc_ref, max_ref, sum_ref,
+):
+    v = pl.program_id(0)
     width = wv_ref.shape[1]
 
-    @pl.when(j == 0)
+    @pl.when(v == 0)
     def _():
         spread_ref[...] = spread_matrix(width, width // HEADS)
-        top = scores_ref[0]
-        for v in range(1, count):
-            top = jnp.maximum(top, scores_ref[v])
-        max_ref[...] = top
-
-    value = mm(tokens_ref[0], wv_ref[...])
-    value_ref[0] = value
-    term = mm(pack(jnp.exp(scores_ref[j] - max_ref[...])), spread_ref[...]) * value
-
-    @pl.when(j == 0)
+        acc_ref[...] = acc0_ref[...]
+        max_ref[...] = max0_ref[...]
+        sum_ref[...] = sum0_ref[...]
+
+    forward_step(
+        v < 0, patches_ref, embed_ref, offset_ref[pl.ds(start + v, 1), :], wq_ref, wv_ref, spread_ref,
+        (tokens_ref, value_ref, scores_ref), (acc_ref, max_ref, sum_ref),
+    )
+
+    @pl.when(v == pl.num_programs(0) - 1)
     def _():
-        acc_ref[...] = term
-
-    @pl.when(j > 0)
-    def _():
-        acc_ref[...] += term
-
-    @pl.when(j == count - 1)
-    def _():
-        top = max_ref[...]
-        total = sum(jnp.exp(scores_ref[v] - top) for v in range(count))
-        low = iota(top.shape, 1) < LANES // 2
-        max_ref[...] = jnp.where(low, top, total)
+        low = iota(max_ref.shape, 1) < LANES // 2
+        max_ref[...] = jnp.where(low, max_ref[...], sum_ref[...])
         block = keep_ref.shape[1]
         core = me_ref[0] & 1
         for c in range(keep_ref.shape[0]):
@@ -491,12 +512,14 @@
         refs[-1][k] = ref[...]
 
 
-def value_grad_body(me_ref, tokens_ref, dv_ref, dl_ref, keep_ref, send_ref, all_ref):
-    width = dv_ref.shape[2]
+def value_grad_body(me_ref, *refs):
+    tokens_refs, dv_refs, dl_refs, (keep_ref, send_ref, all_ref) = refs[:2], refs[2:4], refs[4:6], refs[6:]
+    width = dv_refs[0].shape[2]
     total, both = 0.0, 0.0
-    for v in range(dv_ref.shape[0]):
-        total = total + mm(tokens_ref[v], dv_ref[v], TN)
-        both = both + mm(tokens_ref[v], dl_ref[v], TN)
+    for tokens_ref, dv_ref, dl_ref in zip(tokens_refs, dv_refs, dl_refs):
+        for v in range(dv_ref.shape[0]):
+            total = total + mm(tokens_ref[v], dv_ref[v], TN)
+            both = both + mm(tokens_ref[v], dl_ref[v], TN)
     all_ref[:, :width] = total.astype(BF16)
     all_ref[:, width:] = pack(both[:, :LANES] + both[:, LANES:])
     block = keep_ref.shape[1]
@@ -525,41 +548,45 @@
 
 
 def packet_split_body(n_in, n_space, me_ref, *refs):
-    ins, gathered_ref = refs[:n_in], refs[n_in]
-    small_refs, out_refs = refs[n_in + 1 : n_in + 1 + n_space], refs[n_in + 1 + n_space : n_in + 1 + 2 * n_space]
-    cols_ref = refs[-1]
+    ins, gathered_ref, out_refs, (cols_ref,) = refs[:n_in], refs[n_in], refs[n_in + 1 : -1], refs[-1:]
     block, width = ins[0].shape[0], ins[0].shape[1] - LANES
     total = sum(ref[:, :width].astype(F32) for ref in ins).astype(BF16)
     factor = pack(sum(unpack(ref[:, width:]) for ref in ins))
     half = n_space // 2
-    cols = cols_ref.shape[2]
+    cols = cols_ref.shape[2] // 2
     for c in range(half):
-        cols_ref[c] = total[:, c * cols : (c + 1) * cols]
+        cols_ref[c] = total[:, 2 * c * cols : 2 * (c + 1) * cols]
     height = gathered_ref.shape[1]
-    part = small_refs[0].shape[0] - height
+    part = out_refs[0].shape[0] - height - 2 * block
     for k in range(n_space):
-        out_refs[k][...] = cols_ref[jnp.maximum((me_ref[1] ^ k) - half, 0)]
-        small_refs[k][:height, :] = gathered_ref[me_ref[1] ^ k]
+        out_refs[k][:height, :] = gathered_ref[me_ref[1] ^ k]
         for piece in range(block // part):
             lanes = slice(piece * LANES, (piece + 1) * LANES)
-            small_refs[k][height:, lanes] = factor[piece * part : (piece + 1) * part, :]
+            out_refs[k][height : height + part, lanes] = factor[piece * part : (piece + 1) * part, :]
+        large = cols_ref[jnp.maximum((me_ref[1] ^ k) - half, 0)]
+        out_refs[k][height + part : height + part + block, :] = large[:, :cols]
+        out_refs[k][height + part + block :, :] = large[:, cols:]
 
 
 def space_sum_body(n, *refs):
-    small, large, (out_ref, weight_ref) = refs[:n], refs[n : 2 * n], refs[2 * n :]
-    block, width = large[0].shape
-    out_ref[:block, :width] = sum(ref[...].astype(F32) for ref in large).astype(BF16)
+    ins, (out_ref, weight_ref) = refs[:n], refs[n:]
+    cols = ins[0].shape[1]
+    width = out_ref.shape[1] - LANES - cols
+    block = out_ref.shape[0] - 16
     height = block + 16 + weight_ref.shape[0]
-    part = small[0].shape[0] - height
+    part = ins[0].shape[0] - height - 2 * block
+    total = sum(ref[...].astype(F32) for ref in ins)
+    for piece in range(2):
+        at = slice(height + part + piece * block, height + part + (piece + 1) * block)
+        out_ref[:block, piece * cols : (piece + 1) * cols] = total[at, :].astype(BF16)
     for piece in range(block // part):
         lanes = slice(piece * LANES, (piece + 1) * LANES)
-        factor = pack(sum(unpack(ref[height:, lanes]) for ref in small))
+        factor = pack(sum(unpack(ref[height : height + part, lanes]) for ref in ins))
         out_ref[piece * part : (piece + 1) * part, width : width + LANES] = factor
-    out_ref[block:, : width + LANES] = jnp.zeros((out_ref.shape[0] - block, width + LANES), BF16)
-    total = sum(ref[:height, :].astype(F32) for ref in small)
+    out_ref[block:, : width + LANES] = jnp.zeros((16, width + LANES), BF16)
     out_ref[:block, width + LANES :] = total[:block, :].astype(BF16)
     out_ref[block:, width + LANES :] = three_rows(jnp.sum(total[block : block + 16, :], axis=0, keepdims=True))
-    weight_ref[...] = total[block + 16 :, :]
+    weight_ref[...] = total[block + 16 : height, :]
 
 
 def add_body(n, keep_ref, got_ref, *refs):
@@ -617,43 +644,65 @@
     whole = lambda shape: pl.BlockSpec(shape, lambda v: (0,) * len(shape))
     every = lambda shape: pl.BlockSpec((1,) + shape, lambda v: (v,) + (0,) * len(shape))
     n_chip = n_var // 2
-    tokens, scores, w_back = call(
-        functools.partial(tokens_body, scale),
-        [struct((count, rows, width), BF16), struct((count, rows, LANES), F32), struct((width, LANES), BF16)],
-        limit=LIMITS["tokens"],
-        grid=(count,),
-        in_specs=[
-            every((rows, pixels)),
-            every((pixels, width)),
-            whole((count, width)),
+    half = count // 2
+
+    dattn, cot_own, w_heads = call(
+        early_body,
+        [struct((rows, group), BF16), struct((block, width), BF16), struct(qkv_weight.shape, BF16)],
+        limit=LIMITS["early"],
+        grid=(1,),
+        in_specs=[SMEM] + [whole(x.shape) for x in (cotangent, out_weight, qkv_weight)],
+        out_specs=[whole((rows, group)), whole((block, width)), whole(qkv_weight.shape)],
+        cost_estimate=cost(2e8, 4e6),
+        name="early",
+    )(me, cotangent, out_weight, qkv_weight)
+    dattn_all = gather_direct(dattn, "space")
+
+    def forward_outs(here):
+        shapes = [((here, rows, width), BF16), ((here, rows, width), F32), ((here, rows, LANES), F32)]
+        return [struct(*x) for x in shapes], [every(x[1:]) for x, _ in shapes]
+
+    def inputs(start):
+        at = lambda shape: pl.BlockSpec((1,) + shape, lambda v: (v + start,) + (0,) * len(shape))
+        return [at((rows, pixels)), at((pixels, width)), whole((count, width))]
+
+    state = [((rows, width), F32), ((rows, LANES), F32), ((rows, LANES), F32)]
+    out_shapes, out_specs = forward_outs(half)
+    tokens0, value0, scores0, w_query, w_back, *state0 = call(
+        functools.partial(first_body, scale),
+        out_shapes
+        + [struct((width, 3 * LANES), BF16), struct((width, LANES), BF16)]
+        + [struct(*x) for x in state],
+        limit=LIMITS["forward"],
+        after=[dattn],
+        grid=(half,),
+        in_specs=inputs(0)
+        + [
             whole((1, width)),
             pl.BlockSpec((width, width), lambda v: (0, 0)),
-        ],
-        out_specs=[every((rows, width)), every((rows, LANES)), whole((width, LANES))],
-        scratch_shapes=[pltpu.VMEM((width, 3 * LANES), BF16)],
-        cost_estimate=cost(6e9, 2e7),
-        name="tokens",
-    )(patches, embed_weight, var_embed, query, agg_kv)
-    value, keep, send = call(
-        functools.partial(forward_body, count),
-        [struct((count, rows, width), F32)] + [struct((n_chip, block, packet), F32)] * 2,
-        limit=LIMITS["forward"],
-        grid=(count,),
-        in_specs=[
-            SMEM,
-            every((rows, width)),
-            whole((count, rows, LANES)),
             pl.BlockSpec((width, width), lambda v: (0, 1)),
         ],
-        out_specs=[every((rows, width))] + [whole((n_chip, block, packet))] * 2,
-        scratch_shapes=[
-            pltpu.VMEM((rows, LANES), F32),
-            pltpu.VMEM((LANES, width), BF16),
-            pltpu.VMEM((rows, width), F32),
-        ],
+        out_specs=out_specs + [whole((width, 3 * LANES)), whole((width, LANES))] + [whole(x) for x, _ in state],
+        scratch_shapes=[pltpu.VMEM((LANES, width), BF16)],
+        cost_estimate=cost(6e9, 2e7),
+        name="forward_first",
+    )(patches, embed_weight, var_embed, query, agg_kv, agg_kv)
+    out_shapes, out_specs = forward_outs(count - half)
+    tokens1, value1, scores1, keep, send = call(
+        functools.partial(second_body, half),
+        out_shapes + [struct((n_chip, block, packet), F32)] * 2,
+        limit=LIMITS["forward"],
+        after=dattn_all[1:],
+        grid=(count - half,),
+        in_specs=[SMEM]
+        + inputs(half)
+        + [whole((width, 3 * LANES)), pl.BlockSpec((width, width), lambda v: (0, 1))]
+        + [whole(x) for x, _ in state],
+        out_specs=out_specs + [whole((n_chip, block, packet))] * 2,
+        scratch_shapes=[pltpu.VMEM((LANES, width), BF16)] + [pltpu.VMEM(*x) for x in state],
         cost_estimate=cost(4e9, 1e7),
-        name="forward",
-    )(me, tokens, scores, agg_kv)
+        name="forward_second",
+    )(me, patches, embed_weight, var_embed, w_query, agg_kv, *state0)
 
     def pool_pairs(mine, got):
         return call(
@@ -666,22 +715,10 @@
         )(me, mine, got)
 
     received = exchange_pairs(keep, send, pool_pairs)
-    dattn, cot_own, w_heads = call(
-        early_body,
-        [struct((rows, group), BF16), struct((block, width), BF16), struct(qkv_weight.shape, BF16)],
-        limit=LIMITS["early"],
-        after=[received[0]],
-        in_specs=[SMEM] + [vmem] * 3,
-        cost_estimate=cost(2e8, 4e6),
-        name="early",
-    )(me, cotangent, out_weight, qkv_weight)
-    dattn_all = gather_direct(dattn, "space")
-
     mixed, pooled_packet = call(
         functools.partial(pool_body, n_chip),
         [struct((block, width), F32), struct((block, packet), BF16)],
         limit=LIMITS["pool"],
-        after=dattn_all[1:],
         cost_estimate=cost(1e8, 2e6),
         name="pool",
     )(*received)
@@ -764,17 +801,46 @@
         cost_estimate=cost(6e8, 4e6),
         name="prepare",
     )(me, pooled_packets, joined_even, joined_odd, agg_out)
-    d_value, d_logit = call(
-        dvalue_body,
-        [struct((count, rows, width), BF16), struct((count, rows, 2 * LANES), BF16)],
-        limit=LIMITS["dvalue"],
-        grid=(count,),
-        in_specs=[whole((rows, width)), whole((3, rows, LANES)), every((rows, width)), every((rows, LANES))],
-        out_specs=[every((rows, width)), every((rows, 2 * LANES))],
-        scratch_shapes=[pltpu.VMEM((LANES, width), BF16), pltpu.VMEM((width, LANES), BF16)],
-        cost_estimate=cost(4e9, 1e7),
-        name="dvalue",
-    )(d_pooled, stat, value, scores)
+    def d_values(value, scores):
+        here = value.shape[0]
+        return call(
+            dvalue_body,
+            [struct((here, rows, width), BF16), struct((here, rows, 2 * LANES), BF16)],
+            limit=LIMITS["dvalue"],
+            grid=(here,),
+            in_specs=[whole((rows, width)), whole((3, rows, LANES)), every((rows, width)), every((rows, LANES))],
+            out_specs=[every((rows, width)), every((rows, 2 * LANES))],
+            scratch_shapes=[pltpu.VMEM((LANES, width), BF16), pltpu.VMEM((width, LANES), BF16)],
+            cost_estimate=cost(2e9, 5e6),
+            name="dvalue",
+        )(d_pooled, stat, value, scores)
+
+    def embed(start, d_value, d_logit, after):
+        here = d_value.shape[0]
+        at = lambda shape: pl.BlockSpec((1,) + shape, lambda v: (v + start,) + (0,) * len(shape))
+        blocks = (n_space // 2, here * pixels + 16, cols)
+        return call(
+            functools.partial(embed_body, n_space),
+            [struct(blocks, BF16)] * 2,
+            limit=LIMITS["embed"],
+            after=after,
+            grid=(here,),
+            in_specs=[
+                SMEM,
+                every((rows, width)),
+                every((rows, 2 * LANES)),
+                at((rows, pixels)),
+                pl.BlockSpec((width, width), lambda v: (0, 1)),
+                whole((width, LANES)),
+            ],
+            out_specs=[whole(blocks)] * 2,
+            scratch_shapes=[pltpu.VMEM((n_space, pixels, cols), BF16), pltpu.VMEM((16, width), F32)],
+            cost_estimate=cost(1.5e9, 4e6),
+            name="embed",
+        )(me, d_value, d_logit, patches, agg_kv, w_back)
+
+    dv0, dl0 = d_values(value0, scores0)
+    dv1, dl1 = d_values(value1, scores1)
 
     step = max(drows, 256)
     kv_keep, kv_send = call(
@@ -782,17 +848,14 @@
         [struct((n_chip, drows, packet), BF16)] * 2,
         limit=LIMITS["value_grad"],
         grid=(width // step,),
-        in_specs=[
-            SMEM,
-            pl.BlockSpec((count, rows, step), lambda i: (0, 0, i)),
-            whole((count, rows, width)),
-            whole((count, rows, 2 * LANES)),
-        ],
+        in_specs=[SMEM]
+        + [pl.BlockSpec(x.shape[:2] + (step,), lambda i: (0, 0, i)) for x in (tokens0, tokens1)]
+        + [whole(x.shape) for x in (dv0, dv1, dl0, dl1)],
         out_specs=[whole((n_chip, drows, packet))] * 2,
         scratch_shapes=[pltpu.VMEM((step, packet), BF16)],
         cost_estimate=cost(4e9, 1e7),
         name="value_grad",
-    )(me, tokens, d_value, d_logit)
+    )(me, tokens0, tokens1, dv0, dv1, dl0, dl1)
     kv_got = swap(kv_send, "var", 1)
 
     out_block = call(
@@ -807,29 +870,6 @@
         cost_estimate=cost(6e8, 3e6),
         name="out_grad",
     )(me, pooled_packets, d_joined, dgain, attn, cotangent)
-
-    def embed(start, here, after):
-        at = lambda shape: pl.BlockSpec((1,) + shape, lambda v: (v + start,) + (0,) * len(shape))
-        half = (n_space // 2, here * pixels + 16, cols)
-        return call(
-            functools.partial(embed_body, n_space),
-            [struct(half, BF16)] * 2,
-            limit=LIMITS["embed"],
-            after=after,
-            grid=(here,),
-            in_specs=[
-                SMEM,
-                at((rows, width)),
-                at((rows, 2 * LANES)),
-                at((rows, pixels)),
-                pl.BlockSpec((width, width), lambda v: (0, 1)),
-                whole((width, LANES)),
-            ],
-            out_specs=[whole(half)] * 2,
-            scratch_shapes=[pltpu.VMEM((n_space, pixels, cols), BF16), pltpu.VMEM((16, width), F32)],
-            cost_estimate=cost(1.5e9, 4e6),
-            name="embed",
-        )(me, d_value, d_logit, patches, agg_kv, w_back)
 
     def scatter_embed(keep, arrived, after):
         n = n_space // 2 - 1
@@ -852,36 +892,34 @@
             bit *= 2
         return mine, list(sums)
 
-    half = count // 2
-    keep0, send0 = embed(0, half, [kv_keep])
+    keep0, send0 = embed(0, dv0, dl0, [kv_keep])
     arrived0 = swap(send0, "space", 1)
-    keep1, send1 = embed(half, count - half, [])
-    arrived1 = swap(send1, "space", 1)
-
     kv_blocks = call(
         functools.partial(pair_sum_body, n_chip),
         [struct((drows, packet), BF16)] * n_chip,
         limit=LIMITS["pair_sum"],
+        after=[keep0],
         in_specs=[SMEM] + [vmem] * 2,
         cost_estimate=cost(1e6, 1e6),
         name="pair_sum",
     )(me, kv_keep, kv_got)
     kv_parts = [kv_blocks[0]] + [swap(kv_blocks[k], "var", 2 * k) for k in range(1, n_chip)]
-    mine0, sums0 = scatter_embed(keep0, arrived0, [kv_parts[-1]])
+    keep1, send1 = embed(half, dv1, dl1, [kv_blocks[0]])
+    arrived1 = swap(send1, "space", 1)
     height = drows + 16 + group
     part = drows * LANES // cols
     pieces = call(
         functools.partial(packet_split_body, n_chip, n_space),
-        [struct((height + part, cols), BF16)] * n_space + [struct((drows, kv_cols), BF16)] * n_space,
+        [struct((height + part + 2 * drows, cols), BF16)] * n_space,
         limit=LIMITS["packet_split"],
-        after=sums0,
         in_specs=[SMEM] + [vmem] * (n_chip + 1),
         scratch_shapes=[pltpu.VMEM((n_space // 2, drows, kv_cols), BF16)],
         cost_estimate=cost(1e6, 1e6),
         name="packet_split",
     )(me, *kv_parts, out_block)
-    small, large = pieces[:n_space], pieces[n_space:]
-    mine1, sums1 = scatter_embed(keep1, arrived1, [small[0]])
+    pieces_all = exchange_direct(pieces, "space")
+    mine0, sums0 = scatter_embed(keep0, arrived0, [pieces[0]])
+    mine1, sums1 = scatter_embed(keep1, arrived1, sums0)
     grad_qkv, head_flag = call(
         functools.partial(head_grads_body, n_space),
         [struct((cols, 3 * group), F32), struct((8, LANES), F32)],
@@ -889,24 +927,20 @@
         cost_estimate=cost(1e9, 3e6),
         name="head_grads",
     )(*normed_all, dqkv)
-    small_all = exchange_direct(small, "space")
-    large_all = [large[0]] + [
-        swap(large[k], "space", k, lambda target: target >= n_space // 2) for k in range(1, n_space)
-    ]
     kv_sum, grad_out = call(
         functools.partial(space_sum_body, n_space),
         [struct((drows + 16, kv_cols + LANES + cols), BF16), struct((group, cols), F32)],
         limit=LIMITS["space_sum"],
-        after=mine0[2:] + sums1 + [head_flag],
+        after=sums1 + [head_flag],
         cost_estimate=cost(1e6, 1e6),
         name="space_sum",
-    )(*small_all, *large_all)
+    )(*pieces_all)
 
     def stack(parts):
         return call(
             stack_body,
             struct((len(parts),) + parts[0].shape, BF16),
-            after=mine1[2:],
+            after=mine0[2:] + mine1[2:],
             cost_estimate=cost(1e6, 1e6),
             name="stack",
         )(*parts)

time: 227 us -> 224 us (0.987)
  the two profiles are of different devices: /device:TPU:17 before, /device:TPU:0 now
where the time goes in v5:
time: 224 us
  waiting for transfers between devices  104 us (46%)
  Pallas kernels  72.4 us (32%)
  starting transfers between devices  43.6 us (19%)
  local copies, waits for them, and re-layouts  2.31 us (1%)
    ppermute x40, waiting for transfers between devices, swap(): return lax.ppermute(x, axis, pairs)  104 us
    pallas_call x27, Pallas kernels, run(): pl.pallas_call(lambda *refs: body(*refs[:n], *refs[n + m:]), out_shape=ou...  72.4 us
    ppermute x40, starting transfers between devices, swap(): return lax.ppermute(x, axis, pairs)  43.6 us
  transfers between devices with their start and end apart: 40, of which 24 were waited for; matrix products, arithmetic and copies ran while one was open for 0% of the time, Pallas kernels for 17%

profile of v5, /device:TPU:0, one launch (start us, length us, event | category | flops | bytes accessed | tf_op | source)
XLA Modules:
  0.0 224.0 jit_solution(129874060530981667)
XLA Ops:
  1.2 3.1 %early.1 = (bf16[256,128]{1,0:T(8,128)(2,1)}, bf16[32,1024]{1,0:T(8,128)(2,1)}, bf16[1024,384]{1,0:T(8,128)(2,1)}) custom-call(s32[2]{0:T(128)} %pad_add_fusion.refs_0_, bf16[256,1024]{1,0:T(8,128)(2,1)} %refs_5_.5, bf16[128,1024]{1,0:T(8,128)(2,1)} %refs_2_.3, bf16[1024,384]{1,0:T(8,128)(2,1)} %refs_3_.5), custom_call_target="tpu_custom_call" | custom-call | flops 200000000 | bytes 4000000 | tf_op jit(solution)/shard_map/early/pallas_call | solution.py:84
  4.3 5.0 %collective-permute-start.2 = (bf16[256,128]{1,0:T(8,128)(2,1)}, bf16[256,128]{1,0:T(8,128)(2,1)S(1)}, u32[]{:S(2)}, u32[]{:S(2)}) collective-permute-start(bf16[256,128]{1,0:T(8,128)(2,1)} %get-tuple-element.80.refs_6_.refs_4_), channel_id=1, source_target_pairs={{0,3},{1,2},{2,1},{3,0},{4,7},{5,6},{6,5},{7,4},{8,11},{9,10},{10,... | collective-permute-start | bytes 196616 | tf_op jit(solution)/shard_map/ppermute | solution.py:110
  9.9 10.8 %forward_first.1 = (bf16[3,256,1024]{2,1,0:T(8,128)(2,1)}, f32[3,256,1024]{2,1,0:T(8,128)}, f32[3,256,128]{2,1,0:T(8,128)}, bf16[1024,384]{1,0:T(8,128)(2,1)}, b...) custom-call(bf16[6,256,256]{2,1,0:T(8,128)(2,1)} %refs_3_.9, ...), custom_call_target="tpu_custom_call" | custom-call | flops 6000000000 | bytes 20000000 | tf_op jit(solution)/shard_map/forward_first/pallas_call | solution.py:84
  21.4 9.2 %forward_second.1 = (bf16[3,256,1024]{2,1,0:T(8,128)(2,1)}, f32[3,256,1024]{2,1,0:T(8,128)}, f32[3,256,128]{2,1,0:T(8,128)}, f32[4,32,1152]{2,1,0:T(8,128)}, f32[4,32,1152]{2,1,0:T(8,128)}) custom-call(s32[2]{0:T(128)} %pad_add_fusion.refs_0_, bf16[6,256,256]{2,1,0:T(8,128)(2,1)} %refs_3_.9, bf16[6,256,1024]{2,1,0:T(8,128)(2,1)} %refs_2_.5, ...), custom_call_target="tpu_custom_call" | custom-call | flops 4000000000 | bytes 10000000 | tf_op jit(solution)/shard_map/forward_second/pallas_call | solution.py:84
  30.8 2.2 collective-permute-done.3.refs_2_
  38.5 2.9 %collective-permute-done.4.refs_1_ = f32[32,1152]{1,0:T(8,128)S(1)} collective-permute-done((f32[32,1152]{1,0:T(8,128)S(1)}, f32[32,1152]{1,0:T(8,128)S(1)}, u32[]{:S(2)}, u32[]{:S(2)}) %collective-permute-start.4) | collective-permute-done | bytes 147488 | tf_op jit(solution)/shard_map/ppermute | solution.py:110
  41.4 4.1 %collective-permute-done.5.refs_2_ = f32[32,1152]{1,0:T(8,128)S(1)} collective-permute-done((f32[32,1152]{1,0:T(8,128)S(1)}, f32[32,1152]{1,0:T(8,128)S(1)}, u32[]{:S(2)}, u32[]{:S(2)}) %collective-permute-start.5) | collective-permute-done | bytes 147488 | tf_op jit(solution)/shard_map/ppermute | solution.py:110
  49.4 2.2 collective-permute-done.9
  54.7 2.0 norm.1
  56.6 3.7 %collective-permute-start.13 = (bf16[256,384]{1,0:T(8,128)(2,1)S(1)}, bf16[256,384]{1,0:T(8,128)(2,1)S(1)}, u32[]{:S(2)}, u32[]{:S(2)}) collective-permute-start(bf16[256,384]{1,0:T(8,128)(2,1)S(1)} %get-tuple-element.94.refs_0_), channel_id=1, source_target_pairs={{0,3},{1,2},{2,1},{3,0},{4,7},{5,6},{6,5},{7,4},{8,11},{9,10},{10,... | collective-permute-start | bytes 589832 | tf_op jit(solution)/shard_map/ppermute | solution.py:110
  61.1 5.3 %collective-permute-done.13.refs_4_.refs_3_ = bf16[256,384]{1,0:T(8,128)(2,1)S(1)} collective-permute-done((bf16[256,384]{1,0:T(8,128)(2,1)S(1)}, bf16[256,384]{1,0:T(8,128)(2,1)S(1)}, u32[]{:S(2)}, u32[]{:S(2)}) %collective-permute-start.13) | collective-permute-done | bytes 196640 | tf_op jit(solution)/shard_map/ppermute | solution.py:110
  66.4 10.6 %collective-permute-done.12.refs_3_.refs_2_ = bf16[256,384]{1,0:T(8,128)(2,1)S(1)} collective-permute-done((bf16[256,384]{1,0:T(8,128)(2,1)S(1)}, bf16[256,384]{1,0:T(8,128)(2,1)S(1)}, u32[]{:S(2)}, u32[]{:S(2)}) %collective-permute-start.12) | collective-permute-done | bytes 196640 | tf_op jit(solution)/shard_map/ppermute | solution.py:110
  77.6 2.9 %collective-permute-start.15 = (bf16[256,256]{1,0:T(8,128)(2,1)S(1)}, bf16[256,256]{1,0:T(8,128)(2,1)S(1)}, u32[]{:S(2)}, u32[]{:S(2)}) collective-permute-start(bf16[256,256]{1,0:T(8,128)(2,1)S(1)} %get-tuple-element.99), channel_id=1, source_target_pairs={{0,2},{1,3},{2,0},{3,1},{4,6},{5,7},{6,4},{7,5},{8,10},{9,11},{10,... | collective-permute-start | bytes 393224 | tf_op jit(solution)/shard_map/ppermute | solution.py:110
  82.0 11.5 %attention.1 = (bf16[1024,128]{1,0:T(8,128)(2,1)S(1)}, bf16[1024,384]{1,0:T(8,128)(2,1)S(1)}) custom-call(bf16[256,384]{1,0:T(8,128)(2,1)S(1)} %get-tuple-element.94.refs_0_, bf16[256,384]{1,0:T(8,128)(2,1)S(1)} %collective-permute-done.11.refs_2_.refs_1_, bf16[256,384]{1,0:T(8,128)(2,1)S(1)} %collective-permute-done.12.refs_3_.refs_2_, ...), custom_call_target="tpu_custom_call" | custom-call | flops 6000000000 | bytes 4000000 | tf_op jit(solution)/shard_map/attention/pallas_call | solution.py:84
  101.9 2.4 %collective-permute-done.20.refs_3_ = bf16[32,1024]{1,0:T(8,128)(2,1)S(1)} collective-permute-done((bf16[32,1024]{1,0:T(8,128)(2,1)S(1)}, bf16[32,1024]{1,0:T(8,128)(2,1)S(1)}, u32[]{:S(2)}, u32[]{:S(2)}) %collective-permute-start.20) | collective-permute-done | bytes 65568 | tf_op jit(solution)/shard_map/ppermute | solution.py:110
  108.9 1.8 collective-permute-done.23
  115.4 2.5 %dvalue.3 = (bf16[3,256,1024]{2,1,0:T(8,128)(2,1)S(1)}, bf16[3,256,256]{2,1,0:T(8,128)(2,1)S(1)}) custom-call(f32[256,1024]{1,0:T(8,128)S(1)} %get-tuple-element.112.refs_0_, f32[3,256,128]{2,1,0:T(8,128)S(1)} %get-tuple-element.113.refs_1_, f32[3,256,1024]{2,1,0:T(8,128)S(1)} %copy-done.19, f32[3,256,128]{2,1,0:T(8,128)S(1)} %copy-done.22), custom_call_target="tpu_custom_call" | custom-call | flops 2000000000 | bytes 5000000 | tf_op jit(solution)/shard_map/dvalue/pallas_call | solution.py:84
  117.9 2.5 %dvalue.2 = (bf16[3,256,1024]{2,1,0:T(8,128)(2,1)S(1)}, bf16[3,256,256]{2,1,0:T(8,128)(2,1)S(1)}) custom-call(f32[256,1024]{1,0:T(8,128)S(1)} %get-tuple-element.112.refs_0_, f32[3,256,128]{2,1,0:T(8,128)S(1)} %get-tuple-element.113.refs_1_, f32[3,256,1024]{2,1,0:T(8,128)S(1)} %copy-done.18, f32[3,256,128]{2,1,0:T(8,128)S(1)} %copy-done.21), custom_call_target="tpu_custom_call" | custom-call | flops 2000000000 | bytes 5000000 | tf_op jit(solution)/shard_map/dvalue/pallas_call | solution.py:84
  120.4 6.1 %value_grad.1 = (bf16[4,128,1152]{2,1,0:T(8,128)(2,1)S(1)}, bf16[4,128,1152]{2,1,0:T(8,128)(2,1)S(1)}) custom-call(s32[2]{0:T(128)S(1)} %copy-done.7, bf16[3,256,1024]{2,1,0:T(8,128)(2,1)S(1)} %copy-done.23, bf16[3,256,1024]{2,1,0:T(8,128)(2,1)S(1)} %copy-done.20, bf16[3,256,1024]{2,1,0:T(8,128)(2,1)S(1)} %get-tuple-element.116.refs_3_.refs_1_, ...), custom_call_target="tpu_custom_call" | custom-call | flops 4000000000 | bytes 10000000 | tf_op jit(solution)/shard_map/value_grad/pallas_call | solution.py:84
  126.8 4.1 %embed.2 = (bf16[2,784,256]{2,1,0:T(8,128)(2,1)S(1)}, bf16[2,784,256]{2,1,0:T(8,128)(2,1)S(1)}) custom-call(s32[2]{0:T(128)S(1)} %copy-done.7, bf16[3,256,1024]{2,1,0:T(8,128)(2,1)S(1)} %get-tuple-element.116.refs_3_.refs_1_, bf16[3,256,256]{2,1,0:T(8,128)(2,1)S(1)} %get-tuple-element.117.refs_5_.refs_2_, bf16[6,256,256]{2,1,0:T(8,128)(2,1)S(1)} %copy-done.3, ...), custom_call_target="tpu_custom_call" | custom-call | flops 1500000000 | bytes 4000000 | tf_op jit(solution)/shard_map/embed/pallas_call | solution.py:84
  132.1 4.3 %embed.3 = (bf16[2,784,256]{2,1,0:T(8,128)(2,1)S(1)}, bf16[2,784,256]{2,1,0:T(8,128)(2,1)S(1)}) custom-call(s32[2]{0:T(128)S(1)} %copy-done.7, bf16[3,256,1024]{2,1,0:T(8,128)(2,1)S(1)} %get-tuple-element.123.refs_4_.refs_1_, bf16[3,256,256]{2,1,0:T(8,128)(2,1)S(1)} %get-tuple-element.124.refs_6_.refs_2_, bf16[6,256,256]{2,1,0:T(8,128)(2,1)S(1)} %copy-done.3, ...), custom_call_target="tpu_custom_call" | custom-call | flops 1500000000 | bytes 4000000 | tf_op jit(solution)/shard_map/embed/pallas_call | solution.py:84
  136.4 2.1 collective-permute-start.31
  143.3 5.1 %collective-permute-done.27.refs_2_ = bf16[128,1152]{1,0:T(8,128)(2,1)S(1)} collective-permute-done((bf16[128,1152]{1,0:T(8,128)(2,1)S(1)}, bf16[128,1152]{1,0:T(8,128)(2,1)S(1)}, u32[]{:S(2)}, u32[]{:S(2)}) %collective-permute-start.27) | collective-permute-done | bytes 294944 | tf_op jit(solution)/shard_map/ppermute | solution.py:110
  148.4 6.3 %collective-permute-done.28.refs_3_ = bf16[128,1152]{1,0:T(8,128)(2,1)S(1)} collective-permute-done((bf16[128,1152]{1,0:T(8,128)(2,1)S(1)}, bf16[128,1152]{1,0:T(8,128)(2,1)S(1)}, u32[]{:S(2)}, u32[]{:S(2)}) %collective-permute-start.28) | collective-permute-done | bytes 294944 | tf_op jit(solution)/shard_map/ppermute | solution.py:110
  156.0 2.6 %collective-permute-start.34 = (bf16[592,256]{1,0:T(8,128)(2,1)S(1)}, bf16[592,256]{1,0:T(8,128)(2,1)S(1)}, u32[]{:S(2)}, u32[]{:S(2)}) collective-permute-start(bf16[592,256]{1,0:T(8,128)(2,1)S(1)} %get-tuple-element.142), channel_id=1, source_target_pairs={{0,2},{1,3},{2,0},{3,1},{4,6},{5,7},{6,4},{7,5},{8,10},{9,11},{10,... | collective-permute-start | bytes 909320 | tf_op jit(solution)/shard_map/ppermute | solution.py:110
  160.6 19.2 %collective-permute-done.31.refs_1_.refs_4_ = bf16[2,784,256]{2,1,0:T(8,128)(2,1)S(1)} collective-permute-done((bf16[2,784,256]{2,1,0:T(8,128)(2,1)S(1)}, bf16[2,784,256]{2,1,0:T(8,128)(2,1)S(1)}, u32[]{:S(2)}, u32[]{:S(2)}) %collective-permute-start.31) | collective-permute-done | bytes 802848 | tf_op jit(solution)/shard_map/ppermute | solution.py:110
  180.0 1.8 head_grads.1
  181.8 10.4 %collective-permute-done.33.refs_1_ = bf16[592,256]{1,0:T(8,128)(2,1)S(1)} collective-permute-done((bf16[592,256]{1,0:T(8,128)(2,1)S(1)}, bf16[592,256]{1,0:T(8,128)(2,1)S(1)}, u32[]{:S(2)}, u32[]{:S(2)}) %collective-permute-start.33) | collective-permute-done | bytes 303136 | tf_op jit(solution)/shard_map/ppermute | solution.py:110
  194.3 2.6 %collective-permute-start.37 = (bf16[144,896]{1,0:T(8,128)(2,1)S(1)}, bf16[144,896]{1,0:T(8,128)(2,1)S(1)}, u32[]{:S(2)}, u32[]{:S(2)}) collective-permute-start(bf16[144,896]{1,0:T(8,128)(2,1)S(1)} %get-tuple-element.145.refs_0_), channel_id=1, source_target_pairs={{0,16},{4,20},{8,24},{12,28},{16,0},{20,4},{24,8},{28,12},{1,17},{... | collective-permute-start | bytes 774152 | tf_op jit(solution)/shard_map/ppermute | solution.py:110
  196.9 15.6 %collective-permute-done.30.refs_2_.refs_4_ = bf16[784,256]{1,0:T(8,128)(2,1)S(1)} collective-permute-done((bf16[784,256]{1,0:T(8,128)(2,1)S(1)}, bf16[784,256]{1,0:T(8,128)(2,1)S(1)}, u32[]{:S(2)}, u32[]{:S(2)}) %collective-permute-start.30) | collective-permute-done | bytes 401440 | tf_op jit(solution)/shard_map/ppermute | solution.py:110
  212.4 6.0 %collective-permute-done.32.refs_5_ = bf16[784,256]{1,0:T(8,128)(2,1)S(1)} collective-permute-done((bf16[784,256]{1,0:T(8,128)(2,1)S(1)}, bf16[784,256]{1,0:T(8,128)(2,1)S(1)}, u32[]{:S(2)}, u32[]{:S(2)}) %collective-permute-start.32) | collective-permute-done | bytes 401440 | tf_op jit(solution)/shard_map/ppermute | solution.py:110
  221.3 2.8 %final.1 = (f32[1024,512]{1,0:T(8,128)}, f32[1,256]{1,0:T(1,128)}, f32[1024,256]{1,0:T(8,128)}, f32[1,256]{1,0:T(1,128)}) custom-call(s32[2]{0:T(128)S(1)} %copy-done.7, bf16[4,144,896]{2,1,0:T(8,128)(2,1)S(1)} %stack.53.refs_1_, bf16[4,144,896]{2,1,0:T(8,128)(2,1)S(1)} %collective-permute-done.39.refs_2_, f32[1,1024]{1,0:T(1,128)S(1)} %bitcast.19, ...), custom_call_target="tpu_custom_call" | custom-call | flops 200000000 | bytes 5000000 | tf_op jit(solution)/shard_map/final/pallas_call | solution.py:84
  (126 shorter events, 49.4 us)
Async XLA Ops:
  4.3 16.4 %collective-permute-start.2 = (bf16[256,128]{1,0:T(8,128)(2,1)}, bf16[256,128]{1,0:T(8,128)(2,1)S(1)}, u32[]{:S(2)}, u32[]{:S(2)}) collective-permute-start(bf16[256,128]{1,0:T(8,128)(2,1)} %get-tuple-element.80.refs_6_.refs_4_), channel_id=1, source_target_pairs={{0,3},{1,2},{2,1},{3,0},{4,7},{5,6},{6,5},{7,4},{8,11},{9,10},{10,... | collective-permute-start | bytes 196616 | tf_op jit(solution)/shard_map/ppermute | solution.py:110
  9.4 11.4 %collective-permute-start.1 = (bf16[256,128]{1,0:T(8,128)(2,1)}, bf16[256,128]{1,0:T(8,128)(2,1)S(1)}, u32[]{:S(2)}, u32[]{:S(2)}) collective-permute-start(bf16[256,128]{1,0:T(8,128)(2,1)} %get-tuple-element.80.refs_6_.refs_4_), channel_id=1, source_target_pairs={{0,2},{1,3},{2,0},{3,1},{4,6},{5,7},{6,4},{7,5},{8,10},{9,11},{10,... | collective-permute-start | bytes 196616 | tf_op jit(solution)/shard_map/ppermute | solution.py:110
  9.4 11.4 %collective-permute-start = (bf16[256,128]{1,0:T(8,128)(2,1)}, bf16[256,128]{1,0:T(8,128)(2,1)S(1)}, u32[]{:S(2)}, u32[]{:S(2)}) collective-permute-start(bf16[256,128]{1,0:T(8,128)(2,1)} %get-tuple-element.80.refs_6_.refs_4_), channel_id=1, source_target_pairs={{0,1},{1,0},{2,3},{3,2},{4,5},{5,4},{6,7},{7,6},{8,9},{9,8},{10,11... | collective-permute-start | bytes 196616 | tf_op jit(solution)/shard_map/ppermute | solution.py:110
  34.9 6.4 %collective-permute-start.4 = (f32[32,1152]{1,0:T(8,128)S(1)}, f32[32,1152]{1,0:T(8,128)S(1)}, u32[]{:S(2)}, u32[]{:S(2)}) collective-permute-start(f32[32,1152]{1,0:T(8,128)S(1)} %get-tuple-element.88), channel_id=1, source_target_pairs={{0,8},{4,12},{8,0},{12,4},{16,24},{20,28},{24,16},{28,20},{1,9},{5... | collective-permute-start | bytes 442376 | tf_op jit(solution)/shard_map/ppermute | solution.py:110
  36.7 8.8 %collective-permute-start.5 = (f32[32,1152]{1,0:T(8,128)S(1)}, f32[32,1152]{1,0:T(8,128)S(1)}, u32[]{:S(2)}, u32[]{:S(2)}) collective-permute-start(f32[32,1152]{1,0:T(8,128)S(1)} %get-tuple-element.89), channel_id=1, source_target_pairs={{0,16},{4,20},{8,24},{12,28},{16,0},{20,4},{24,8},{28,12},{1,17},{... | collective-permute-start | bytes 442376 | tf_op jit(solution)/shard_map/ppermute | solution.py:110
  38.2 7.3 %collective-permute-start.6 = (f32[32,1152]{1,0:T(8,128)S(1)}, f32[32,1152]{1,0:T(8,128)S(1)}, u32[]{:S(2)}, u32[]{:S(2)}) collective-permute-start(f32[32,1152]{1,0:T(8,128)S(1)} %get-tuple-element.90), channel_id=1, source_target_pairs={{0,24},{4,28},{8,16},{12,20},{16,8},{20,12},{24,0},{28,4},{1,25},{... | collective-permute-start | bytes 442376 | tf_op jit(solution)/shard_map/ppermute | solution.py:110
  45.8 5.8 %collective-permute-start.9 = (bf16[32,1152]{1,0:T(8,128)(2,1)S(1)}, bf16[32,1152]{1,0:T(8,128)(2,1)S(1)}, u32[]{:S(2)}, u32[]{:S(2)}) collective-permute-start(bf16[32,1152]{1,0:T(8,128)(2,1)S(1)} %get-tuple-element.91), channel_id=1, source_target_pairs={{0,24},{4,28},{8,16},{12,20},{16,8},{20,12},{24,0},{28,4},{1,25},{... | collective-permute-start | bytes 221192 | tf_op jit(solution)/shard_map/ppermute | solution.py:110
  47.4 4.8 %collective-permute-start.8 = (bf16[32,1152]{1,0:T(8,128)(2,1)S(1)}, bf16[32,1152]{1,0:T(8,128)(2,1)S(1)}, u32[]{:S(2)}, u32[]{:S(2)}) collective-permute-start(bf16[32,1152]{1,0:T(8,128)(2,1)S(1)} %get-tuple-element.91), channel_id=1, source_target_pairs={{0,16},{4,20},{8,24},{12,28},{16,0},{20,4},{24,8},{28,12},{1,17},{... | collective-permute-start | bytes 221192 | tf_op jit(solution)/shard_map/ppermute | solution.py:110
  48.6 4.4 %collective-permute-start.7 = (bf16[32,1152]{1,0:T(8,128)(2,1)S(1)}, bf16[32,1152]{1,0:T(8,128)(2,1)S(1)}, u32[]{:S(2)}, u32[]{:S(2)}) collective-permute-start(bf16[32,1152]{1,0:T(8,128)(2,1)S(1)} %get-tuple-element.91), channel_id=1, source_target_pairs={{0,8},{4,12},{8,0},{12,4},{16,24},{20,28},{24,16},{28,20},{1,9},{5... | collective-permute-start | bytes 221192 | tf_op jit(solution)/shard_map/ppermute | solution.py:110
  56.6 9.8 %collective-permute-start.13 = (bf16[256,384]{1,0:T(8,128)(2,1)S(1)}, bf16[256,384]{1,0:T(8,128)(2,1)S(1)}, u32[]{:S(2)}, u32[]{:S(2)}) collective-permute-start(bf16[256,384]{1,0:T(8,128)(2,1)S(1)} %get-tuple-element.94.refs_0_), channel_id=1, source_target_pairs={{0,3},{1,2},{2,1},{3,0},{4,7},{5,6},{6,5},{7,4},{8,11},{9,10},{10,... | collective-permute-start | bytes 589832 | tf_op jit(solution)/shard_map/ppermute | solution.py:110
  60.3 16.7 %collective-permute-start.12 = (bf16[256,384]{1,0:T(8,128)(2,1)S(1)}, bf16[256,384]{1,0:T(8,128)(2,1)S(1)}, u32[]{:S(2)}, u32[]{:S(2)}) collective-permute-start(bf16[256,384]{1,0:T(8,128)(2,1)S(1)} %get-tuple-element.94.refs_0_), channel_id=1, source_target_pairs={{0,2},{1,3},{2,0},{3,1},{4,6},{5,7},{6,4},{7,5},{8,10},{9,11},{10,... | collective-permute-start | bytes 589832 | tf_op jit(solution)/shard_map/ppermute | solution.py:110
  60.3 16.7 %collective-permute-start.11 = (bf16[256,384]{1,0:T(8,128)(2,1)S(1)}, bf16[256,384]{1,0:T(8,128)(2,1)S(1)}, u32[]{:S(2)}, u32[]{:S(2)}) collective-permute-start(bf16[256,384]{1,0:T(8,128)(2,1)S(1)} %get-tuple-element.94.refs_0_), channel_id=1, source_target_pairs={{0,1},{1,0},{2,3},{3,2},{4,5},{5,4},{6,7},{7,6},{8,9},{9,8},{10,11... | collective-permute-start | bytes 589832 | tf_op jit(solution)/shard_map/ppermute | solution.py:110
  77.6 16.0 %collective-permute-start.14 = (bf16[256,256]{1,0:T(8,128)(2,1)S(1)}, bf16[256,256]{1,0:T(8,128)(2,1)S(1)}, u32[]{:S(2)}, u32[]{:S(2)}) collective-permute-start(bf16[256,256]{1,0:T(8,128)(2,1)S(1)} %get-tuple-element.98), channel_id=1, source_target_pairs={{0,1},{1,0},{2,3},{3,2},{4,5},{5,4},{6,7},{7,6},{8,9},{9,8},{10,11... | collective-permute-start | bytes 393224 | tf_op jit(solution)/shard_map/ppermute | solution.py:110
  77.6 15.9 %collective-permute-start.15 = (bf16[256,256]{1,0:T(8,128)(2,1)S(1)}, bf16[256,256]{1,0:T(8,128)(2,1)S(1)}, u32[]{:S(2)}, u32[]{:S(2)}) collective-permute-start(bf16[256,256]{1,0:T(8,128)(2,1)S(1)} %get-tuple-element.99), channel_id=1, source_target_pairs={{0,2},{1,3},{2,0},{3,1},{4,6},{5,7},{6,4},{7,5},{8,10},{9,11},{10,... | collective-permute-start | bytes 393224 | tf_op jit(solution)/shard_map/ppermute | solution.py:110
  80.6 13.0 %collective-permute-start.16 = (bf16[256,256]{1,0:T(8,128)(2,1)S(1)}, bf16[256,256]{1,0:T(8,128)(2,1)S(1)}, u32[]{:S(2)}, u32[]{:S(2)}) collective-permute-start(bf16[256,256]{1,0:T(8,128)(2,1)S(1)} %get-tuple-element.100), channel_id=1, source_target_pairs={{0,3},{1,2},{2,1},{3,0},{4,7},{5,6},{6,5},{7,4},{8,11},{9,10},{10,... | collective-permute-start | bytes 393224 | tf_op jit(solution)/shard_map/ppermute | solution.py:110
  99.2 5.2 %collective-permute-start.20 = (bf16[32,1024]{1,0:T(8,128)(2,1)S(1)}, bf16[32,1024]{1,0:T(8,128)(2,1)S(1)}, u32[]{:S(2)}, u32[]{:S(2)}) collective-permute-start(bf16[32,1024]{1,0:T(8,128)(2,1)S(1)} %get-tuple-element.106), channel_id=1, source_target_pairs={{0,24},{4,28},{8,16},{12,20},{16,8},{20,12},{24,0},{28,4},{1,25},{... | collective-permute-start | bytes 196616 | tf_op jit(solution)/shard_map/ppermute | solution.py:110
  105.4 5.4 %collective-permute-start.23 = (bf16[32,1152]{1,0:T(8,128)(2,1)S(1)}, bf16[32,1152]{1,0:T(8,128)(2,1)S(1)}, u32[]{:S(2)}, u32[]{:S(2)}) collective-permute-start(bf16[32,1152]{1,0:T(8,128)(2,1)S(1)} %get-tuple-element.111), channel_id=1, source_target_pairs={{0,24},{4,28},{8,16},{12,20},{16,8},{20,12},{24,0},{28,4},{1,25},{... | collective-permute-start | bytes 221192 | tf_op jit(solution)/shard_map/ppermute | solution.py:110
  106.6 4.9 %collective-permute-start.22 = (bf16[32,1152]{1,0:T(8,128)(2,1)S(1)}, bf16[32,1152]{1,0:T(8,128)(2,1)S(1)}, u32[]{:S(2)}, u32[]{:S(2)}) collective-permute-start(bf16[32,1152]{1,0:T(8,128)(2,1)S(1)} %get-tuple-element.111), channel_id=1, source_target_pairs={{0,16},{4,20},{8,24},{12,28},{16,0},{20,4},{24,8},{28,12},{1,17},{... | collective-permute-start | bytes 221192 | tf_op jit(solution)/shard_map/ppermute | solution.py:110
  126.5 4.4 %collective-permute-start.26 = (bf16[4,128,1152]{2,1,0:T(8,128)(2,1)S(1)}, bf16[4,128,1152]{2,1,0:T(8,128)(2,1)S(1)}, u32[]{:S(2)}, u32[]{:S(2)}) collective-permute-start(bf16[4,128,1152]{2,1,0:T(8,128)(2,1)S(1)} %get-tuple-element.128), channel_id=1, source_target_pairs={{0,4},{4,0},{8,12},{12,8},{16,20},{20,16},{24,28},{28,24},{1,5},{5... | collective-permute-start | bytes 3538952 | tf_op jit(solution)/shard_map/ppermute | solution.py:110
  130.8 29.2 %collective-permute-start.25 = (bf16[2,784,256]{2,1,0:T(8,128)(2,1)S(1)}, bf16[2,784,256]{2,1,0:T(8,128)(2,1)S(1)}, u32[]{:S(2)}, u32[]{:S(2)}) collective-permute-start(bf16[2,784,256]{2,1,0:T(8,128)(2,1)S(1)} %get-tuple-element.127), channel_id=1, source_target_pairs={{0,1},{1,0},{2,3},{3,2},{4,5},{5,4},{6,7},{7,6},{8,9},{9,8},{10,11... | collective-permute-start | bytes 2408456 | tf_op jit(solution)/shard_map/ppermute | solution.py:110
  136.4 43.4 %collective-permute-start.31 = (bf16[2,784,256]{2,1,0:T(8,128)(2,1)S(1)}, bf16[2,784,256]{2,1,0:T(8,128)(2,1)S(1)}, u32[]{:S(2)}, u32[]{:S(2)}) collective-permute-start(bf16[2,784,256]{2,1,0:T(8,128)(2,1)S(1)} %get-tuple-element.138), channel_id=1, source_target_pairs={{0,1},{1,0},{2,3},{3,2},{4,5},{5,4},{6,7},{7,6},{8,9},{9,8},{10,11... | collective-permute-start | bytes 2408456 | tf_op jit(solution)/shard_map/ppermute | solution.py:110
  138.5 9.9 %collective-permute-start.27 = (bf16[128,1152]{1,0:T(8,128)(2,1)S(1)}, bf16[128,1152]{1,0:T(8,128)(2,1)S(1)}, u32[]{:S(2)}, u32[]{:S(2)}) collective-permute-start(bf16[128,1152]{1,0:T(8,128)(2,1)S(1)} %get-tuple-element.130), channel_id=1, source_target_pairs={{0,8},{4,12},{8,0},{12,4},{16,24},{20,28},{24,16},{28,20},{1,9},{5... | collective-permute-start | bytes 884744 | tf_op jit(solution)/shard_map/ppermute | solution.py:110
  140.0 14.7 %collective-permute-start.28 = (bf16[128,1152]{1,0:T(8,128)(2,1)S(1)}, bf16[128,1152]{1,0:T(8,128)(2,1)S(1)}, u32[]{:S(2)}, u32[]{:S(2)}) collective-permute-start(bf16[128,1152]{1,0:T(8,128)(2,1)S(1)} %get-tuple-element.131), channel_id=1, source_target_pairs={{0,16},{4,20},{8,24},{12,28},{16,0},{20,4},{24,8},{28,12},{1,17},{... | collective-permute-start | bytes 884744 | tf_op jit(solution)/shard_map/ppermute | solution.py:110
  140.5 14.2 %collective-permute-start.29 = (bf16[128,1152]{1,0:T(8,128)(2,1)S(1)}, bf16[128,1152]{1,0:T(8,128)(2,1)S(1)}, u32[]{:S(2)}, u32[]{:S(2)}) collective-permute-start(bf16[128,1152]{1,0:T(8,128)(2,1)S(1)} %get-tuple-element.132), channel_id=1, source_target_pairs={{0,24},{4,28},{8,16},{12,20},{16,8},{20,12},{24,0},{28,4},{1,25},{... | collective-permute-start | bytes 884744 | tf_op jit(solution)/shard_map/ppermute | solution.py:110
  155.6 36.6 %collective-permute-start.33 = (bf16[592,256]{1,0:T(8,128)(2,1)S(1)}, bf16[592,256]{1,0:T(8,128)(2,1)S(1)}, u32[]{:S(2)}, u32[]{:S(2)}) collective-permute-start(bf16[592,256]{1,0:T(8,128)(2,1)S(1)} %get-tuple-element.141), channel_id=1, source_target_pairs={{0,1},{1,0},{2,3},{3,2},{4,5},{5,4},{6,7},{7,6},{8,9},{9,8},{10,11... | collective-permute-start | bytes 909320 | tf_op jit(solution)/shard_map/ppermute | solution.py:110
  156.0 36.2 %collective-permute-start.34 = (bf16[592,256]{1,0:T(8,128)(2,1)S(1)}, bf16[592,256]{1,0:T(8,128)(2,1)S(1)}, u32[]{:S(2)}, u32[]{:S(2)}) collective-permute-start(bf16[592,256]{1,0:T(8,128)(2,1)S(1)} %get-tuple-element.142), channel_id=1, source_target_pairs={{0,2},{1,3},{2,0},{3,1},{4,6},{5,7},{6,4},{7,5},{8,10},{9,11},{10,... | collective-permute-start | bytes 909320 | tf_op jit(solution)/shard_map/ppermute | solution.py:110
  158.6 33.6 %collective-permute-start.35 = (bf16[592,256]{1,0:T(8,128)(2,1)S(1)}, bf16[592,256]{1,0:T(8,128)(2,1)S(1)}, u32[]{:S(2)}, u32[]{:S(2)}) collective-permute-start(bf16[592,256]{1,0:T(8,128)(2,1)S(1)} %get-tuple-element.143), channel_id=1, source_target_pairs={{0,3},{1,2},{2,1},{3,0},{4,7},{5,6},{6,5},{7,4},{8,11},{9,10},{10,... | collective-permute-start | bytes 909320 | tf_op jit(solution)/shard_map/ppermute | solution.py:110
  160.2 52.3 %collective-permute-start.30 = (bf16[784,256]{1,0:T(8,128)(2,1)S(1)}, bf16[784,256]{1,0:T(8,128)(2,1)S(1)}, u32[]{:S(2)}, u32[]{:S(2)}) collective-permute-start(bf16[784,256]{1,0:T(8,128)(2,1)S(1)} %add.4.refs_2_), channel_id=1, source_target_pairs={{0,2},{1,3},{2,0},{3,1},{4,6},{5,7},{6,4},{7,5},{8,10},{9,11},{10,... | collective-permute-start | bytes 1204232 | tf_op jit(solution)/shard_map/ppermute | solution.py:110
  179.9 38.6 %collective-permute-start.32 = (bf16[784,256]{1,0:T(8,128)(2,1)S(1)}, bf16[784,256]{1,0:T(8,128)(2,1)S(1)}, u32[]{:S(2)}, u32[]{:S(2)}) collective-permute-start(bf16[784,256]{1,0:T(8,128)(2,1)S(1)} %add.5.refs_4_), channel_id=1, source_target_pairs={{0,2},{1,3},{2,0},{3,1},{4,6},{5,7},{6,4},{7,5},{8,10},{9,11},{10,... | collective-permute-start | bytes 1204232 | tf_op jit(solution)/shard_map/ppermute | solution.py:110
  193.2 19.3 %collective-permute-start.38 = (bf16[144,896]{1,0:T(8,128)(2,1)S(1)}, bf16[144,896]{1,0:T(8,128)(2,1)S(1)}, u32[]{:S(2)}, u32[]{:S(2)}) collective-permute-start(bf16[144,896]{1,0:T(8,128)(2,1)S(1)} %get-tuple-element.145.refs_0_), channel_id=1, source_target_pairs={{0,24},{4,28},{8,16},{12,20},{16,8},{20,12},{24,0},{28,4},{1,25},{... | collective-permute-start | bytes 774152 | tf_op jit(solution)/shard_map/ppermute | solution.py:110
  194.3 18.1 %collective-permute-start.37 = (bf16[144,896]{1,0:T(8,128)(2,1)S(1)}, bf16[144,896]{1,0:T(8,128)(2,1)S(1)}, u32[]{:S(2)}, u32[]{:S(2)}) collective-permute-start(bf16[144,896]{1,0:T(8,128)(2,1)S(1)} %get-tuple-element.145.refs_0_), channel_id=1, source_target_pairs={{0,16},{4,20},{8,24},{12,28},{16,0},{20,4},{24,8},{28,12},{1,17},{... | collective-permute-start | bytes 774152 | tf_op jit(solution)/shard_map/ppermute | solution.py:110
  196.9 15.6 %collective-permute-start.36 = (bf16[144,896]{1,0:T(8,128)(2,1)S(1)}, bf16[144,896]{1,0:T(8,128)(2,1)S(1)}, u32[]{:S(2)}, u32[]{:S(2)}) collective-permute-start(bf16[144,896]{1,0:T(8,128)(2,1)S(1)} %get-tuple-element.145.refs_0_), channel_id=1, source_target_pairs={{0,8},{4,12},{8,0},{12,4},{16,24},{20,28},{24,16},{28,20},{1,9},{5... | collective-permute-start | bytes 774152 | tf_op jit(solution)/shard_map/ppermute | solution.py:110
  (32 other events, 294.7 us)
